TPU v7x, 32 devices: a whole 2x2x4 slice. The times are simulated.
32 devices in a mesh: groups: 2 (over x), ctx: 16 (over z, y, core).
Axes of the slice: x: 2, y: 2, z: 4, core: 2. Of those that a mesh axis runs over, the one named last changes fastest.
Arguments:
- queries: bfloat16 [4096, 1024], P(('groups', 'ctx')), parts along dimension 0, may hold values from -6 to 6
- keys: bfloat16 [4096, 1024], P(('groups', 'ctx')), parts along dimension 0, may hold values from -0.5 to 0.5
- values: bfloat16 [4096, 1024], P(('groups', 'ctx')), parts along dimension 0, may hold values from -6 to 6
- out_grad: bfloat16 [4096, 1024], P(('groups', 'ctx')), parts along dimension 0, may hold values from -0.059814453 to 0.059814453
- log_decay: bfloat16 [4096, 8], P(('groups', 'ctx')), parts along dimension 0, may hold values from -1 to 0
- frame_pos: int32 [4096], P(('groups', 'ctx')), parts along dimension 0, may hold values from 0 to 2047, as said below
- trial_lengths: int32 [16], P('groups'), parts along dimension 0, may hold values from 1 to 1024, 2048 in all
Outputs:
- query_grad: bfloat16 [4096, 1024], P(('groups', 'ctx')), parts along dimension 0
- key_grad: bfloat16 [4096, 1024], P(('groups', 'ctx')), parts along dimension 0
- value_grad: bfloat16 [4096, 1024], P(('groups', 'ctx')), parts along dimension 0
- decay_grad: bfloat16 [4096, 8], P(('groups', 'ctx')), parts along dimension 0
There are 2 independent parts, one for each index of `groups`. A program takes and returns all parts, laid end to end along the dimension named above; each array names one. Nothing has to cross between parts.
Inputs may be any that keep to these rules, and one draw needn't show every extreme that they name: frame_pos is a permutation: the frame in loader row r sits at chain position frame_pos[r], and chain position p belongs to ctx index p // 128. The rows of one device bound for one device number at most 16, and exactly 16 for some pair of devices in every draw. `trial_lengths`: the lengths sum to 2048; the longest is exactly 1024; trials lie end to end in chain order.
All inputs are finite; a program needn't handle non-finite values.
Results may differ from a plain program's by a relative error of at most 0.0085.
Values may be sent and summed in bfloat16 or wider, within the bound.
No kernel may reach another device: no remote copies, remote signals or barrier semaphores. Data moves between devices by JAX's collectives and lax.ppermute only.
A program may use at most 192 MiB of HBM per device.

v0:
```python
import jax
import jax.numpy as jnp
from jax import lax
from jax.sharding import PartitionSpec as P

SPAN = 128


def prefix(shard, axis, combine, identity, reverse):
    peers, place = (lax.axis_size(axis), lax.axis_index(axis))
    everything = jax.tree.map(lambda part: lax.all_gather(part, axis), shard)
    start = jax.tree.map(
        lambda part, zero: jnp.broadcast_to(jnp.asarray(zero, part.dtype), part.shape),
        shard,
        identity,
    )

    def turn(k, before):
        at = peers - 1 - k if reverse else k
        reached = at > place if reverse else at < place
        new = combine(before, jax.tree.map(lambda part: part[at], everything))
        return jax.tree.map(lambda a, b: jnp.where(reached, a, b), new, before)

    return lax.fori_loop(0, peers, turn, start)


def join_state(earlier, later):
    return (earlier[0] * later[0], later[0][:, None, None] * earlier[1] + later[1])


def join_tail(earlier, later):
    return (earlier[0] * later[0], later[0] * earlier[1] + later[1])


def body(queries, keys, values, out_grad, log_decay, frame_pos, trial_lengths):
    row_count = queries.shape[0]
    model_width = queries.shape[1]
    head_count = log_decay.shape[1]
    head_width = model_width // head_count
    peer_count = lax.axis_size("ctx")
    slot_room = 2 * row_count // peer_count
    slot_total = peer_count * slot_room
    owner_dev = frame_pos // row_count
    offset = frame_pos % row_count
    owner_hot = (owner_dev[:, None] == jnp.arange(peer_count, dtype=jnp.int32)[None, :]).astype(
        jnp.int32
    )
    slot_rank = jnp.sum((jnp.cumsum(owner_hot, axis=0) - owner_hot) * owner_hot, axis=1)
    send_slot = owner_dev * slot_room + slot_rank

    def pack_rows(source):
        return jnp.zeros((slot_total,) + source.shape[1:], source.dtype).at[send_slot].set(source)

    place_at = jnp.full((slot_total,), row_count, jnp.int32).at[send_slot].set(offset)
    arrived_rows = (
        lax.all_to_all(pack_rows(queries), "ctx", split_axis=0, concat_axis=0, tiled=True),
        lax.all_to_all(pack_rows(keys), "ctx", split_axis=0, concat_axis=0, tiled=True),
        lax.all_to_all(pack_rows(values), "ctx", split_axis=0, concat_axis=0, tiled=True),
        lax.all_to_all(pack_rows(out_grad), "ctx", split_axis=0, concat_axis=0, tiled=True),
        lax.all_to_all(pack_rows(log_decay), "ctx", split_axis=0, concat_axis=0, tiled=True),
        lax.all_to_all(place_at, "ctx", split_axis=0, concat_axis=0, tiled=True),
    )
    arrived_at = arrived_rows[5]

    def place_rows(source):
        return (
            jnp.zeros((row_count,) + source.shape[1:], source.dtype)
            .at[arrived_at]
            .set(source, mode="drop")
        )

    block_count = row_count // SPAN
    block_shape = (block_count, SPAN, head_count, head_width)
    query_rows = place_rows(arrived_rows[0]).reshape(block_shape)
    key_rows = place_rows(arrived_rows[1]).reshape(block_shape)
    value_rows = place_rows(arrived_rows[2]).reshape(block_shape)
    grad_rows = place_rows(arrived_rows[3]).reshape(block_shape)
    cum_decay = jnp.cumsum(
        place_rows(arrived_rows[4]).astype(jnp.float32).reshape(block_count, SPAN, head_count),
        axis=1,
    )
    position = lax.axis_index("ctx") * row_count + jnp.arange(row_count, dtype=jnp.int32)
    starts = jnp.cumsum(trial_lengths) - trial_lengths
    is_start = jnp.any(position[:, None] == starts[None, :], axis=1)
    start_marks = jnp.cumsum(is_start.reshape(block_count, SPAN).astype(jnp.int32), axis=1)
    last_mark = start_marks[:, -1:]
    query_gain = jnp.where(start_marks[:, :, None] == 0, jnp.exp(cum_decay), 0.0)
    key_gain = jnp.where(
        start_marks[:, :, None] == last_mark[:, :, None],
        jnp.exp(cum_decay[:, -1:, :] - cum_decay),
        0.0,
    )
    span_fade = jnp.where(last_mark == 0, jnp.exp(cum_decay[:, -1, :]), 0.0)
    key_end = (key_rows * key_gain[..., None]).astype(jnp.bfloat16)
    query_start = (query_rows * query_gain[..., None]).astype(jnp.bfloat16)
    carried = jnp.einsum("bjhd,bjhe->bhde", key_end, value_rows, preferred_element_type=jnp.float32)
    pulled = jnp.einsum(
        "bihd,bihe->bhde", query_start, grad_rows, preferred_element_type=jnp.float32
    )
    empty_state = jnp.zeros((head_count, head_width, head_width), jnp.float32)
    own_fade = jnp.ones((head_count,), jnp.float32)
    own_state = empty_state
    block_index = 0
    own_state = span_fade[block_index][:, None, None] * own_state + carried[block_index]
    own_fade = own_fade * span_fade[block_index]
    own_pull = empty_state
    for block_index in reversed(range(block_count)):
        own_pull = pulled[block_index] + span_fade[block_index][:, None, None] * own_pull
    scan_unit = (jnp.ones((head_count,), jnp.float32), empty_state)
    entering = prefix((own_fade, own_state), "ctx", join_state, scan_unit, False)[1]
    leaving = prefix((own_fade, own_pull), "ctx", join_state, scan_unit, True)[1]
    block_index = 0
    state_list = [entering]
    grad_list = [empty_state] * block_count
    grad_now = leaving
    for block_index in reversed(range(block_count)):
        grad_list[block_index] = grad_now
        grad_now = pulled[block_index] + span_fade[block_index][:, None, None] * grad_now
    state_low = jnp.stack(state_list).astype(jnp.bfloat16)
    grad_low = jnp.stack(grad_list).astype(jnp.bfloat16)
    lower_tri = jnp.arange(SPAN)[:, None] >= jnp.arange(SPAN)[None, :]
    keep_pair = (lower_tri[None] & (start_marks[:, :, None] == start_marks[:, None, :]))[:, None]
    decay_head = jnp.transpose(cum_decay, (0, 2, 1))
    decay_gap = decay_head[:, :, :, None] - decay_head[:, :, None, :]
    weight = jnp.where(keep_pair, jnp.exp(jnp.where(keep_pair, decay_gap, 0.0)), 0.0)
    scores = jnp.einsum("bihd,bjhd->bhij", query_rows, key_rows, preferred_element_type=jnp.float32)
    grad_score = jnp.einsum(
        "bihe,bjhe->bhij", grad_rows, value_rows, preferred_element_type=jnp.float32
    )
    score_weighted = (scores * weight).astype(jnp.bfloat16)
    grad_weighted = (grad_score * weight).astype(jnp.bfloat16)
    query_grad = jnp.einsum(
        "bhij,bjhd->bihd", grad_weighted, key_rows, preferred_element_type=jnp.float32
    ) + query_gain[..., None] * jnp.einsum(
        "bihe,bhde->bihd", grad_rows, state_low, preferred_element_type=jnp.float32
    )
    key_grad = jnp.einsum(
        "bhij,bihd->bjhd", grad_weighted, query_rows, preferred_element_type=jnp.float32
    ) + key_gain[..., None] * jnp.einsum(
        "bjhe,bhde->bjhd", value_rows, grad_low, preferred_element_type=jnp.float32
    )
    value_grad = jnp.einsum(
        "bhij,bihe->bjhe", score_weighted, grad_rows, preferred_element_type=jnp.float32
    ) + key_gain[..., None] * jnp.einsum(
        "bjhd,bhde->bjhe", key_rows, grad_low, preferred_element_type=jnp.float32
    )
    decay_term = jnp.sum(query_rows * query_grad - key_rows * key_grad, axis=3).reshape(
        row_count, head_count
    )
    segment = jnp.cumsum(is_start.astype(jnp.int32))
    later_pos = jnp.arange(row_count)[None, :] >= jnp.arange(row_count)[:, None]
    same_trial = later_pos & (segment[None, :] == segment[:, None])
    local_tail = jnp.dot(
        same_trial.astype(jnp.float32), decay_term, precision=lax.Precision.HIGHEST
    )
    head_part = jnp.sum(jnp.where(segment[:, None] == 0, decay_term, 0.0), axis=0)
    passes = jnp.where(segment[-1] == 0, 1.0, 0.0) * jnp.ones((head_count,), jnp.float32)
    tail_unit = (jnp.ones((head_count,), jnp.float32), jnp.zeros((head_count,), jnp.float32))
    tail_carry = prefix((passes, head_part), "ctx", join_tail, tail_unit, True)[1]
    tail_grad = local_tail + jnp.where(segment[:, None] == segment[-1], tail_carry[None, :], 0.0)
    tail_grad = jnp.where(is_start[:, None], 0.0, tail_grad).astype(jnp.bfloat16)
    back_rows = jnp.clip(arrived_at, 0, row_count - 1)

    def chain_out(source):
        return source.reshape(row_count, model_width).astype(jnp.bfloat16)[back_rows]

    returned = (
        lax.all_to_all(chain_out(query_grad), "ctx", split_axis=0, concat_axis=0, tiled=True),
        lax.all_to_all(chain_out(key_grad), "ctx", split_axis=0, concat_axis=0, tiled=True),
        lax.all_to_all(chain_out(value_grad), "ctx", split_axis=0, concat_axis=0, tiled=True),
        lax.all_to_all(tail_grad[back_rows], "ctx", split_axis=0, concat_axis=0, tiled=True),
    )
    return (
        returned[0][send_slot],
        returned[1][send_slot],
        returned[2][send_slot],
        returned[3][send_slot],
    )


def solution(mesh):
    placed = (
        P(("groups", "ctx"), None),
        P(("groups", "ctx"), None),
        P(("groups", "ctx"), None),
        P(("groups", "ctx"), None),
        P(("groups", "ctx"), None),
        P(("groups", "ctx")),
        P("groups"),
    )
    return jax.shard_map(
        body,
        mesh=mesh,
        in_specs=placed,
        out_specs=(
            P(("groups", "ctx"), None),
            P(("groups", "ctx"), None),
            P(("groups", "ctx"), None),
            P(("groups", "ctx"), None),
        ),
        check_vma=False,
    )
```

profile of v0, /device:TPU:0, one launch (start us, length us, event | category | flops | bytes accessed | tf_op | source)
XLA Modules:
  0.0 368.0 jit_solution(12840954331756360141)
XLA Ops:
  10.0 7.4 %all-to-all-start = ((s32[16,16,1]{1,2,0:T(1,128)}), s32[16,16,1]{1,2,0:T(1,128)S(1)}, u32[]{:S(2)}, u32[]{:S(2)}) async-start(s32[16,16,1]{1,2,0:T(1,128)} %bitcast), calls=%async_computation | async-start | bytes 16384 | tf_op jit(solution)/shard_map/all_to_all | solution.py:61
  19.8 3.9 %all-to-all-done = s32[16,16,1]{1,2,0:T(1,128)S(1)} async-done(((s32[16,16,1]{1,2,0:T(1,128)}), s32[16,16,1]{1,2,0:T(1,128)S(1)}, u32[]{:S(2)}, u32[]{:S(2)}) %all-to-all-start) | async-done | bytes 1056 | tf_op jit(solution)/shard_map/all_to_all | solution.py:61
  23.7 3.5 all-to-all-start.4
  27.2 2.4 scatter_custom_fusion.3
  29.6 4.2 %all-to-all-done.4 = bf16[16,16,8]{1,2,0:T(8,128)(2,1)S(1)} async-done(((bf16[16,16,8]{1,2,0:T(8,128)(2,1)}), bf16[16,16,8]{1,2,0:T(8,128)(2,1)S(1)}, u32[]{:S(2)}, u32[]{:S(2)}) %all-to-all-start.4) | async-done | bytes 4128 | tf_op jit(solution)/shard_map/all_to_all | solution.py:60
  33.8 3.6 all-to-all-start.2
  39.9 2.4 scatter_custom_fusion.9
  44.8 7.0 %all-to-all-done.2 = bf16[16,16,1024]{2,1,0:T(8,128)(2,1)S(1)} async-done(((bf16[16,16,1024]{2,1,0:T(8,128)(2,1)}), bf16[16,16,1024]{2,1,0:T(8,128)(2,1)S(1)}, u32[]{:S(2)}, u32[]{:S(2)}) %all-to-all-start.2) | async-done | bytes 524320 | tf_op jit(solution)/shard_map/all_to_all | solution.py:59
  51.8 4.0 %all-to-all-start.6 = ((bf16[16,16,1024]{2,1,0:T(8,128)(2,1)}), bf16[16,16,1024]{2,1,0:T(8,128)(2,1)S(1)}, u32[]{:S(2)}, u32[]{:S(2)}) async-start(bf16[16,16,1024]{2,1,0:T(8,128)(2,1)} %bitcast.35), calls=%async_computation.6 | async-start | bytes 1048576 | tf_op jit(solution)/shard_map/all_to_all | solution.py:56
  56.0 1.2 scatter_custom_fusion.8
  57.5 1.7 scatter_custom_fusion.4
  59.4 10.9 %all-to-all-done.6 = bf16[16,16,1024]{2,1,0:T(8,128)(2,1)S(1)} async-done(((bf16[16,16,1024]{2,1,0:T(8,128)(2,1)}), bf16[16,16,1024]{2,1,0:T(8,128)(2,1)S(1)}, u32[]{:S(2)}, u32[]{:S(2)}) %all-to-all-start.6) | async-done | bytes 524320 | tf_op jit(solution)/shard_map/all_to_all | solution.py:56
  70.3 1.7 scatter_custom_fusion.10
  73.3 2.4 scatter_custom_fusion.5
  75.7 4.1 %all-to-all-start.3 = ((bf16[16,16,1024]{2,1,0:T(8,128)(2,1)}), bf16[16,16,1024]{2,1,0:T(8,128)(2,1)S(1)}, u32[]{:S(2)}, u32[]{:S(2)}) async-start(bf16[16,16,1024]{2,1,0:T(8,128)(2,1)} %bitcast.7), calls=%async_computation.3 | async-start | bytes 1048576 | tf_op jit(solution)/shard_map/all_to_all | solution.py:58
  79.9 2.4 scatter_custom_fusion.1
  82.3 19.8 %all-to-all-done.3 = bf16[16,16,1024]{2,1,0:T(8,128)(2,1)S(1)} async-done(((bf16[16,16,1024]{2,1,0:T(8,128)(2,1)}), bf16[16,16,1024]{2,1,0:T(8,128)(2,1)S(1)}, u32[]{:S(2)}, u32[]{:S(2)}) %all-to-all-start.3) | async-done | bytes 524320 | tf_op jit(solution)/shard_map/all_to_all | solution.py:58
  102.1 8.5 %all-to-all-start.1 = ((bf16[16,16,1024]{2,1,0:T(8,128)(2,1)}), bf16[16,16,1024]{2,1,0:T(8,128)(2,1)S(1)}, u32[]{:S(2)}, u32[]{:S(2)}) async-start(bf16[16,16,1024]{2,1,0:T(8,128)(2,1)} %bitcast.2), calls=%async_computation.1 | async-start | bytes 1048576 | tf_op jit(solution)/shard_map/all_to_all | solution.py:57
  110.6 1.9 scatter_custom_fusion.6
  112.7 16.3 %all-to-all-done.1 = bf16[16,16,1024]{2,1,0:T(8,128)(2,1)S(1)} async-done(((bf16[16,16,1024]{2,1,0:T(8,128)(2,1)}), bf16[16,16,1024]{2,1,0:T(8,128)(2,1)S(1)}, u32[]{:S(2)}, u32[]{:S(2)}) %all-to-all-start.1) | async-done | bytes 524320 | tf_op jit(solution)/shard_map/all_to_all | solution.py:57
  129.0 1.7 scatter_custom_fusion.2
  136.2 24.7 %all-gather = f32[16,1,8]{2,1,0:T(1,128)S(1)} all-gather(f32[1,1,8]{2,1,0:T(1,128)S(1)} %get-tuple-element.539), channel_id=3, replica_groups=mesh['groups'=2,'ctx'=16] {'ctx'}, dimensions={0}, use_global_device_ids=true | all-gather | bytes 544 | tf_op jit(solution)/shard_map/all_gather | solution.py:11
  163.1 19.7 %while.47 = (s32[]{:T(128)}, f32[8,128,128]{2,1,0:T(8,128)S(1)}, s32[]{:T(128)}, f32[16,8]{1,0:T(8,128)S(1)}, f32[16,8,128,128]{3,2,1,0:T(8,128)}, /*index=5*/s32[]{:T(128)}, s32[]{:T(128)}, s32[]{:T(128)}, s32[]{:T(128)}) while((s32[]{:T(128)}, f32[8,128,128]{2,1,0:T(8,128)S(1)}, s32[]{:T(128)}, f32[16,8]{1,0:T(8,128)S(1)}, ...), condition=%wide.region_20.21_spmd.clone, body=%wide.region_19.20_spmd.clone.sunk | while | flops 524296 | bytes 1573127 | solution.py:24
  163.1 1.2 fusion.74
  164.4 1.2 fusion.74
  165.6 1.2 fusion.74
  166.8 1.2 fusion.74
  168.1 1.2 fusion.74
  169.3 1.2 fusion.74
  170.5 1.2 fusion.74
  171.8 1.2 fusion.74
  173.0 1.2 fusion.74
  174.2 1.2 fusion.74
  175.5 1.2 fusion.74
  176.7 1.2 fusion.74
  177.9 1.2 fusion.74
  179.2 1.2 fusion.74
  180.4 1.2 fusion.74
  181.6 1.2 fusion.74
  183.8 53.8 %all-gather.7.cloned.1.call-done = f32[128,128,128]{2,1,0:T(8,128)} async-done(((f32[8,128,128]{2,1,0:T(8,128)}), f32[128,128,128]{2,1,0:T(8,128)}) %all-gather.7.cloned.1.call-update) | async-done | bytes 8388624 | tf_op jit(solution)/shard_map/all_gather | solution.py:11
  237.6 19.4 %while.46 = (s32[]{:T(128)}, f32[8,128,128]{2,1,0:T(8,128)S(1)}, s32[]{:T(128)}, f32[16,8]{1,0:T(8,128)S(1)}, f32[16,8,128,128]{3,2,1,0:T(8,128)}, /*index=5*/s32[]{:T(128)}, s32[]{:T(128)}) while((s32[]{:T(128)}, f32[8,128,128]{2,1,0:T(8,128)S(1)}, s32[]{:T(128)}, f32[16,8]{1,0:T(8,128)S(1)}, f32[16,8,128,128]{3,2,1,0:T(8,128)}, ...), condition=%wide.region_16.17_spmd.clone, body=%wide.region_15.16_spmd.clone.sunk | while | flops 524292 | bytes 1573065 | solution.py:24
  240.1 1.2 fusion.73
  241.3 1.2 fusion.73
  242.5 1.2 fusion.73
  246.1 1.2 fusion.73
  247.3 1.2 fusion.73
  248.6 1.2 fusion.73
  257.3 1.2 fusion.2
  258.5 1.4 subtract_reduce_fusion
  260.6 31.0 %all-reduce.2 = (f32[16]{0:T(128)S(1)}, f32[128]{0:T(128)S(1)}) all-reduce(f32[16]{0:T(128)S(1)} %dynamic-update-slice, f32[128]{0:T(128)S(1)} %dynamic-update-slice.1), channel_id=2, replica_groups=mesh['groups'=2,'ctx'=16] {'ctx'}, use_global_device_ids=true, to_apply=%add | all-reduce | flops 144 | bytes 1152
  294.4 3.5 all-to-all-start.9
  298.6 2.0 gather_fusion.4
  300.6 4.0 %all-to-all-done.9 = bf16[16,16,8]{1,2,0:T(8,128)(2,1)S(1)} async-done(((bf16[16,16,8]{1,2,0:T(8,128)(2,1)}), bf16[16,16,8]{1,2,0:T(8,128)(2,1)S(1)}, u32[]{:S(2)}, u32[]{:S(2)}) %all-to-all-start.9) | async-done | bytes 4128 | tf_op jit(solution)/shard_map/all_to_all | solution.py:171
  304.5 3.6 all-to-all-start.8
  308.3 2.0 gather_fusion.2
  310.2 12.3 %all-to-all-done.8 = bf16[16,16,1024]{2,1,0:T(8,128)(2,1)S(1)} async-done(((bf16[16,16,1024]{2,1,0:T(8,128)(2,1)}), bf16[16,16,1024]{2,1,0:T(8,128)(2,1)S(1)}, u32[]{:S(2)}, u32[]{:S(2)}) %all-to-all-start.8) | async-done | bytes 524320 | tf_op jit(solution)/shard_map/all_to_all | solution.py:170
  322.5 4.0 %all-to-all-start.7 = ((bf16[16,16,1024]{2,1,0:T(8,128)(2,1)}), bf16[16,16,1024]{2,1,0:T(8,128)(2,1)S(1)}, u32[]{:S(2)}, u32[]{:S(2)}) async-start(bf16[16,16,1024]{2,1,0:T(8,128)(2,1)} %bitcast.44), calls=%async_computation.7 | async-start | bytes 1048576 | tf_op jit(solution)/shard_map/all_to_all | solution.py:169
  326.7 2.0 gather_fusion
  328.7 12.3 %all-to-all-done.7 = bf16[16,16,1024]{2,1,0:T(8,128)(2,1)S(1)} async-done(((bf16[16,16,1024]{2,1,0:T(8,128)(2,1)}), bf16[16,16,1024]{2,1,0:T(8,128)(2,1)S(1)}, u32[]{:S(2)}, u32[]{:S(2)}) %all-to-all-start.7) | async-done | bytes 524320 | tf_op jit(solution)/shard_map/all_to_all | solution.py:169
  341.0 4.1 %all-to-all-start.5 = ((bf16[16,16,1024]{2,1,0:T(8,128)(2,1)}), bf16[16,16,1024]{2,1,0:T(8,128)(2,1)S(1)}, u32[]{:S(2)}, u32[]{:S(2)}) async-start(bf16[16,16,1024]{2,1,0:T(8,128)(2,1)} %bitcast.33), calls=%async_computation.5 | async-start | bytes 1048576 | tf_op jit(solution)/shard_map/all_to_all | solution.py:168
  346.6 1.6 gather_fusion.5
  348.2 1.6 gather_fusion.3
  349.8 9.9 %all-to-all-done.5 = bf16[16,16,1024]{2,1,0:T(8,128)(2,1)S(1)} async-done(((bf16[16,16,1024]{2,1,0:T(8,128)(2,1)}), bf16[16,16,1024]{2,1,0:T(8,128)(2,1)S(1)}, u32[]{:S(2)}, u32[]{:S(2)}) %all-to-all-start.5) | async-done | bytes 524320 | tf_op jit(solution)/shard_map/all_to_all | solution.py:168
  359.6 1.6 gather_fusion.1
  (140 shorter events, 37.5 us)
Async XLA Ops:
  7.2 126.4 %copy-start.1 = (u32[32]{0:T(128)S(1)}, u32[32]{0:T(128)}, u32[]{:S(2)}) copy-start(u32[32]{0:T(128)} %constant.182) | copy-start | bytes 388
  10.0 13.7 %all-to-all-start = ((s32[16,16,1]{1,2,0:T(1,128)}), s32[16,16,1]{1,2,0:T(1,128)S(1)}, u32[]{:S(2)}, u32[]{:S(2)}) async-start(s32[16,16,1]{1,2,0:T(1,128)} %bitcast), calls=%async_computation | async-start | bytes 16384 | tf_op jit(solution)/shard_map/all_to_all | solution.py:61
  23.7 10.1 %all-to-all-start.4 = ((bf16[16,16,8]{1,2,0:T(8,128)(2,1)}), bf16[16,16,8]{1,2,0:T(8,128)(2,1)S(1)}, u32[]{:S(2)}, u32[]{:S(2)}) async-start(bf16[16,16,8]{1,2,0:T(8,128)(2,1)} %copy.168), calls=%async_computation.4 | async-start | bytes 65536 | tf_op jit(solution)/shard_map/all_to_all | solution.py:60
  33.8 18.0 %all-to-all-start.2 = ((bf16[16,16,1024]{2,1,0:T(8,128)(2,1)}), bf16[16,16,1024]{2,1,0:T(8,128)(2,1)S(1)}, u32[]{:S(2)}, u32[]{:S(2)}) async-start(bf16[16,16,1024]{2,1,0:T(8,128)(2,1)} %bitcast.5), calls=%async_computation.2 | async-start | bytes 1048576 | tf_op jit(solution)/shard_map/all_to_all | solution.py:59
  51.8 18.5 %all-to-all-start.6 = ((bf16[16,16,1024]{2,1,0:T(8,128)(2,1)}), bf16[16,16,1024]{2,1,0:T(8,128)(2,1)S(1)}, u32[]{:S(2)}, u32[]{:S(2)}) async-start(bf16[16,16,1024]{2,1,0:T(8,128)(2,1)} %bitcast.35), calls=%async_computation.6 | async-start | bytes 1048576 | tf_op jit(solution)/shard_map/all_to_all | solution.py:56
  55.8 107.2 %all-gather.9.cloned.1.call-start = ((), (), s32[]{:S(2)}) async-start(), calls=%async_computation.11 | async-start | bytes 8912896 | tf_op jit(solution)/shard_map/all_gather | solution.py:11
  75.7 26.4 %all-to-all-start.3 = ((bf16[16,16,1024]{2,1,0:T(8,128)(2,1)}), bf16[16,16,1024]{2,1,0:T(8,128)(2,1)S(1)}, u32[]{:S(2)}, u32[]{:S(2)}) async-start(bf16[16,16,1024]{2,1,0:T(8,128)(2,1)} %bitcast.7), calls=%async_computation.3 | async-start | bytes 1048576 | tf_op jit(solution)/shard_map/all_to_all | solution.py:58
  102.1 26.8 %all-to-all-start.1 = ((bf16[16,16,1024]{2,1,0:T(8,128)(2,1)}), bf16[16,16,1024]{2,1,0:T(8,128)(2,1)S(1)}, u32[]{:S(2)}, u32[]{:S(2)}) async-start(bf16[16,16,1024]{2,1,0:T(8,128)(2,1)} %bitcast.2), calls=%async_computation.1 | async-start | bytes 1048576 | tf_op jit(solution)/shard_map/all_to_all | solution.py:57
  110.6 127.1 %all-gather.7.cloned.1.call-start = ((), (), s32[]{:S(2)}) async-start(), calls=%async_computation.10 | async-start | bytes 8912896 | tf_op jit(solution)/shard_map/all_gather | solution.py:11
  163.1 95.4 %copy-start = (f32[128,1024]{0,1:T(8,128)S(1)}, f32[128,1024]{0,1:T(8,128)}, u32[]{:S(2)}) copy-start(f32[128,1024]{0,1:T(8,128)} %copy.193) | copy-start | bytes 1572868
  294.4 10.1 %all-to-all-start.9 = ((bf16[16,16,8]{1,2,0:T(8,128)(2,1)}), bf16[16,16,8]{1,2,0:T(8,128)(2,1)S(1)}, u32[]{:S(2)}, u32[]{:S(2)}) async-start(bf16[16,16,8]{1,2,0:T(8,128)(2,1)} %copy.195), calls=%async_computation.9 | async-start | bytes 65536 | tf_op jit(solution)/shard_map/all_to_all | solution.py:171
  304.5 18.0 %all-to-all-start.8 = ((bf16[16,16,1024]{2,1,0:T(8,128)(2,1)}), bf16[16,16,1024]{2,1,0:T(8,128)(2,1)S(1)}, u32[]{:S(2)}, u32[]{:S(2)}) async-start(bf16[16,16,1024]{2,1,0:T(8,128)(2,1)} %bitcast.51), calls=%async_computation.8 | async-start | bytes 1048576 | tf_op jit(solution)/shard_map/all_to_all | solution.py:170
  322.5 18.5 %all-to-all-start.7 = ((bf16[16,16,1024]{2,1,0:T(8,128)(2,1)}), bf16[16,16,1024]{2,1,0:T(8,128)(2,1)S(1)}, u32[]{:S(2)}, u32[]{:S(2)}) async-start(bf16[16,16,1024]{2,1,0:T(8,128)(2,1)} %bitcast.44), calls=%async_computation.7 | async-start | bytes 1048576 | tf_op jit(solution)/shard_map/all_to_all | solution.py:169
  341.0 18.6 %all-to-all-start.5 = ((bf16[16,16,1024]{2,1,0:T(8,128)(2,1)}), bf16[16,16,1024]{2,1,0:T(8,128)(2,1)S(1)}, u32[]{:S(2)}, u32[]{:S(2)}) async-start(bf16[16,16,1024]{2,1,0:T(8,128)(2,1)} %bitcast.33), calls=%async_computation.5 | async-start | bytes 1048576 | tf_op jit(solution)/shard_map/all_to_all | solution.py:168
Sparse Core Ops, SparseCore 0:
  73.4 88.1 all-gather.8
  163.7 73.8 all-gather.6
where the time goes:
time: 371 us; the launch traced here: 368 us
  waiting for transfers between devices  154 us (42%)
  blocking collectives  55.7 us (15%)
  starting transfers between devices  46.3 us (12%)
  other arithmetic  43.7 us (12%)
  local copies, waits for them, and re-layouts  41.9 us (11%)
  between operations  16.4 us (4%)
  matrix products  8.11 us (2%)
    all_gather x2, waiting for transfers between devices, prefix(): everything = jax.tree.map(lambda part: lax.all_gather(part, axis), shard)  53.8 us
    select_n x48, other arithmetic, turn(): return jax.tree.map(lambda a, b: jnp.where(reached, a, b), new, before)  38 us
    unnamed x1, blocking collectives  31 us
    all_gather x1, blocking collectives, prefix(): everything = jax.tree.map(lambda part: lax.all_gather(part, axis), shard)  24.7 us
    all_to_all x1, waiting for transfers between devices, body(): lax.all_to_all(pack_rows(values), 'ctx', split_axis=0, concat_axis=0, til...  19.8 us
    all_to_all x1, waiting for transfers between devices, body(): lax.all_to_all(pack_rows(keys), 'ctx', split_axis=0, concat_axis=0, tiled...  16.3 us
    all_to_all x1, waiting for transfers between devices, body(): lax.all_to_all(chain_out(key_grad), 'ctx', split_axis=0, concat_axis=0, t...  12.3 us
    all_to_all x1, waiting for transfers between devices, body(): lax.all_to_all(chain_out(value_grad), 'ctx', split_axis=0, concat_axis=0,...  12.3 us
  transfers between devices with their start and end apart: 12, of which 11 were waited for; matrix products, arithmetic and copies ran while one was open for 17% of the time, Pallas kernels for 0%

commit v1 on v0

v1 whole, which is shorter than its diff:
```python
import functools

import jax
import jax.numpy as jnp
from jax import lax
from jax.experimental import pallas as pl
from jax.experimental.pallas import tpu as pltpu
from jax.sharding import PartitionSpec as P

SPAN = 128
META = 16
F32 = jnp.float32
BF16 = jnp.bfloat16
I32 = jnp.int32
VMEM = pl.BlockSpec(memory_space=pltpu.VMEM)
SMEM = pl.BlockSpec(memory_space=pltpu.SMEM)


def dot(a, b, dims):
    return lax.dot_general(a, b, ((dims[:1], dims[1:]), ((), ())), preferred_element_type=F32)


NN = (1, 0)
NT = (1, 1)
TN = (0, 0)


def iota(shape, dim):
    return lax.broadcasted_iota(I32, shape, dim)


def pack_kernel(chip_ref, q_ref, k_ref, v_ref, g_ref, ld_ref, pos_ref, *outs):
    rows = q_ref.shape[0]
    heads = len(outs)
    chip = chip_ref[0]
    eye = (iota((META, heads), 0) == iota((META, heads), 1)).astype(BF16)
    decay = dot(eye, ld_ref[...], NT)
    pos = pos_ref[...]
    line = iota((META, rows), 0)
    tail = jnp.where(line == 1, (pos // SPAN).astype(F32), jnp.where(line == 2, (pos % SPAN).astype(F32), 0.0))
    for s in range(heads):
        head = chip ^ s
        at = pl.ds(pl.multiple_of(head * SPAN, SPAN), SPAN)
        for n, ref in enumerate((q_ref, k_ref, v_ref, g_ref)):
            outs[s][n * rows:(n + 1) * rows, :] = ref[:, at]
        mine = jnp.sum(jnp.where(line == head, decay, 0.0), axis=0, keepdims=True)
        outs[s][4 * rows:, :] = jnp.where(line == 0, mine, tail).astype(BF16)


def segments(position, starts):
    total = jnp.zeros_like(position)
    for start in starts:
        total = total + (position >= start).astype(I32)
    return total


def chain_kernel(heads, lengths_ref, *refs):
    sources = len(refs) - heads - 12
    blocks, outs, scratch = refs[:sources], refs[sources:sources + heads], refs[sources + heads:]
    (x_ref, hi_ref, lo_ref, cum_ref, chain_ref, gained_ref, weighted_ref,
     carried_ref, pulled_ref, state_ref, grad_ref, tail_ref) = scratch
    rows = (blocks[0].shape[0] - META) // 4
    frames = rows * sources
    spans = frames // SPAN
    starts = []
    total = jnp.int32(0)
    for t in range(lengths_ref.shape[0]):
        starts.append(total)
        total = total + lengths_ref[t]

    for n, ref in enumerate(blocks):
        for a in range(4):
            x_ref[n * rows:(n + 1) * rows, a * SPAN:(a + 1) * SPAN] = ref[a * rows:(a + 1) * rows, :]
        meta = ref[4 * rows:, :].astype(F32)
        hi_ref[:, n * rows:(n + 1) * rows] = meta[1:2].astype(I32)
        lo_ref[:, n * rows:(n + 1) * rows] = meta[2:3].astype(I32)
    decay_parts = [ref[4 * rows:, :].astype(F32)[0:1] for ref in blocks]
    decay = jnp.concatenate(decay_parts, axis=1)
    hi = hi_ref[...]
    lo = lo_ref[...]
    pad = cum_ref.shape[0]
    spread = jnp.where(hi == iota((pad, frames), 0), decay, 0.0).astype(BF16)
    where_lo = (lo == iota((SPAN, frames), 0)).astype(BF16)
    in_chain = dot(spread, where_lo, NT).astype(BF16)
    upper = (iota((SPAN, SPAN), 0) <= iota((SPAN, SPAN), 1)).astype(BF16)
    cum_ref[...] = dot(in_chain, upper, NN)
    tail_ref[...] = jnp.zeros_like(tail_ref)

    row_i = iota((SPAN, SPAN), 0)
    col_j = iota((SPAN, SPAN), 1)

    def first(b):
        base = b * SPAN
        at = pl.ds(pl.multiple_of(base, SPAN), SPAN)
        key = jnp.where(hi_ref[...] == b, lo_ref[...], -1)
        hot = (key == iota((SPAN, frames), 0)).astype(BF16)
        chain = dot(hot, x_ref[...], NN).astype(BF16)
        chain_ref[at, :] = chain
        q, k, v, g = (chain[:, a * SPAN:(a + 1) * SPAN] for a in range(4))
        cum_j = cum_ref[pl.ds(b, 1), :]
        cum_i = jnp.transpose(jnp.broadcast_to(cum_j, (SPAN, SPAN)))
        last = cum_j[:, SPAN - 1:]
        seg_i = segments(base + row_i, starts)
        seg_j = segments(base + iota((1, SPAN), 1), starts)
        before = segments(jnp.full((1, 1), base - 1, I32), starts)
        end = segments(jnp.full((1, 1), base + SPAN - 1, I32), starts)
        same = seg_i == seg_j
        gap = cum_i - cum_j
        lower = same & (row_i >= col_j)
        higher = same & (row_i <= col_j)
        weight = jnp.where(lower, jnp.exp(jnp.where(lower, gap, 0.0)), 0.0)
        weight_t = jnp.where(higher, jnp.exp(jnp.where(higher, -gap, 0.0)), 0.0)
        query_gain = jnp.where(seg_i == before, jnp.exp(cum_i), 0.0)
        key_gain = jnp.where(seg_i == end, jnp.exp(last - cum_i), 0.0)
        key_end = (k.astype(F32) * key_gain).astype(BF16)
        query_start = (q.astype(F32) * query_gain).astype(BF16)
        gained_ref[at, 0:SPAN] = (g.astype(F32) * query_gain).astype(BF16)
        gained_ref[at, SPAN:2 * SPAN] = (v.astype(F32) * key_gain).astype(BF16)
        gained_ref[at, 2 * SPAN:] = key_end
        carried_ref[at, :] = dot(key_end, v, TN)
        pulled_ref[at, :] = dot(query_start, g, TN)
        weighted_ref[at, 0:SPAN] = (dot(g, v, NT) * weight).astype(BF16)
        weighted_ref[at, SPAN:2 * SPAN] = (dot(v, g, NT) * weight_t).astype(BF16)
        weighted_ref[at, 2 * SPAN:] = (dot(k, q, NT) * weight_t).astype(BF16)

    def second(b):
        base = b * SPAN
        at = pl.ds(pl.multiple_of(base, SPAN), SPAN)
        q, k, v, g = (chain_ref[at, a * SPAN:(a + 1) * SPAN] for a in range(4))
        state = state_ref[at, :]
        grad = grad_ref[at, :]
        dq = dot(weighted_ref[at, 0:SPAN], k, NN) + dot(gained_ref[at, 0:SPAN], state, NT)
        dk = dot(weighted_ref[at, SPAN:2 * SPAN], q, NN) + dot(gained_ref[at, SPAN:2 * SPAN], grad, NT)
        dv = dot(weighted_ref[at, 2 * SPAN:], g, NN) + dot(gained_ref[at, 2 * SPAN:], grad, NN)
        term = jnp.sum(q.astype(F32) * dq - k.astype(F32) * dk, axis=1, keepdims=True)
        seg_i = segments(base + row_i, starts)
        seg_j = segments(base + iota((1, SPAN), 1), starts)
        lower = (seg_i == seg_j) & (row_i >= col_j)
        tail_ref[pl.ds(b, 1), :] = jnp.sum(jnp.where(lower, term, 0.0), axis=0, keepdims=True)
        chain_ref[at, 0:SPAN] = dq.astype(BF16)
        chain_ref[at, SPAN:2 * SPAN] = dk.astype(BF16)
        chain_ref[at, 2 * SPAN:3 * SPAN] = dv.astype(BF16)

    step = 4 if spans % 4 == 0 else 1

    @pl.loop(0, spans // step)
    def _(turn):
        for u in range(step):
            first(turn * step + u)

    def fade(b):
        last = cum_ref[pl.ds(b, 1), SPAN - 1:]
        before = segments(jnp.full((1, 1), b * SPAN - 1, I32), starts)
        end = segments(jnp.full((1, 1), b * SPAN + SPAN - 1, I32), starts)
        return jnp.where(before == end, jnp.exp(last), 0.0)

    def scan(turn, held):
        state, grad = held
        b, c = turn, spans - 1 - turn
        at_b = pl.ds(pl.multiple_of(b * SPAN, SPAN), SPAN)
        at_c = pl.ds(pl.multiple_of(c * SPAN, SPAN), SPAN)
        state_ref[at_b, :] = state.astype(BF16)
        grad_ref[at_c, :] = grad.astype(BF16)
        return fade(b) * state + carried_ref[at_b, :], fade(c) * grad + pulled_ref[at_c, :]

    empty = jnp.zeros((SPAN, SPAN), F32)
    lax.fori_loop(0, spans, scan, (empty, empty))

    @pl.loop(0, spans // step)
    def _(turn):
        for u in range(step):
            second(turn * step + u)

    local = tail_ref[...]
    firsts = jnp.transpose(local)[0:1, :]
    seg_last = segments(row_i * SPAN + SPAN - 1, starts)
    seg_first = segments(col_j * SPAN, starts)
    later = (col_j > row_i) & (seg_first == seg_last)
    carry = jnp.sum(jnp.where(later, firsts, 0.0), axis=1, keepdims=True)
    place = row_i * SPAN + col_j
    full = local + jnp.where(segments(place, starts) == seg_last, carry, 0.0)
    begins = place == starts[0]
    for start in starts[1:]:
        begins = begins | (place == start)
    tails = jnp.where(begins, 0.0, full).astype(BF16)

    wanted = hi_ref[:, :heads * rows] * SPAN + lo_ref[:, :heads * rows]
    for s in range(heads):
        part = slice(s * rows, (s + 1) * rows)
        where_row = jnp.broadcast_to(wanted[:, part].astype(F32), (SPAN, rows))
        where_col = jnp.transpose(where_row)[:, 0:1].astype(I32)
        hot = (where_col == iota((rows, frames), 1)).astype(BF16)
        back = dot(hot, chain_ref[:, 0:3 * SPAN], NN).astype(BF16)
        for a in range(3):
            outs[s][a * rows:(a + 1) * rows, :] = back[:, a * SPAN:(a + 1) * SPAN]
        hot_lo = (lo_ref[:, part] == iota((SPAN, rows), 0)).astype(BF16)
        found = dot(tails, hot_lo, NN)
        found = jnp.sum(jnp.where(hi_ref[:, part] == iota((SPAN, rows), 0), found, 0.0), axis=0, keepdims=True)
        outs[s][3 * rows:, :] = jnp.broadcast_to(found, (META, rows)).astype(BF16)


def unpack_kernel(chip_ref, *refs):
    heads = len(refs) - 4
    blocks, outs = refs[:heads], refs[heads:]
    rows = outs[0].shape[0]
    chip = chip_ref[0]
    line = iota((SPAN, rows), 0)
    tails = jnp.zeros((SPAN, rows), F32)
    for s in range(heads):
        head = chip ^ s
        at = pl.ds(pl.multiple_of(head * SPAN, SPAN), SPAN)
        for a in range(3):
            outs[a][:, at] = blocks[s][a * rows:(a + 1) * rows, :]
        tails = jnp.where(line == head, blocks[s][3 * rows:, :].astype(F32)[0:1], tails)
    outs[3][...] = jnp.transpose(tails)[:, :heads].astype(BF16)


def body(queries, keys, values, out_grad, log_decay, frame_pos, trial_lengths):
    rows, width = queries.shape
    heads = log_decay.shape[1]
    peers = lax.axis_size("ctx")
    cores = peers // heads
    frames = rows * peers
    spans = frames // SPAN
    chip = (lax.axis_index("ctx") // cores).astype(I32).reshape(1)

    def across(x, s):
        return lax.ppermute(x, "ctx", [(p, p ^ (s * cores)) for p in range(peers)])

    def beside(x, t):
        return lax.ppermute(x, "ctx", [(p, p ^ t) for p in range(peers)])

    packets = pl.pallas_call(
        pack_kernel,
        out_shape=[jax.ShapeDtypeStruct((4 * rows + META, SPAN), BF16)] * heads,
        in_specs=[SMEM] + [VMEM] * 6,
        out_specs=[VMEM] * heads,
        name="pack",
    )(chip, queries, keys, values, out_grad, log_decay, frame_pos.reshape(1, rows))
    got = list(packets)
    for s in (6, 7, 4, 5, 2, 3, 1):
        got[s] = across(packets[s], s)
    everything = list(got)
    for t in range(1, cores):
        everything += [beside(x, t) for x in got]

    tall = max(SPAN, spans)
    back = pl.pallas_call(
        functools.partial(chain_kernel, heads),
        out_shape=[jax.ShapeDtypeStruct((3 * rows + META, SPAN), BF16)] * heads,
        in_specs=[SMEM] + [VMEM] * peers,
        out_specs=[VMEM] * heads,
        scratch_shapes=[
            pltpu.VMEM((frames, 4 * SPAN), BF16),
            pltpu.VMEM((1, frames), I32),
            pltpu.VMEM((1, frames), I32),
            pltpu.VMEM((tall, SPAN), F32),
            pltpu.VMEM((frames, 4 * SPAN), BF16),
            pltpu.VMEM((frames, 3 * SPAN), BF16),
            pltpu.VMEM((frames, 3 * SPAN), BF16),
            pltpu.VMEM((frames, SPAN), F32),
            pltpu.VMEM((frames, SPAN), F32),
            pltpu.VMEM((frames, SPAN), BF16),
            pltpu.VMEM((frames, SPAN), BF16),
            pltpu.VMEM((tall, SPAN), F32),
        ],
        compiler_params=pltpu.CompilerParams(vmem_limit_bytes=60 * 2**20),
        name="chain",
    )(trial_lengths, *everything)
    returned = list(back)
    for s in (6, 7, 4, 5, 2, 3, 1):
        returned[s] = across(back[s], s)

    return tuple(pl.pallas_call(
        unpack_kernel,
        out_shape=[jax.ShapeDtypeStruct((rows, width), BF16)] * 3 + [jax.ShapeDtypeStruct((rows, heads), BF16)],
        in_specs=[SMEM] + [VMEM] * heads,
        out_specs=[VMEM] * 4,
        name="unpack",
    )(chip, *returned))


def solution(mesh):
    rows = P(("groups", "ctx"), None)
    return jax.shard_map(
        body,
        mesh=mesh,
        in_specs=(rows, rows, rows, rows, rows, P(("groups", "ctx")), P("groups")),
        out_specs=(rows, rows, rows, rows),
        check_vma=False,
    )
```

time: 371 us -> 87.6 us (0.24)
  waiting for transfers between devices: 154 us -> 26 us
  blocking collectives: 55.7 us -> 0 us
  other arithmetic: 43.7 us -> 0 us
  local copies, waits for them, and re-layouts: 41.9 us -> 4.41 us
  Pallas kernels: 0 us -> 25.6 us
  starting transfers between devices: 46.3 us -> 29.6 us
  between operations: 16.4 us -> 0.85 us
  matrix products: 8.11 us -> 0 us
    all_to_all x10 -> x0, waiting for transfers between devices: 101 us -> none  [the longest x1 19.8 us: body(): lax.all_to_all(pack_rows(values), 'ctx', split_axis=0, concat_axis=0, til...]
    all_gather x2 -> x0, waiting for transfers between devices: 53.8 us -> none  [prefix(): everything = jax.tree.map(lambda part: lax.all_gather(part, axis), shard)]
    all_to_all x10 -> x0, starting transfers between devices: 46.2 us -> none  [the longest x1 8.45 us: body(): lax.all_to_all(pack_rows(keys), 'ctx', split_axis=0, concat_axis=0, tiled...]
    select_n x52 -> x0, other arithmetic: 38.7 us -> none  [the longest x48 38 us: turn(): return jax.tree.map(lambda a, b: jnp.where(reached, a, b), new, before)]
    unnamed x1 -> x0, blocking collectives: 31 us -> none
    ppermute x0 -> x22, starting transfers between devices: none -> 29.6 us  [the longest x14 27.8 us: across(): return lax.ppermute(x, 'ctx', [(p, p ^ s * cores) for p in range(peers)])]
    ppermute x0 -> x22, waiting for transfers between devices: none -> 26 us  [the longest x14 24.6 us: across(): return lax.ppermute(x, 'ctx', [(p, p ^ s * cores) for p in range(peers)])]
    pallas_call x0 -> x3, Pallas kernels: none -> 25.6 us  [the longest x1 20.9 us: body(): pl.pallas_call(functools.partial(chain_kernel, heads), out_shape=[jax.Sha...]
  transfers between devices with their start and end apart: 12 -> 22, of which waited for: 11 -> 8; matrix products, arithmetic and copies ran while one was open for 17% -> 0% of each run, Pallas kernels for 0% -> 0%
where the time goes in v1:
time: 87.6 us; the launch traced here: 86.5 us
  starting transfers between devices  29.6 us (34%)
  waiting for transfers between devices  26 us (30%)
  Pallas kernels  25.6 us (29%)
  local copies, waits for them, and re-layouts  4.41 us (5%)
    ppermute x14, starting transfers between devices, across(): return lax.ppermute(x, 'ctx', [(p, p ^ s * cores) for p in range(peers)])  27.8 us
    ppermute x14, waiting for transfers between devices, across(): return lax.ppermute(x, 'ctx', [(p, p ^ s * cores) for p in range(peers)])  24.6 us
    pallas_call x1, Pallas kernels, body(): pl.pallas_call(functools.partial(chain_kernel, heads), out_shape=[jax.Sha...  20.9 us
    unnamed x47, local copies, waits for them, and re-layouts  3.01 us
    pallas_call x1, Pallas kernels, body(): pl.pallas_call(pack_kernel, out_shape=[jax.ShapeDtypeStruct((4 * rows + M...  2.41 us
    pallas_call x1, Pallas kernels, body(): pl.pallas_call(unpack_kernel, out_shape=[jax.ShapeDtypeStruct((rows, widt...  2.33 us
    ppermute x8, starting transfers between devices, beside(): return lax.ppermute(x, 'ctx', [(p, p ^ t) for p in range(peers)])  1.79 us
  transfers between devices with their start and end apart: 22, of which 8 were waited for; matrix products, arithmetic and copies ran while one was open for 0% of the time, Pallas kernels for 0%

profile of v1, /device:TPU:0, one launch (start us, length us, event | category | flops | bytes accessed | tf_op | source)
XLA Modules:
  0.0 86.5 jit_solution(14590615206332231337)
XLA Ops:
  0.6 0.0 copy-start.22
  0.6 0.7 copy-done.22
  1.3 0.7 copy.11.ld_ref
  2.0 2.4 %pack.1 = (bf16[528,128]{1,0:T(8,128)(2,1)}, bf16[528,128]{1,0:T(8,128)(2,1)}, bf16[528,128]{1,0:T(8,128)(2,1)}, bf16[528,128]{1,0:T(8,128)(2,1)}, bf16[528,128]...) custom-call(s32[1]{0:T(128)} %bitcast.chip_ref, ...), custom_call_target="tpu_custom_call" | custom-call | tf_op jit(solution)/shard_map/pack/pallas_call | solution.py:233
  4.4 3.0 %collective-permute-start = (bf16[528,128]{1,0:T(8,128)(2,1)}, bf16[528,128]{1,0:T(8,128)(2,1)S(1)}, u32[]{:S(2)}, u32[]{:S(2)}) collective-permute-start(bf16[528,128]{1,0:T(8,128)(2,1)} %get-tuple-element.21), channel_id=1, source_target_pairs={{0,2},{1,3},{2,0},{3,1},{4,6},{5,7},{6,4},{7,5},{8,10},{9,11},{10,... | collective-permute-start | bytes 405512 | tf_op jit(solution)/shard_map/ppermute | solution.py:228
  7.4 1.6 %collective-permute-start.1 = (bf16[528,128]{1,0:T(8,128)(2,1)}, bf16[528,128]{1,0:T(8,128)(2,1)S(1)}, u32[]{:S(2)}, u32[]{:S(2)}) collective-permute-start(bf16[528,128]{1,0:T(8,128)(2,1)} %get-tuple-element.22), channel_id=1, source_target_pairs={{0,4},{1,5},{2,6},{3,7},{4,0},{5,1},{6,2},{7,3},{8,12},{9,13},{10,... | collective-permute-start | bytes 405512 | tf_op jit(solution)/shard_map/ppermute | solution.py:228
  9.0 0.0 collective-permute-start.2
  9.0 3.0 %collective-permute-start.3 = (bf16[528,128]{1,0:T(8,128)(2,1)}, bf16[528,128]{1,0:T(8,128)(2,1)S(1)}, u32[]{:S(2)}, u32[]{:S(2)}) collective-permute-start(bf16[528,128]{1,0:T(8,128)(2,1)} %get-tuple-element.24), channel_id=1, source_target_pairs={{0,8},{1,9},{2,10},{3,11},{4,12},{5,13},{6,14},{7,15},{8,0},{9,1},... | collective-permute-start | bytes 405512 | tf_op jit(solution)/shard_map/ppermute | solution.py:228
  12.0 1.3 %collective-permute-start.4 = (bf16[528,128]{1,0:T(8,128)(2,1)}, bf16[528,128]{1,0:T(8,128)(2,1)S(1)}, u32[]{:S(2)}, u32[]{:S(2)}) collective-permute-start(bf16[528,128]{1,0:T(8,128)(2,1)} %get-tuple-element.25), channel_id=1, source_target_pairs={{0,10},{1,11},{2,8},{3,9},{4,14},{5,15},{6,12},{7,13},{8,2},{9,3},... | collective-permute-start | bytes 405512 | tf_op jit(solution)/shard_map/ppermute | solution.py:228
  13.3 0.0 collective-permute-done.refs_1_
  13.3 3.6 %collective-permute-start.5 = (bf16[528,128]{1,0:T(8,128)(2,1)}, bf16[528,128]{1,0:T(8,128)(2,1)S(1)}, u32[]{:S(2)}, u32[]{:S(2)}) collective-permute-start(bf16[528,128]{1,0:T(8,128)(2,1)} %get-tuple-element.26), channel_id=1, source_target_pairs={{0,12},{1,13},{2,14},{3,15},{4,8},{5,9},{6,10},{7,11},{8,4},{9,5},... | collective-permute-start | bytes 405512 | tf_op jit(solution)/shard_map/ppermute | solution.py:228
  16.9 1.8 %collective-permute-done.1.refs_2_ = bf16[528,128]{1,0:T(8,128)(2,1)S(1)} collective-permute-done((bf16[528,128]{1,0:T(8,128)(2,1)}, bf16[528,128]{1,0:T(8,128)(2,1)S(1)}, u32[]{:S(2)}, u32[]{:S(2)}) %collective-permute-start.1) | collective-permute-done | bytes 135200 | tf_op jit(solution)/shard_map/ppermute | solution.py:228
  18.7 0.8 collective-permute-start.6
  19.5 0.0 collective-permute-done.2.refs_3_
  19.5 0.0 collective-permute-start.7
  19.5 0.0 collective-permute-done.3.refs_4_
  19.5 0.0 copy-start.3
  19.5 0.5 collective-permute-start.8
  20.0 12.1 %collective-permute-done.4.refs_5_ = bf16[528,128]{1,0:T(8,128)(2,1)S(1)} collective-permute-done((bf16[528,128]{1,0:T(8,128)(2,1)}, bf16[528,128]{1,0:T(8,128)(2,1)S(1)}, u32[]{:S(2)}, u32[]{:S(2)}) %collective-permute-start.4) | collective-permute-done | bytes 135200 | tf_op jit(solution)/shard_map/ppermute | solution.py:228
  32.1 0.0 collective-permute-start.9
  32.1 0.0 collective-permute-done.5.refs_6_
  32.1 0.0 copy-start.5
  32.1 0.5 collective-permute-start.10
  32.6 0.0 collective-permute-done.6.refs_7_
  32.6 0.1 collective-permute-start.11
  32.7 0.0 collective-permute-done.7.refs_8_
  32.7 0.4 collective-permute-start.12
  33.2 0.0 collective-permute-done.8.refs_9_
  33.2 0.1 collective-permute-start.13
  33.2 0.2 collective-permute-done.9.refs_10_
  33.5 0.2 collective-permute-start.14
  33.7 0.0 collective-permute-done.10.refs_11_
  33.7 0.3 collective-permute-done.11.refs_12_
  34.0 0.2 collective-permute-done.12.refs_13_
  34.2 0.3 collective-permute-done.13.refs_14_
  34.5 0.3 collective-permute-done.14.refs_15_
  34.9 0.2 copy-done.13
  35.2 0.6 copy-done.14
  35.8 20.9 %chain.1 = (bf16[400,128]{1,0:T(8,128)(2,1)}, bf16[400,128]{1,0:T(8,128)(2,1)}, bf16[400,128]{1,0:T(8,128)(2,1)}, bf16[400,128]{1,0:T(8,128)(2,1)}, bf16[400,128...) custom-call(s32[8]{0:T(128)} %lengths_ref.1, ...), custom_call_target="tpu_custom_call" | custom-call | tf_op jit(solution)/shard_map/chain/pallas_call | solution.py:248
  56.7 0.8 collective-permute-start.15
  57.5 4.3 %collective-permute-start.16 = (bf16[400,128]{1,0:T(8,128)(2,1)}, bf16[400,128]{1,0:T(8,128)(2,1)S(1)}, u32[]{:S(2)}, u32[]{:S(2)}) collective-permute-start(bf16[400,128]{1,0:T(8,128)(2,1)} %get-tuple-element.30), channel_id=1, source_target_pairs={{0,4},{1,5},{2,6},{3,7},{4,0},{5,1},{6,2},{7,3},{8,12},{9,13},{10,... | collective-permute-start | bytes 307208 | tf_op jit(solution)/shard_map/ppermute | solution.py:228
  61.7 1.1 %collective-permute-start.17 = (bf16[400,128]{1,0:T(8,128)(2,1)}, bf16[400,128]{1,0:T(8,128)(2,1)S(1)}, u32[]{:S(2)}, u32[]{:S(2)}) collective-permute-start(bf16[400,128]{1,0:T(8,128)(2,1)} %get-tuple-element.31), channel_id=1, source_target_pairs={{0,6},{1,7},{2,4},{3,5},{4,2},{5,3},{6,0},{7,1},{8,14},{9,15},{10,... | collective-permute-start | bytes 307208 | tf_op jit(solution)/shard_map/ppermute | solution.py:228
  62.8 3.6 %collective-permute-start.18 = (bf16[400,128]{1,0:T(8,128)(2,1)}, bf16[400,128]{1,0:T(8,128)(2,1)S(1)}, u32[]{:S(2)}, u32[]{:S(2)}) collective-permute-start(bf16[400,128]{1,0:T(8,128)(2,1)} %get-tuple-element.32), channel_id=1, source_target_pairs={{0,8},{1,9},{2,10},{3,11},{4,12},{5,13},{6,14},{7,15},{8,0},{9,1},... | collective-permute-start | bytes 307208 | tf_op jit(solution)/shard_map/ppermute | solution.py:228
  66.5 0.0 collective-permute-start.19
  66.5 0.0 collective-permute-done.15.refs_1_
  66.5 2.4 %collective-permute-start.20 = (bf16[400,128]{1,0:T(8,128)(2,1)}, bf16[400,128]{1,0:T(8,128)(2,1)S(1)}, u32[]{:S(2)}, u32[]{:S(2)}) collective-permute-start(bf16[400,128]{1,0:T(8,128)(2,1)} %get-tuple-element.34), channel_id=1, source_target_pairs={{0,12},{1,13},{2,14},{3,15},{4,8},{5,9},{6,10},{7,11},{8,4},{9,5},... | collective-permute-start | bytes 307208 | tf_op jit(solution)/shard_map/ppermute | solution.py:228
  68.8 0.0 collective-permute-done.16.refs_2_
  68.9 2.5 %collective-permute-start.21 = (bf16[400,128]{1,0:T(8,128)(2,1)}, bf16[400,128]{1,0:T(8,128)(2,1)S(1)}, u32[]{:S(2)}, u32[]{:S(2)}) collective-permute-start(bf16[400,128]{1,0:T(8,128)(2,1)} %get-tuple-element.35), channel_id=1, source_target_pairs={{0,14},{1,15},{2,12},{3,13},{4,10},{5,11},{6,8},{7,9},{8,6},{9,7},... | collective-permute-start | bytes 307208 | tf_op jit(solution)/shard_map/ppermute | solution.py:228
  71.4 0.0 collective-permute-done.17.refs_3_
  71.4 0.0 collective-permute-done.18.refs_4_
  71.4 0.0 copy-start.18
  71.4 10.6 %collective-permute-done.19.refs_5_ = bf16[400,128]{1,0:T(8,128)(2,1)S(1)} collective-permute-done((bf16[400,128]{1,0:T(8,128)(2,1)}, bf16[400,128]{1,0:T(8,128)(2,1)S(1)}, u32[]{:S(2)}, u32[]{:S(2)}) %collective-permute-start.19) | collective-permute-done | bytes 102432 | tf_op jit(solution)/shard_map/ppermute | solution.py:228
  82.0 0.0 collective-permute-done.20.refs_6_
  82.0 0.0 collective-permute-done.21.refs_7_
  82.0 0.0 copy-start.21
  82.0 0.0 copy-done.15
  82.0 0.0 copy-done.16
  82.1 0.0 copy-done.17
  82.1 0.0 copy-done.18
  82.1 0.6 copy-done.19
  82.6 0.1 copy-done.20
  82.7 0.1 copy-done.21
  82.8 2.3 %unpack.1 = (bf16[128,1024]{1,0:T(8,128)(2,1)}, bf16[128,1024]{1,0:T(8,128)(2,1)}, bf16[128,1024]{1,0:T(8,128)(2,1)}, bf16[128,8]{1,0:T(8,128)(2,1)}) custom-call(s32[1]{0:T(128)} %bitcast.chip_ref, bf16[400,128]{1,0:T(8,128)(2,1)} %get-tuple-element.28.refs_0_, bf16[400,128]{1,0:T(8,128)(2,1)} %copy-done.15, bf16[400,128]{1,0:T(8,128)(2,1)} %copy-done.16, ...), custom_call_target="tpu_custom_call" | custom-call | tf_op jit(solution)/shard_map/unpack/pallas_call | solution.py:274
  85.1 1.4 %copy.12 = bf16[128,8]{0,1:T(8,128)(2,1)} copy(bf16[128,8]{1,0:T(8,128)(2,1)} %get-tuple-element.39) | data formatting | bytes 4096 | tf_op jit(solution)/shard_map/unpack/pallas_call | solution.py:274
  (31 shorter events, 0.1 us)
Async XLA Ops:
  0.6 0.7 copy-start.22
  4.4 8.8 %collective-permute-start = (bf16[528,128]{1,0:T(8,128)(2,1)}, bf16[528,128]{1,0:T(8,128)(2,1)S(1)}, u32[]{:S(2)}, u32[]{:S(2)}) collective-permute-start(bf16[528,128]{1,0:T(8,128)(2,1)} %get-tuple-element.21), channel_id=1, source_target_pairs={{0,2},{1,3},{2,0},{3,1},{4,6},{5,7},{6,4},{7,5},{8,10},{9,11},{10,... | collective-permute-start | bytes 405512 | tf_op jit(solution)/shard_map/ppermute | solution.py:228
  7.4 11.3 %collective-permute-start.1 = (bf16[528,128]{1,0:T(8,128)(2,1)}, bf16[528,128]{1,0:T(8,128)(2,1)S(1)}, u32[]{:S(2)}, u32[]{:S(2)}) collective-permute-start(bf16[528,128]{1,0:T(8,128)(2,1)} %get-tuple-element.22), channel_id=1, source_target_pairs={{0,4},{1,5},{2,6},{3,7},{4,0},{5,1},{6,2},{7,3},{8,12},{9,13},{10,... | collective-permute-start | bytes 405512 | tf_op jit(solution)/shard_map/ppermute | solution.py:228
  9.0 10.5 %collective-permute-start.2 = (bf16[528,128]{1,0:T(8,128)(2,1)}, bf16[528,128]{1,0:T(8,128)(2,1)S(1)}, u32[]{:S(2)}, u32[]{:S(2)}) collective-permute-start(bf16[528,128]{1,0:T(8,128)(2,1)} %get-tuple-element.23), channel_id=1, source_target_pairs={{0,6},{1,7},{2,4},{3,5},{4,2},{5,3},{6,0},{7,1},{8,14},{9,15},{10,... | collective-permute-start | bytes 405512 | tf_op jit(solution)/shard_map/ppermute | solution.py:228
  9.0 10.5 %collective-permute-start.3 = (bf16[528,128]{1,0:T(8,128)(2,1)}, bf16[528,128]{1,0:T(8,128)(2,1)S(1)}, u32[]{:S(2)}, u32[]{:S(2)}) collective-permute-start(bf16[528,128]{1,0:T(8,128)(2,1)} %get-tuple-element.24), channel_id=1, source_target_pairs={{0,8},{1,9},{2,10},{3,11},{4,12},{5,13},{6,14},{7,15},{8,0},{9,1},... | collective-permute-start | bytes 405512 | tf_op jit(solution)/shard_map/ppermute | solution.py:228
  12.0 20.1 %collective-permute-start.4 = (bf16[528,128]{1,0:T(8,128)(2,1)}, bf16[528,128]{1,0:T(8,128)(2,1)S(1)}, u32[]{:S(2)}, u32[]{:S(2)}) collective-permute-start(bf16[528,128]{1,0:T(8,128)(2,1)} %get-tuple-element.25), channel_id=1, source_target_pairs={{0,10},{1,11},{2,8},{3,9},{4,14},{5,15},{6,12},{7,13},{8,2},{9,3},... | collective-permute-start | bytes 405512 | tf_op jit(solution)/shard_map/ppermute | solution.py:228
  13.3 21.6 %copy-start = (bf16[528,128]{1,0:T(8,128)(2,1)}, bf16[528,128]{1,0:T(8,128)(2,1)S(1)}, u32[]{:S(2)}) copy-start(bf16[528,128]{1,0:T(8,128)(2,1)S(1)} %collective-permute-done.refs_1_) | copy-start | bytes 405508
  13.3 18.9 %collective-permute-start.5 = (bf16[528,128]{1,0:T(8,128)(2,1)}, bf16[528,128]{1,0:T(8,128)(2,1)S(1)}, u32[]{:S(2)}, u32[]{:S(2)}) collective-permute-start(bf16[528,128]{1,0:T(8,128)(2,1)} %get-tuple-element.26), channel_id=1, source_target_pairs={{0,12},{1,13},{2,14},{3,15},{4,8},{5,9},{6,10},{7,11},{8,4},{9,5},... | collective-permute-start | bytes 405512 | tf_op jit(solution)/shard_map/ppermute | solution.py:228
  18.7 16.1 %copy-start.1 = (bf16[528,128]{1,0:T(8,128)(2,1)}, bf16[528,128]{1,0:T(8,128)(2,1)S(1)}, u32[]{:S(2)}) copy-start(bf16[528,128]{1,0:T(8,128)(2,1)S(1)} %collective-permute-done.1.refs_2_) | copy-start | bytes 405508
  18.7 13.9 %collective-permute-start.6 = (bf16[528,128]{1,0:T(8,128)(2,1)}, bf16[528,128]{1,0:T(8,128)(2,1)S(1)}, u32[]{:S(2)}, u32[]{:S(2)}) collective-permute-start(bf16[528,128]{1,0:T(8,128)(2,1)} %get-tuple-element.27), channel_id=1, source_target_pairs={{0,14},{1,15},{2,12},{3,13},{4,10},{5,11},{6,8},{7,9},{8,6},{9,7},... | collective-permute-start | bytes 405512 | tf_op jit(solution)/shard_map/ppermute | solution.py:228
  19.5 15.4 %copy-start.2 = (bf16[528,128]{1,0:T(8,128)(2,1)}, bf16[528,128]{1,0:T(8,128)(2,1)S(1)}, u32[]{:S(2)}) copy-start(bf16[528,128]{1,0:T(8,128)(2,1)S(1)} %collective-permute-done.2.refs_3_) | copy-start | bytes 405508
  19.5 13.3 %collective-permute-start.7 = (bf16[528,128]{1,0:T(8,128)(2,1)}, bf16[528,128]{1,0:T(8,128)(2,1)S(1)}, u32[]{:S(2)}, u32[]{:S(2)}) collective-permute-start(bf16[528,128]{1,0:T(8,128)(2,1)} %get-tuple-element.20.refs_0_), channel_id=1, source_target_pairs={{0,1},{1,0},{2,3},{3,2},{4,5},{5,4},{6,7},{7,6},{8,9},{9,8},{10,11... | collective-permute-start | bytes 405512 | tf_op jit(solution)/shard_map/ppermute | solution.py:231
  19.5 15.4 %copy-start.3 = (bf16[528,128]{1,0:T(8,128)(2,1)}, bf16[528,128]{1,0:T(8,128)(2,1)S(1)}, u32[]{:S(2)}) copy-start(bf16[528,128]{1,0:T(8,128)(2,1)S(1)} %collective-permute-done.3.refs_4_) | copy-start | bytes 405508
  19.5 13.7 %collective-permute-start.8 = (bf16[528,128]{1,0:T(8,128)(2,1)S(1)}, bf16[528,128]{1,0:T(8,128)(2,1)S(1)}, u32[]{:S(2)}, u32[]{:S(2)}) collective-permute-start(bf16[528,128]{1,0:T(8,128)(2,1)S(1)} %collective-permute-done.refs_1_), channel_id=1, source_target_pairs={{0,1},{1,0},{2,3},{3,2},{4,5},{5,4},{6,7},{7,6},{8,9},{9,8},{10,11... | collective-permute-start | bytes 405512 | tf_op jit(solution)/shard_map/ppermute | solution.py:231
  32.1 2.7 %copy-start.4 = (bf16[528,128]{1,0:T(8,128)(2,1)}, bf16[528,128]{1,0:T(8,128)(2,1)S(1)}, u32[]{:S(2)}) copy-start(bf16[528,128]{1,0:T(8,128)(2,1)S(1)} %collective-permute-done.4.refs_5_) | copy-start | bytes 405508
  32.1 1.4 %collective-permute-start.9 = (bf16[528,128]{1,0:T(8,128)(2,1)S(1)}, bf16[528,128]{1,0:T(8,128)(2,1)S(1)}, u32[]{:S(2)}, u32[]{:S(2)}) collective-permute-start(bf16[528,128]{1,0:T(8,128)(2,1)S(1)} %collective-permute-done.1.refs_2_), channel_id=1, source_target_pairs={{0,1},{1,0},{2,3},{3,2},{4,5},{5,4},{6,7},{7,6},{8,9},{9,8},{10,11... | collective-permute-start | bytes 405512 | tf_op jit(solution)/shard_map/ppermute | solution.py:231
  32.1 2.7 %copy-start.5 = (bf16[528,128]{1,0:T(8,128)(2,1)}, bf16[528,128]{1,0:T(8,128)(2,1)S(1)}, u32[]{:S(2)}) copy-start(bf16[528,128]{1,0:T(8,128)(2,1)S(1)} %collective-permute-done.5.refs_6_) | copy-start | bytes 405508
  32.1 1.5 %collective-permute-start.10 = (bf16[528,128]{1,0:T(8,128)(2,1)S(1)}, bf16[528,128]{1,0:T(8,128)(2,1)S(1)}, u32[]{:S(2)}, u32[]{:S(2)}) collective-permute-start(bf16[528,128]{1,0:T(8,128)(2,1)S(1)} %collective-permute-done.2.refs_3_), channel_id=1, source_target_pairs={{0,1},{1,0},{2,3},{3,2},{4,5},{5,4},{6,7},{7,6},{8,9},{9,8},{10,11... | collective-permute-start | bytes 405512 | tf_op jit(solution)/shard_map/ppermute | solution.py:231
  32.6 2.2 %copy-start.6 = (bf16[528,128]{1,0:T(8,128)(2,1)}, bf16[528,128]{1,0:T(8,128)(2,1)S(1)}, u32[]{:S(2)}) copy-start(bf16[528,128]{1,0:T(8,128)(2,1)S(1)} %collective-permute-done.6.refs_7_) | copy-start | bytes 405508
  32.6 1.4 %collective-permute-start.11 = (bf16[528,128]{1,0:T(8,128)(2,1)S(1)}, bf16[528,128]{1,0:T(8,128)(2,1)S(1)}, u32[]{:S(2)}, u32[]{:S(2)}) collective-permute-start(bf16[528,128]{1,0:T(8,128)(2,1)S(1)} %collective-permute-done.3.refs_4_), channel_id=1, source_target_pairs={{0,1},{1,0},{2,3},{3,2},{4,5},{5,4},{6,7},{7,6},{8,9},{9,8},{10,11... | collective-permute-start | bytes 405512 | tf_op jit(solution)/shard_map/ppermute | solution.py:231
  32.7 2.2 %copy-start.7 = (bf16[528,128]{1,0:T(8,128)(2,1)}, bf16[528,128]{1,0:T(8,128)(2,1)S(1)}, u32[]{:S(2)}) copy-start(bf16[528,128]{1,0:T(8,128)(2,1)S(1)} %collective-permute-done.7.refs_8_) | copy-start | bytes 405508
  32.7 1.5 %collective-permute-start.12 = (bf16[528,128]{1,0:T(8,128)(2,1)S(1)}, bf16[528,128]{1,0:T(8,128)(2,1)S(1)}, u32[]{:S(2)}, u32[]{:S(2)}) collective-permute-start(bf16[528,128]{1,0:T(8,128)(2,1)S(1)} %collective-permute-done.4.refs_5_), channel_id=1, source_target_pairs={{0,1},{1,0},{2,3},{3,2},{4,5},{5,4},{6,7},{7,6},{8,9},{9,8},{10,11... | collective-permute-start | bytes 405512 | tf_op jit(solution)/shard_map/ppermute | solution.py:231
  33.2 1.7 %copy-start.8 = (bf16[528,128]{1,0:T(8,128)(2,1)}, bf16[528,128]{1,0:T(8,128)(2,1)S(1)}, u32[]{:S(2)}) copy-start(bf16[528,128]{1,0:T(8,128)(2,1)S(1)} %collective-permute-done.8.refs_9_) | copy-start | bytes 405508
  33.2 1.4 %collective-permute-start.13 = (bf16[528,128]{1,0:T(8,128)(2,1)S(1)}, bf16[528,128]{1,0:T(8,128)(2,1)S(1)}, u32[]{:S(2)}, u32[]{:S(2)}) collective-permute-start(bf16[528,128]{1,0:T(8,128)(2,1)S(1)} %collective-permute-done.5.refs_6_), channel_id=1, source_target_pairs={{0,1},{1,0},{2,3},{3,2},{4,5},{5,4},{6,7},{7,6},{8,9},{9,8},{10,11... | collective-permute-start | bytes 405512 | tf_op jit(solution)/shard_map/ppermute | solution.py:231
  33.5 1.4 %copy-start.9 = (bf16[528,128]{1,0:T(8,128)(2,1)}, bf16[528,128]{1,0:T(8,128)(2,1)S(1)}, u32[]{:S(2)}) copy-start(bf16[528,128]{1,0:T(8,128)(2,1)S(1)} %collective-permute-done.9.refs_10_) | copy-start | bytes 405508
  33.5 1.4 %collective-permute-start.14 = (bf16[528,128]{1,0:T(8,128)(2,1)S(1)}, bf16[528,128]{1,0:T(8,128)(2,1)S(1)}, u32[]{:S(2)}, u32[]{:S(2)}) collective-permute-start(bf16[528,128]{1,0:T(8,128)(2,1)S(1)} %collective-permute-done.6.refs_7_), channel_id=1, source_target_pairs={{0,1},{1,0},{2,3},{3,2},{4,5},{5,4},{6,7},{7,6},{8,9},{9,8},{10,11... | collective-permute-start | bytes 405512 | tf_op jit(solution)/shard_map/ppermute | solution.py:231
  33.7 1.2 %copy-start.10 = (bf16[528,128]{1,0:T(8,128)(2,1)}, bf16[528,128]{1,0:T(8,128)(2,1)S(1)}, u32[]{:S(2)}) copy-start(bf16[528,128]{1,0:T(8,128)(2,1)S(1)} %collective-permute-done.10.refs_11_) | copy-start | bytes 405508
  34.0 0.9 %copy-start.11 = (bf16[528,128]{1,0:T(8,128)(2,1)}, bf16[528,128]{1,0:T(8,128)(2,1)S(1)}, u32[]{:S(2)}) copy-start(bf16[528,128]{1,0:T(8,128)(2,1)S(1)} %collective-permute-done.11.refs_12_) | copy-start | bytes 405508
  34.2 0.7 copy-start.12
  34.5 0.7 copy-start.13
  35.2 0.6 copy-start.14
  56.7 9.8 %collective-permute-start.15 = (bf16[400,128]{1,0:T(8,128)(2,1)}, bf16[400,128]{1,0:T(8,128)(2,1)S(1)}, u32[]{:S(2)}, u32[]{:S(2)}) collective-permute-start(bf16[400,128]{1,0:T(8,128)(2,1)} %get-tuple-element.29), channel_id=1, source_target_pairs={{0,2},{1,3},{2,0},{3,1},{4,6},{5,7},{6,4},{7,5},{8,10},{9,11},{10,... | collective-permute-start | bytes 307208 | tf_op jit(solution)/shard_map/ppermute | solution.py:228
  57.5 11.4 %collective-permute-start.16 = (bf16[400,128]{1,0:T(8,128)(2,1)}, bf16[400,128]{1,0:T(8,128)(2,1)S(1)}, u32[]{:S(2)}, u32[]{:S(2)}) collective-permute-start(bf16[400,128]{1,0:T(8,128)(2,1)} %get-tuple-element.30), channel_id=1, source_target_pairs={{0,4},{1,5},{2,6},{3,7},{4,0},{5,1},{6,2},{7,3},{8,12},{9,13},{10,... | collective-permute-start | bytes 307208 | tf_op jit(solution)/shard_map/ppermute | solution.py:228
  61.7 9.7 %collective-permute-start.17 = (bf16[400,128]{1,0:T(8,128)(2,1)}, bf16[400,128]{1,0:T(8,128)(2,1)S(1)}, u32[]{:S(2)}, u32[]{:S(2)}) collective-permute-start(bf16[400,128]{1,0:T(8,128)(2,1)} %get-tuple-element.31), channel_id=1, source_target_pairs={{0,6},{1,7},{2,4},{3,5},{4,2},{5,3},{6,0},{7,1},{8,14},{9,15},{10,... | collective-permute-start | bytes 307208 | tf_op jit(solution)/shard_map/ppermute | solution.py:228
  62.8 8.6 %collective-permute-start.18 = (bf16[400,128]{1,0:T(8,128)(2,1)}, bf16[400,128]{1,0:T(8,128)(2,1)S(1)}, u32[]{:S(2)}, u32[]{:S(2)}) collective-permute-start(bf16[400,128]{1,0:T(8,128)(2,1)} %get-tuple-element.32), channel_id=1, source_target_pairs={{0,8},{1,9},{2,10},{3,11},{4,12},{5,13},{6,14},{7,15},{8,0},{9,1},... | collective-permute-start | bytes 307208 | tf_op jit(solution)/shard_map/ppermute | solution.py:228
  66.5 15.5 %collective-permute-start.19 = (bf16[400,128]{1,0:T(8,128)(2,1)}, bf16[400,128]{1,0:T(8,128)(2,1)S(1)}, u32[]{:S(2)}, u32[]{:S(2)}) collective-permute-start(bf16[400,128]{1,0:T(8,128)(2,1)} %get-tuple-element.33), channel_id=1, source_target_pairs={{0,10},{1,11},{2,8},{3,9},{4,14},{5,15},{6,12},{7,13},{8,2},{9,3},... | collective-permute-start | bytes 307208 | tf_op jit(solution)/shard_map/ppermute | solution.py:228
  66.5 15.6 %copy-start.15 = (bf16[400,128]{1,0:T(8,128)(2,1)}, bf16[400,128]{1,0:T(8,128)(2,1)S(1)}, u32[]{:S(2)}) copy-start(bf16[400,128]{1,0:T(8,128)(2,1)S(1)} %collective-permute-done.15.refs_1_) | copy-start | bytes 307204
  66.5 15.5 %collective-permute-start.20 = (bf16[400,128]{1,0:T(8,128)(2,1)}, bf16[400,128]{1,0:T(8,128)(2,1)S(1)}, u32[]{:S(2)}, u32[]{:S(2)}) collective-permute-start(bf16[400,128]{1,0:T(8,128)(2,1)} %get-tuple-element.34), channel_id=1, source_target_pairs={{0,12},{1,13},{2,14},{3,15},{4,8},{5,9},{6,10},{7,11},{8,4},{9,5},... | collective-permute-start | bytes 307208 | tf_op jit(solution)/shard_map/ppermute | solution.py:228
  68.8 13.2 %copy-start.16 = (bf16[400,128]{1,0:T(8,128)(2,1)}, bf16[400,128]{1,0:T(8,128)(2,1)S(1)}, u32[]{:S(2)}) copy-start(bf16[400,128]{1,0:T(8,128)(2,1)S(1)} %collective-permute-done.16.refs_2_) | copy-start | bytes 307204
  68.9 13.2 %collective-permute-start.21 = (bf16[400,128]{1,0:T(8,128)(2,1)}, bf16[400,128]{1,0:T(8,128)(2,1)S(1)}, u32[]{:S(2)}, u32[]{:S(2)}) collective-permute-start(bf16[400,128]{1,0:T(8,128)(2,1)} %get-tuple-element.35), channel_id=1, source_target_pairs={{0,14},{1,15},{2,12},{3,13},{4,10},{5,11},{6,8},{7,9},{8,6},{9,7},... | collective-permute-start | bytes 307208 | tf_op jit(solution)/shard_map/ppermute | solution.py:228
  71.4 10.7 %copy-start.17 = (bf16[400,128]{1,0:T(8,128)(2,1)}, bf16[400,128]{1,0:T(8,128)(2,1)S(1)}, u32[]{:S(2)}) copy-start(bf16[400,128]{1,0:T(8,128)(2,1)S(1)} %collective-permute-done.17.refs_3_) | copy-start | bytes 307204
  71.4 10.7 %copy-start.18 = (bf16[400,128]{1,0:T(8,128)(2,1)}, bf16[400,128]{1,0:T(8,128)(2,1)S(1)}, u32[]{:S(2)}) copy-start(bf16[400,128]{1,0:T(8,128)(2,1)S(1)} %collective-permute-done.18.refs_4_) | copy-start | bytes 307204
  82.0 0.6 copy-start.19
  82.0 0.7 copy-start.20
  82.0 0.7 copy-start.21

commit v2 on v1

v2 whole, which is shorter than its diff:
```python
import functools

import jax
import jax.numpy as jnp
from jax import lax
from jax.experimental import pallas as pl
from jax.experimental.pallas import tpu as pltpu
from jax.sharding import PartitionSpec as P

SPAN = 128
META = 16
F32 = jnp.float32
BF16 = jnp.bfloat16
I32 = jnp.int32
VMEM = pl.BlockSpec(memory_space=pltpu.VMEM)
SMEM = pl.BlockSpec(memory_space=pltpu.SMEM)


def dot(a, b, dims):
    return lax.dot_general(a, b, ((dims[:1], dims[1:]), ((), ())), preferred_element_type=F32)


NN = (1, 0)
NT = (1, 1)
TN = (0, 0)


def iota(shape, dim):
    return lax.broadcasted_iota(I32, shape, dim)


def order(pos):
    rows = pos.shape[1]
    across = jnp.broadcast_to(pos.astype(F32), (rows, rows))
    down = jnp.transpose(across)
    as_row = jnp.sum((down < across).astype(F32), axis=0, keepdims=True)
    as_col = jnp.sum((across < down).astype(F32), axis=1, keepdims=True)
    return as_row.astype(I32), as_col.astype(I32)


def pack_kernel(chip_ref, q_ref, k_ref, v_ref, g_ref, ld_ref, pos_ref, *outs):
    rows = q_ref.shape[0]
    heads = len(outs)
    chip = chip_ref[0]
    pos = pos_ref[...]
    rank, _ = order(pos)
    sort = (rank == iota((rows, rows), 0)).astype(BF16)
    for s in range(heads):
        head = chip ^ ((heads - s) % heads)
        at = pl.ds(pl.multiple_of(head * SPAN, SPAN), SPAN)
        together = jnp.concatenate([ref[:, at] for ref in (q_ref, k_ref, v_ref, g_ref)], axis=1)
        together = dot(sort, together, NN).astype(BF16)
        for a in range(4):
            outs[s][a * rows:(a + 1) * rows, :] = together[:, a * SPAN:(a + 1) * SPAN]
    line = iota((META, rows), 0)
    where = jnp.where(line == 1, (pos // SPAN).astype(F32), jnp.where(line == 2, (pos % SPAN + 1).astype(F32), 0.0))
    where = dot(where.astype(BF16), sort, NT)
    decay = dot(ld_ref[...], sort, NT)
    for s in range(heads):
        head = chip ^ ((heads - s) % heads)
        mine = jnp.sum(jnp.where(iota((heads, rows), 0) == head, decay, 0.0), axis=0, keepdims=True)
        outs[s][4 * rows:, :] = jnp.where(line == 0, mine, where).astype(BF16)


def segments(position, starts):
    total = jnp.zeros_like(position)
    for start in starts:
        total = total + (position >= start).astype(I32)
    return total


def chain_kernel(heads, lengths_ref, *refs):
    sources = len(refs) - heads - 14
    blocks, outs, scratch = refs[:sources], refs[sources:sources + heads], refs[sources + heads:]
    (hi_ref, lo_ref, win_ref, at_ref, sem, key_ref, cum_ref, chain_ref, gained_ref, weighted_ref,
     carried_ref, pulled_ref, low_ref, tail_ref) = scratch
    rows = (blocks[0].shape[0] - META) // 4
    frames = rows * sources
    spans = frames // SPAN
    window = 16 * pl.cdiv(2 * rows // sources, 16) + 16
    tall = cum_ref.shape[0]
    starts = []
    total = jnp.int32(0)
    for t in range(lengths_ref.shape[0]):
        starts.append(total)
        total = total + lengths_ref[t]

    for n, ref in enumerate(blocks):
        meta = ref[4 * rows:, :].astype(F32)
        hi_ref[n:n + 1, :] = meta[1:2]
        lo_ref[n:n + 1, :] = meta[2:3]
    hi = hi_ref[...]
    lane = iota((sources, SPAN), 1)
    count = jnp.zeros((sources, SPAN), F32)
    for b in range(1, spans):
        ahead = jnp.sum((hi < b).astype(F32), axis=1, keepdims=True)
        count = jnp.where(lane == b, ahead, count)
    win_ref[...] = jnp.minimum((count.astype(I32) // 16) * 16, rows - window)
    copy = pltpu.make_async_copy(win_ref, at_ref, sem)
    copy.start()

    spread = []
    hots = []
    for n, ref in enumerate(blocks):
        meta = ref[4 * rows:, :].astype(F32)
        spread.append(jnp.where(meta[1:2] == iota((tall, rows), 0).astype(F32), meta[0:1], 0.0).astype(BF16))
        hots.append((meta[2:3] == (iota((SPAN, rows), 0) + 1).astype(F32)).astype(BF16))
    in_chain = dot(jnp.concatenate(spread, axis=1), jnp.concatenate(hots, axis=1), NT).astype(BF16)
    upper = (iota((SPAN, SPAN), 0) <= iota((SPAN, SPAN), 1)).astype(BF16)
    place = iota((tall, SPAN), 0) * SPAN + iota((tall, SPAN), 1)
    marks = segments(place, starts) - segments(iota((tall, SPAN), 0) * SPAN - 1, starts)
    cum_ref[...] = dot(in_chain, upper, NN) - 128.0 * marks.astype(F32)
    tail_ref[...] = jnp.zeros_like(tail_ref)
    for ref in outs:
        ref[...] = jnp.zeros_like(ref)

    row_i = iota((SPAN, SPAN), 0)
    col_j = iota((SPAN, SPAN), 1)
    per = SPAN // window
    copy.wait()

    def first(b):
        base = b * SPAN
        at = pl.ds(pl.multiple_of(base, SPAN), SPAN)
        keys = jnp.where(hi_ref[...] == b.astype(F32), lo_ref[...], 0.0)
        chain = jnp.zeros((SPAN, 4 * SPAN), F32)
        for n0 in range(0, sources, 2 * per):
            parts, found = [], []
            for n1 in range(n0, n0 + 2 * per, per):
                row = None
                for n in range(n1, n1 + per):
                    begin = pl.multiple_of(at_ref[n, b], 16)
                    turned = pltpu.roll(keys[n:n + 1], (n - n1) * window + SPAN - begin, 1)
                    row = turned if row is None else row + turned
                    found.append(jnp.concatenate(
                        [blocks[n][pl.ds(a * rows + begin, window), :] for a in range(4)], axis=1))
                parts.append(row)
            row = jnp.concatenate(parts, axis=1)
            key_ref[pl.ds(b, 1), n0 * window:(n0 + 2 * per) * window] = row
            hot = (row == (iota((SPAN, 2 * per * window), 0) + 1).astype(F32)).astype(BF16)
            chain = chain + dot(hot, jnp.concatenate(found, axis=0), NN)
        chain = chain.astype(BF16)
        chain_ref[at, :] = chain
        q, k, v, g = (chain[:, a * SPAN:(a + 1) * SPAN] for a in range(4))
        cum_j = cum_ref[pl.ds(b, 1), :]
        cum_i = jnp.transpose(jnp.broadcast_to(cum_j, (SPAN, SPAN)))
        last = cum_j[:, SPAN - 1:]
        gap = cum_i - cum_j
        weight = jnp.where(row_i >= col_j, jnp.exp(jnp.minimum(gap, 0.0)), 0.0)
        weight_t = jnp.where(row_i <= col_j, jnp.exp(jnp.minimum(-gap, 0.0)), 0.0)
        query_gain = jnp.exp(cum_i)
        key_gain = jnp.exp(last - cum_i)
        key_end = (k.astype(F32) * key_gain).astype(BF16)
        query_start = (q.astype(F32) * query_gain).astype(BF16)
        gained_ref[at, 0:SPAN] = (g.astype(F32) * query_gain).astype(BF16)
        gained_ref[at, SPAN:2 * SPAN] = (v.astype(F32) * key_gain).astype(BF16)
        gained_ref[at, 2 * SPAN:] = key_end
        carried_ref[at, :] = dot(key_end, v, TN)
        pulled_ref[at, :] = dot(query_start, g, TN)
        weighted_ref[at, 0:SPAN] = (dot(g, v, NT) * weight).astype(BF16)
        weighted_ref[at, SPAN:2 * SPAN] = (dot(v, g, NT) * weight_t).astype(BF16)
        weighted_ref[at, 2 * SPAN:] = (dot(k, q, NT) * weight_t).astype(BF16)

    def second(b):
        base = b * SPAN
        at = pl.ds(pl.multiple_of(base, SPAN), SPAN)
        q, k, v, g = (chain_ref[at, a * SPAN:(a + 1) * SPAN] for a in range(4))
        state = low_ref[at, 0:SPAN]
        grad = low_ref[at, SPAN:]
        dq = dot(weighted_ref[at, 0:SPAN], k, NN) + dot(gained_ref[at, 0:SPAN], state, NT)
        dk = dot(weighted_ref[at, SPAN:2 * SPAN], q, NN) + dot(gained_ref[at, SPAN:2 * SPAN], grad, NT)
        dv = dot(weighted_ref[at, 2 * SPAN:], g, NN) + dot(gained_ref[at, 2 * SPAN:], grad, NN)
        term = jnp.sum(q.astype(F32) * dq - k.astype(F32) * dk, axis=1, keepdims=True)
        seg_i = segments(base + row_i, starts)
        seg_j = segments(base + iota((1, SPAN), 1), starts)
        lower = (seg_i == seg_j) & (row_i >= col_j)
        tail_ref[pl.ds(b, 1), :] = jnp.sum(jnp.where(lower, term, 0.0), axis=0, keepdims=True)
        key = key_ref[pl.ds(b, 1), 0:heads * window]
        hot = (key == (iota((SPAN, heads * window), 0) + 1).astype(F32)).astype(BF16)
        three = jnp.concatenate([dq.astype(BF16), dk.astype(BF16), dv.astype(BF16)], axis=1)
        back = dot(hot, three, TN).astype(BF16)
        for s in range(heads):
            begin = pl.multiple_of(at_ref[s, b], 16)
            for a in range(3):
                to = pl.ds(a * rows + begin, window)
                outs[s][to, :] += back[s * window:(s + 1) * window, a * SPAN:(a + 1) * SPAN]

    step = max(1, 64 // sources)

    @pl.loop(0, spans // step)
    def _(turn):
        for u in range(step):
            first(turn * step + u)

    def scan(turn, held):
        state, grad = held
        b, c = turn, spans - 1 - turn
        at_b = pl.ds(pl.multiple_of(b * SPAN, SPAN), SPAN)
        at_c = pl.ds(pl.multiple_of(c * SPAN, SPAN), SPAN)
        low_ref[at_b, 0:SPAN] = state.astype(BF16)
        low_ref[at_c, SPAN:] = grad.astype(BF16)
        fade_b = jnp.exp(cum_ref[pl.ds(b, 1), SPAN - 1:])
        fade_c = jnp.exp(cum_ref[pl.ds(c, 1), SPAN - 1:])
        return fade_b * state + carried_ref[at_b, :], fade_c * grad + pulled_ref[at_c, :]

    empty = jnp.zeros((SPAN, SPAN), F32)

    def scans(turn, held):
        for u in range(4):
            held = scan(turn * 4 + u, held)
        return held

    lax.fori_loop(0, spans // 4, scans, (empty, empty))

    @pl.loop(0, spans // step)
    def _(turn):
        for u in range(step):
            second(turn * step + u)

    firsts = jnp.transpose(tail_ref[...])[0:1, :]
    local = tail_ref[0:tall, :]
    seg_last = segments(iota((tall, SPAN), 0) * SPAN + SPAN - 1, starts)
    seg_first = segments(iota((tall, SPAN), 1) * SPAN, starts)
    later = (iota((tall, SPAN), 1) > iota((tall, SPAN), 0)) & (seg_first == seg_last)
    carry = jnp.sum(jnp.where(later, firsts, 0.0), axis=1, keepdims=True)
    full = local + jnp.where(segments(place, starts) == seg_last, carry, 0.0)
    begins = place == starts[0]
    for start in starts[1:]:
        begins = begins | (place == start)
    tails = jnp.where(begins, 0.0, full).astype(BF16)
    for s in range(heads):
        hot = (lo_ref[s:s + 1, :] == (iota((SPAN, rows), 0) + 1).astype(F32)).astype(BF16)
        found = dot(tails, hot, NN)
        mine = hi_ref[s:s + 1, :] == iota((tall, rows), 0).astype(F32)
        found = jnp.sum(jnp.where(mine, found, 0.0), axis=0, keepdims=True)
        outs[s][3 * rows:, :] = jnp.broadcast_to(found, (META, rows)).astype(BF16)


def unpack_kernel(chip_ref, pos_ref, *refs):
    heads = len(refs) - 4
    blocks, outs = refs[:heads], refs[heads:]
    rows = outs[0].shape[0]
    chip = chip_ref[0]
    _, rank = order(pos_ref[...])
    loose = (rank == iota((rows, rows), 1)).astype(BF16)
    line = iota((META, rows), 0)
    tails = jnp.zeros((META, rows), F32)
    for s in range(heads):
        head = chip ^ ((heads - s) % heads)
        at = pl.ds(pl.multiple_of(head * SPAN, SPAN), SPAN)
        together = jnp.concatenate([blocks[s][a * rows:(a + 1) * rows, :] for a in range(3)], axis=1)
        together = dot(loose, together, NN).astype(BF16)
        for a in range(3):
            outs[a][:, at] = together[:, a * SPAN:(a + 1) * SPAN]
        tails = jnp.where(line == head, blocks[s][3 * rows:, :].astype(F32), tails)
    outs[3][...] = dot(tails.astype(BF16), loose, NT)[:heads].astype(BF16)


def body(queries, keys, values, out_grad, log_decay, frame_pos, trial_lengths):
    rows, width = queries.shape
    heads = log_decay.shape[1]
    peers = lax.axis_size("ctx")
    cores = peers // heads
    frames = rows * peers
    spans = frames // SPAN
    chip = (lax.axis_index("ctx") // cores).astype(I32).reshape(1)

    def across(x, s):
        return lax.ppermute(x, "ctx", [(p, p ^ (s * cores)) for p in range(peers)])

    def beside(x, t):
        return lax.ppermute(x, "ctx", [(p, p ^ t) for p in range(peers)])

    packets = pl.pallas_call(
        pack_kernel,
        out_shape=[jax.ShapeDtypeStruct((4 * rows + META, SPAN), BF16)] * heads,
        in_specs=[SMEM] + [VMEM] * 6,
        out_specs=[VMEM] * heads,
        name="pack",
    )(chip, queries, keys, values, out_grad, log_decay.T, frame_pos.reshape(1, rows))
    got = [packets[0]] + [across(packets[s], heads - s) for s in range(1, heads)]
    everything = list(got)
    for t in range(1, cores):
        everything += [beside(x, t) for x in got]

    tall = max(META, spans)
    back = pl.pallas_call(
        functools.partial(chain_kernel, heads),
        out_shape=[jax.ShapeDtypeStruct((3 * rows + META, SPAN), BF16)] * heads,
        in_specs=[SMEM] + [VMEM] * peers,
        out_specs=[VMEM] * heads,
        scratch_shapes=[
            pltpu.VMEM((peers, SPAN), F32),
            pltpu.VMEM((peers, SPAN), F32),
            pltpu.VMEM((peers, SPAN), I32),
            pltpu.SMEM((peers, SPAN), I32),
            pltpu.SemaphoreType.DMA,
            pltpu.VMEM((spans, peers * (16 * pl.cdiv(2 * rows // peers, 16) + 16)), F32),
            pltpu.VMEM((tall, SPAN), F32),
            pltpu.VMEM((frames, 4 * SPAN), BF16),
            pltpu.VMEM((frames, 3 * SPAN), BF16),
            pltpu.VMEM((frames, 3 * SPAN), BF16),
            pltpu.VMEM((frames, SPAN), F32),
            pltpu.VMEM((frames, SPAN), F32),
            pltpu.VMEM((frames, 2 * SPAN), BF16),
            pltpu.VMEM((SPAN, SPAN), F32),
        ],
        compiler_params=pltpu.CompilerParams(vmem_limit_bytes=60 * 2**20),
        name="chain",
    )(trial_lengths, *everything)
    returned = [back[0]] + [across(back[s], heads - s) for s in range(1, heads)]

    *grads, tails = pl.pallas_call(
        unpack_kernel,
        out_shape=[jax.ShapeDtypeStruct((rows, width), BF16)] * 3 + [jax.ShapeDtypeStruct((heads, rows), BF16)],
        in_specs=[SMEM] + [VMEM] * (1 + heads),
        out_specs=[VMEM] * 4,
        name="unpack",
    )(chip, frame_pos.reshape(1, rows), *returned)
    return (*grads, tails.T)


def solution(mesh):
    rows = P(("groups", "ctx"), None)
    return jax.shard_map(
        body,
        mesh=mesh,
        in_specs=(rows, rows, rows, rows, rows, P(("groups", "ctx")), P("groups")),
        out_specs=(rows, rows, rows, rows),
        check_vma=False,
    )
```

time: 87.6 us -> 75.9 us (0.87)
  waiting for transfers between devices: 26 us -> 17.1 us
  starting transfers between devices: 29.6 us -> 35.7 us
  Pallas kernels: 25.6 us -> 20.4 us
  local copies, waits for them, and re-layouts: 4.41 us -> 1.63 us
    ppermute x14, waiting for transfers between devices: 24.6 us -> 15.8 us  [across(): return lax.ppermute(x, 'ctx', [(p, p ^ s * cores) for p in range(peers)])]
    ppermute x14, starting transfers between devices: 27.8 us -> 34.1 us  [across(): return lax.ppermute(x, 'ctx', [(p, p ^ s * cores) for p in range(peers)])]
    pallas_call x1, Pallas kernels: 20.9 us -> 15 us  [body(): pl.pallas_call(functools.partial(chain_kernel, heads), out_shape=[jax.Sha...]
    pallas_call x1 -> x0, local copies, waits for them, and re-layouts: 1.41 us -> none  [body(): pl.pallas_call(unpack_kernel, out_shape=[jax.ShapeDtypeStruct((rows, widt...]
    unnamed x47 -> x44, local copies, waits for them, and re-layouts: 3.01 us -> 1.63 us
  transfers between devices with their start and end apart: 22 -> 22, of which waited for: 8 -> 12; matrix products, arithmetic and copies ran while one was open for 0% -> 0% of each run, Pallas kernels for 0% -> 0%
where the time goes in v2:
time: 75.9 us; the launch traced here: 75.7 us
  starting transfers between devices  35.7 us (47%)
  Pallas kernels  20.4 us (27%)
  waiting for transfers between devices  17.1 us (23%)
  local copies, waits for them, and re-layouts  1.63 us (2%)
  between operations  0.84 us (1%)
    ppermute x14, starting transfers between devices, across(): return lax.ppermute(x, 'ctx', [(p, p ^ s * cores) for p in range(peers)])  34.1 us
    ppermute x14, waiting for transfers between devices, across(): return lax.ppermute(x, 'ctx', [(p, p ^ s * cores) for p in range(peers)])  15.8 us
    pallas_call x1, Pallas kernels, body(): pl.pallas_call(functools.partial(chain_kernel, heads), out_shape=[jax.Sha...  15 us
    pallas_call x1, Pallas kernels, body(): pl.pallas_call(pack_kernel, out_shape=[jax.ShapeDtypeStruct((4 * rows + M...  2.72 us
    pallas_call x1, Pallas kernels, body(): pl.pallas_call(unpack_kernel, out_shape=[jax.ShapeDtypeStruct((rows, widt...  2.67 us
    unnamed x44, local copies, waits for them, and re-layouts  1.63 us
    ppermute x8, starting transfers between devices, beside(): return lax.ppermute(x, 'ctx', [(p, p ^ t) for p in range(peers)])  1.6 us
  transfers between devices with their start and end apart: 22, of which 12 were waited for; matrix products, arithmetic and copies ran while one was open for 0% of the time, Pallas kernels for 0%

profile of v2, /device:TPU:0, one launch (start us, length us, event | category | flops | bytes accessed | tf_op | source)
XLA Modules:
  0.0 75.7 jit_solution(18333203712630868022)
XLA Ops:
  0.6 2.7 %pack.1 = (bf16[528,128]{1,0:T(8,128)(2,1)}, bf16[528,128]{1,0:T(8,128)(2,1)}, bf16[528,128]{1,0:T(8,128)(2,1)}, bf16[528,128]{1,0:T(8,128)(2,1)}, bf16[528,128]...) custom-call(s32[1]{0:T(128)} %bitcast.chip_ref, ...), custom_call_target="tpu_custom_call" | custom-call | tf_op jit(solution)/shard_map/pack/pallas_call | solution.py:274
  3.4 6.0 %collective-permute-start = (bf16[528,128]{1,0:T(8,128)(2,1)}, bf16[528,128]{1,0:T(8,128)(2,1)S(1)}, u32[]{:S(2)}, u32[]{:S(2)}) collective-permute-start(bf16[528,128]{1,0:T(8,128)(2,1)} %get-tuple-element.25), channel_id=1, source_target_pairs={{0,14},{1,15},{2,12},{3,13},{4,10},{5,11},{6,8},{7,9},{8,6},{9,7},... | collective-permute-start | bytes 405512 | tf_op jit(solution)/shard_map/ppermute | solution.py:269
  9.4 0.2 collective-permute-start.1
  9.6 0.7 collective-permute-start.2
  10.3 2.0 %collective-permute-start.3 = (bf16[528,128]{1,0:T(8,128)(2,1)}, bf16[528,128]{1,0:T(8,128)(2,1)S(1)}, u32[]{:S(2)}, u32[]{:S(2)}) collective-permute-start(bf16[528,128]{1,0:T(8,128)(2,1)} %get-tuple-element.28), channel_id=1, source_target_pairs={{0,8},{1,9},{2,10},{3,11},{4,12},{5,13},{6,14},{7,15},{8,0},{9,1},... | collective-permute-start | bytes 405512 | tf_op jit(solution)/shard_map/ppermute | solution.py:269
  12.3 2.3 %collective-permute-start.4 = (bf16[528,128]{1,0:T(8,128)(2,1)}, bf16[528,128]{1,0:T(8,128)(2,1)S(1)}, u32[]{:S(2)}, u32[]{:S(2)}) collective-permute-start(bf16[528,128]{1,0:T(8,128)(2,1)} %get-tuple-element.29), channel_id=1, source_target_pairs={{0,6},{1,7},{2,4},{3,5},{4,2},{5,3},{6,0},{7,1},{8,14},{9,15},{10,... | collective-permute-start | bytes 405512 | tf_op jit(solution)/shard_map/ppermute | solution.py:269
  14.7 0.0 collective-permute-done.refs_1_
  14.7 11.1 %collective-permute-start.5 = (bf16[528,128]{1,0:T(8,128)(2,1)}, bf16[528,128]{1,0:T(8,128)(2,1)S(1)}, u32[]{:S(2)}, u32[]{:S(2)}) collective-permute-start(bf16[528,128]{1,0:T(8,128)(2,1)} %get-tuple-element.30), channel_id=1, source_target_pairs={{0,4},{1,5},{2,6},{3,7},{4,0},{5,1},{6,2},{7,3},{8,12},{9,13},{10,... | collective-permute-start | bytes 405512 | tf_op jit(solution)/shard_map/ppermute | solution.py:269
  25.8 0.0 collective-permute-done.1.refs_2_
  25.8 1.4 %collective-permute-start.6 = (bf16[528,128]{1,0:T(8,128)(2,1)}, bf16[528,128]{1,0:T(8,128)(2,1)S(1)}, u32[]{:S(2)}, u32[]{:S(2)}) collective-permute-start(bf16[528,128]{1,0:T(8,128)(2,1)} %get-tuple-element.31), channel_id=1, source_target_pairs={{0,2},{1,3},{2,0},{3,1},{4,6},{5,7},{6,4},{7,5},{8,10},{9,11},{10,... | collective-permute-start | bytes 405512 | tf_op jit(solution)/shard_map/ppermute | solution.py:269
  27.2 3.6 %collective-permute-done.2.refs_3_ = bf16[528,128]{1,0:T(8,128)(2,1)S(1)} collective-permute-done((bf16[528,128]{1,0:T(8,128)(2,1)}, bf16[528,128]{1,0:T(8,128)(2,1)S(1)}, u32[]{:S(2)}, u32[]{:S(2)}) %collective-permute-start.2) | collective-permute-done | bytes 135200 | tf_op jit(solution)/shard_map/ppermute | solution.py:269
  30.8 0.0 collective-permute-start.7
  30.8 1.9 %collective-permute-done.3.refs_4_ = bf16[528,128]{1,0:T(8,128)(2,1)S(1)} collective-permute-done((bf16[528,128]{1,0:T(8,128)(2,1)}, bf16[528,128]{1,0:T(8,128)(2,1)S(1)}, u32[]{:S(2)}, u32[]{:S(2)}) %collective-permute-start.3) | collective-permute-done | bytes 135200 | tf_op jit(solution)/shard_map/ppermute | solution.py:269
  32.7 0.0 collective-permute-start.8
  32.7 0.0 collective-permute-done.4.refs_5_
  32.7 0.0 copy-start.4
  32.7 0.5 collective-permute-start.9
  33.2 0.7 collective-permute-done.5.refs_6_
  34.0 0.0 collective-permute-start.10
  34.0 0.0 collective-permute-done.6.refs_7_
  34.0 0.0 copy-start.6
  34.0 0.5 collective-permute-start.11
  34.5 0.0 collective-permute-done.7.refs_8_
  34.5 0.1 collective-permute-start.12
  34.6 0.0 collective-permute-done.8.refs_9_
  34.6 0.4 collective-permute-start.13
  35.0 0.0 collective-permute-done.9.refs_10_
  35.0 0.1 collective-permute-start.14
  35.1 0.2 collective-permute-done.10.refs_11_
  35.3 0.2 collective-permute-done.11.refs_12_
  35.5 0.3 collective-permute-done.12.refs_13_
  35.8 0.2 collective-permute-done.13.refs_14_
  36.0 0.3 collective-permute-done.14.refs_15_
  36.4 0.0 copy-done
  36.4 0.0 copy-done.1
  36.4 0.0 copy-done.2
  36.4 0.0 copy-done.3
  36.4 0.0 copy-done.4
  36.4 0.0 copy-done.5
  36.4 0.0 copy-done.6
  36.4 0.0 copy-done.7
  36.5 0.0 copy-done.12
  36.5 0.2 copy-done.13
  36.7 0.6 copy-done.14
  37.3 15.0 %chain.1 = (bf16[400,128]{1,0:T(8,128)(2,1)}, bf16[400,128]{1,0:T(8,128)(2,1)}, bf16[400,128]{1,0:T(8,128)(2,1)}, bf16[400,128]{1,0:T(8,128)(2,1)}, bf16[400,128...) custom-call(s32[8]{0:T(128)} %lengths_ref.1, ...), custom_call_target="tpu_custom_call" | custom-call | tf_op jit(solution)/shard_map/chain/pallas_call | solution.py:287
  52.4 2.5 %collective-permute-start.15 = (bf16[400,128]{1,0:T(8,128)(2,1)}, bf16[400,128]{1,0:T(8,128)(2,1)S(1)}, u32[]{:S(2)}, u32[]{:S(2)}) collective-permute-start(bf16[400,128]{1,0:T(8,128)(2,1)} %get-tuple-element.33), channel_id=1, source_target_pairs={{0,14},{1,15},{2,12},{3,13},{4,10},{5,11},{6,8},{7,9},{8,6},{9,7},... | collective-permute-start | bytes 307208 | tf_op jit(solution)/shard_map/ppermute | solution.py:269
  54.9 1.4 %collective-permute-start.16 = (bf16[400,128]{1,0:T(8,128)(2,1)}, bf16[400,128]{1,0:T(8,128)(2,1)S(1)}, u32[]{:S(2)}, u32[]{:S(2)}) collective-permute-start(bf16[400,128]{1,0:T(8,128)(2,1)} %get-tuple-element.34), channel_id=1, source_target_pairs={{0,12},{1,13},{2,14},{3,15},{4,8},{5,9},{6,10},{7,11},{8,4},{9,5},... | collective-permute-start | bytes 307208 | tf_op jit(solution)/shard_map/ppermute | solution.py:269
  56.3 0.0 collective-permute-start.17
  56.3 3.8 %collective-permute-start.18 = (bf16[400,128]{1,0:T(8,128)(2,1)}, bf16[400,128]{1,0:T(8,128)(2,1)S(1)}, u32[]{:S(2)}, u32[]{:S(2)}) collective-permute-start(bf16[400,128]{1,0:T(8,128)(2,1)} %get-tuple-element.36), channel_id=1, source_target_pairs={{0,8},{1,9},{2,10},{3,11},{4,12},{5,13},{6,14},{7,15},{8,0},{9,1},... | collective-permute-start | bytes 307208 | tf_op jit(solution)/shard_map/ppermute | solution.py:269
  60.1 0.1 collective-permute-start.19
  60.2 0.6 collective-permute-done.15.refs_1_
  60.8 1.3 %collective-permute-start.20 = (bf16[400,128]{1,0:T(8,128)(2,1)}, bf16[400,128]{1,0:T(8,128)(2,1)S(1)}, u32[]{:S(2)}, u32[]{:S(2)}) collective-permute-start(bf16[400,128]{1,0:T(8,128)(2,1)} %get-tuple-element.38), channel_id=1, source_target_pairs={{0,4},{1,5},{2,6},{3,7},{4,0},{5,1},{6,2},{7,3},{8,12},{9,13},{10,... | collective-permute-start | bytes 307208 | tf_op jit(solution)/shard_map/ppermute | solution.py:269
  62.1 0.6 collective-permute-done.16.refs_2_
  62.7 1.2 %collective-permute-start.21 = (bf16[400,128]{1,0:T(8,128)(2,1)}, bf16[400,128]{1,0:T(8,128)(2,1)S(1)}, u32[]{:S(2)}, u32[]{:S(2)}) collective-permute-start(bf16[400,128]{1,0:T(8,128)(2,1)} %get-tuple-element.39), channel_id=1, source_target_pairs={{0,2},{1,3},{2,0},{3,1},{4,6},{5,7},{6,4},{7,5},{8,10},{9,11},{10,... | collective-permute-start | bytes 307208 | tf_op jit(solution)/shard_map/ppermute | solution.py:269
  63.9 7.5 %collective-permute-done.17.refs_3_ = bf16[400,128]{1,0:T(8,128)(2,1)S(1)} collective-permute-done((bf16[400,128]{1,0:T(8,128)(2,1)}, bf16[400,128]{1,0:T(8,128)(2,1)S(1)}, u32[]{:S(2)}, u32[]{:S(2)}) %collective-permute-start.17) | collective-permute-done | bytes 102432 | tf_op jit(solution)/shard_map/ppermute | solution.py:269
  71.5 0.7 collective-permute-done.18.refs_4_
  72.2 0.0 collective-permute-done.19.refs_5_
  72.2 0.0 collective-permute-done.20.refs_6_
  72.2 0.0 collective-permute-done.21.refs_7_
  72.3 0.6 copy-done.18
  72.8 0.1 copy-done.19
  72.9 0.0 copy-done.20
  72.9 0.0 copy-done.21
  73.0 2.7 %unpack.1 = (bf16[128,1024]{1,0:T(8,128)(2,1)}, bf16[128,1024]{1,0:T(8,128)(2,1)}, bf16[128,1024]{1,0:T(8,128)(2,1)}, bf16[8,128]{1,0:T(8,128)(2,1)}) custom-call(s32[1]{0:T(128)} %bitcast.chip_ref, s32[1,128]{1,0:T(1,128)} %bitcast.5, bf16[400,128]{1,0:T(8,128)(2,1)} %get-tuple-element.32.refs_0_, bf16[400,128]{1,0:T(8,128)(2,1)} %copy-done.15, ...), custom_call_target="tpu_custom_call" | custom-call | tf_op jit(solution)/shard_map/unpack/pallas_call | solution.py:313
  (27 shorter events, 0.0 us)
Async XLA Ops:
  3.4 11.3 %collective-permute-start = (bf16[528,128]{1,0:T(8,128)(2,1)}, bf16[528,128]{1,0:T(8,128)(2,1)S(1)}, u32[]{:S(2)}, u32[]{:S(2)}) collective-permute-start(bf16[528,128]{1,0:T(8,128)(2,1)} %get-tuple-element.25), channel_id=1, source_target_pairs={{0,14},{1,15},{2,12},{3,13},{4,10},{5,11},{6,8},{7,9},{8,6},{9,7},... | collective-permute-start | bytes 405512 | tf_op jit(solution)/shard_map/ppermute | solution.py:269
  9.4 16.4 %collective-permute-start.1 = (bf16[528,128]{1,0:T(8,128)(2,1)}, bf16[528,128]{1,0:T(8,128)(2,1)S(1)}, u32[]{:S(2)}, u32[]{:S(2)}) collective-permute-start(bf16[528,128]{1,0:T(8,128)(2,1)} %get-tuple-element.26), channel_id=1, source_target_pairs={{0,12},{1,13},{2,14},{3,15},{4,8},{5,9},{6,10},{7,11},{8,4},{9,5},... | collective-permute-start | bytes 405512 | tf_op jit(solution)/shard_map/ppermute | solution.py:269
  9.6 21.2 %collective-permute-start.2 = (bf16[528,128]{1,0:T(8,128)(2,1)}, bf16[528,128]{1,0:T(8,128)(2,1)S(1)}, u32[]{:S(2)}, u32[]{:S(2)}) collective-permute-start(bf16[528,128]{1,0:T(8,128)(2,1)} %get-tuple-element.27), channel_id=1, source_target_pairs={{0,10},{1,11},{2,8},{3,9},{4,14},{5,15},{6,12},{7,13},{8,2},{9,3},... | collective-permute-start | bytes 405512 | tf_op jit(solution)/shard_map/ppermute | solution.py:269
  10.3 22.4 %collective-permute-start.3 = (bf16[528,128]{1,0:T(8,128)(2,1)}, bf16[528,128]{1,0:T(8,128)(2,1)S(1)}, u32[]{:S(2)}, u32[]{:S(2)}) collective-permute-start(bf16[528,128]{1,0:T(8,128)(2,1)} %get-tuple-element.28), channel_id=1, source_target_pairs={{0,8},{1,9},{2,10},{3,11},{4,12},{5,13},{6,14},{7,15},{8,0},{9,1},... | collective-permute-start | bytes 405512 | tf_op jit(solution)/shard_map/ppermute | solution.py:269
  12.3 20.4 %collective-permute-start.4 = (bf16[528,128]{1,0:T(8,128)(2,1)}, bf16[528,128]{1,0:T(8,128)(2,1)S(1)}, u32[]{:S(2)}, u32[]{:S(2)}) collective-permute-start(bf16[528,128]{1,0:T(8,128)(2,1)} %get-tuple-element.29), channel_id=1, source_target_pairs={{0,6},{1,7},{2,4},{3,5},{4,2},{5,3},{6,0},{7,1},{8,14},{9,15},{10,... | collective-permute-start | bytes 405512 | tf_op jit(solution)/shard_map/ppermute | solution.py:269
  14.7 21.7 %copy-start = (bf16[528,128]{1,0:T(8,128)(2,1)}, bf16[528,128]{1,0:T(8,128)(2,1)S(1)}, u32[]{:S(2)}) copy-start(bf16[528,128]{1,0:T(8,128)(2,1)S(1)} %collective-permute-done.refs_1_) | copy-start | bytes 405508
  14.7 19.3 %collective-permute-start.5 = (bf16[528,128]{1,0:T(8,128)(2,1)}, bf16[528,128]{1,0:T(8,128)(2,1)S(1)}, u32[]{:S(2)}, u32[]{:S(2)}) collective-permute-start(bf16[528,128]{1,0:T(8,128)(2,1)} %get-tuple-element.30), channel_id=1, source_target_pairs={{0,4},{1,5},{2,6},{3,7},{4,0},{5,1},{6,2},{7,3},{8,12},{9,13},{10,... | collective-permute-start | bytes 405512 | tf_op jit(solution)/shard_map/ppermute | solution.py:269
  25.8 10.6 %copy-start.1 = (bf16[528,128]{1,0:T(8,128)(2,1)}, bf16[528,128]{1,0:T(8,128)(2,1)S(1)}, u32[]{:S(2)}) copy-start(bf16[528,128]{1,0:T(8,128)(2,1)S(1)} %collective-permute-done.1.refs_2_) | copy-start | bytes 405508
  25.8 8.2 %collective-permute-start.6 = (bf16[528,128]{1,0:T(8,128)(2,1)}, bf16[528,128]{1,0:T(8,128)(2,1)S(1)}, u32[]{:S(2)}, u32[]{:S(2)}) collective-permute-start(bf16[528,128]{1,0:T(8,128)(2,1)} %get-tuple-element.31), channel_id=1, source_target_pairs={{0,2},{1,3},{2,0},{3,1},{4,6},{5,7},{6,4},{7,5},{8,10},{9,11},{10,... | collective-permute-start | bytes 405512 | tf_op jit(solution)/shard_map/ppermute | solution.py:269
  30.8 5.6 %copy-start.2 = (bf16[528,128]{1,0:T(8,128)(2,1)}, bf16[528,128]{1,0:T(8,128)(2,1)S(1)}, u32[]{:S(2)}) copy-start(bf16[528,128]{1,0:T(8,128)(2,1)S(1)} %collective-permute-done.2.refs_3_) | copy-start | bytes 405508
  30.8 3.7 %collective-permute-start.7 = (bf16[528,128]{1,0:T(8,128)(2,1)}, bf16[528,128]{1,0:T(8,128)(2,1)S(1)}, u32[]{:S(2)}, u32[]{:S(2)}) collective-permute-start(bf16[528,128]{1,0:T(8,128)(2,1)} %get-tuple-element.24.refs_0_), channel_id=1, source_target_pairs={{0,1},{1,0},{2,3},{3,2},{4,5},{5,4},{6,7},{7,6},{8,9},{9,8},{10,11... | collective-permute-start | bytes 405512 | tf_op jit(solution)/shard_map/ppermute | solution.py:272
  32.7 3.7 %copy-start.3 = (bf16[528,128]{1,0:T(8,128)(2,1)}, bf16[528,128]{1,0:T(8,128)(2,1)S(1)}, u32[]{:S(2)}) copy-start(bf16[528,128]{1,0:T(8,128)(2,1)S(1)} %collective-permute-done.3.refs_4_) | copy-start | bytes 405508
  32.7 1.9 %collective-permute-start.8 = (bf16[528,128]{1,0:T(8,128)(2,1)S(1)}, bf16[528,128]{1,0:T(8,128)(2,1)S(1)}, u32[]{:S(2)}, u32[]{:S(2)}) collective-permute-start(bf16[528,128]{1,0:T(8,128)(2,1)S(1)} %collective-permute-done.refs_1_), channel_id=1, source_target_pairs={{0,1},{1,0},{2,3},{3,2},{4,5},{5,4},{6,7},{7,6},{8,9},{9,8},{10,11... | collective-permute-start | bytes 405512 | tf_op jit(solution)/shard_map/ppermute | solution.py:272
  32.7 3.7 %copy-start.4 = (bf16[528,128]{1,0:T(8,128)(2,1)}, bf16[528,128]{1,0:T(8,128)(2,1)S(1)}, u32[]{:S(2)}) copy-start(bf16[528,128]{1,0:T(8,128)(2,1)S(1)} %collective-permute-done.4.refs_5_) | copy-start | bytes 405508
  32.7 2.3 %collective-permute-start.9 = (bf16[528,128]{1,0:T(8,128)(2,1)S(1)}, bf16[528,128]{1,0:T(8,128)(2,1)S(1)}, u32[]{:S(2)}, u32[]{:S(2)}) collective-permute-start(bf16[528,128]{1,0:T(8,128)(2,1)S(1)} %collective-permute-done.1.refs_2_), channel_id=1, source_target_pairs={{0,1},{1,0},{2,3},{3,2},{4,5},{5,4},{6,7},{7,6},{8,9},{9,8},{10,11... | collective-permute-start | bytes 405512 | tf_op jit(solution)/shard_map/ppermute | solution.py:272
  34.0 2.4 %copy-start.5 = (bf16[528,128]{1,0:T(8,128)(2,1)}, bf16[528,128]{1,0:T(8,128)(2,1)S(1)}, u32[]{:S(2)}) copy-start(bf16[528,128]{1,0:T(8,128)(2,1)S(1)} %collective-permute-done.5.refs_6_) | copy-start | bytes 405508
  34.0 1.4 %collective-permute-start.10 = (bf16[528,128]{1,0:T(8,128)(2,1)S(1)}, bf16[528,128]{1,0:T(8,128)(2,1)S(1)}, u32[]{:S(2)}, u32[]{:S(2)}) collective-permute-start(bf16[528,128]{1,0:T(8,128)(2,1)S(1)} %collective-permute-done.2.refs_3_), channel_id=1, source_target_pairs={{0,1},{1,0},{2,3},{3,2},{4,5},{5,4},{6,7},{7,6},{8,9},{9,8},{10,11... | collective-permute-start | bytes 405512 | tf_op jit(solution)/shard_map/ppermute | solution.py:272
  34.0 2.4 %copy-start.6 = (bf16[528,128]{1,0:T(8,128)(2,1)}, bf16[528,128]{1,0:T(8,128)(2,1)S(1)}, u32[]{:S(2)}) copy-start(bf16[528,128]{1,0:T(8,128)(2,1)S(1)} %collective-permute-done.6.refs_7_) | copy-start | bytes 405508
  34.0 1.5 %collective-permute-start.11 = (bf16[528,128]{1,0:T(8,128)(2,1)S(1)}, bf16[528,128]{1,0:T(8,128)(2,1)S(1)}, u32[]{:S(2)}, u32[]{:S(2)}) collective-permute-start(bf16[528,128]{1,0:T(8,128)(2,1)S(1)} %collective-permute-done.3.refs_4_), channel_id=1, source_target_pairs={{0,1},{1,0},{2,3},{3,2},{4,5},{5,4},{6,7},{7,6},{8,9},{9,8},{10,11... | collective-permute-start | bytes 405512 | tf_op jit(solution)/shard_map/ppermute | solution.py:272
  34.5 1.9 %copy-start.7 = (bf16[528,128]{1,0:T(8,128)(2,1)}, bf16[528,128]{1,0:T(8,128)(2,1)S(1)}, u32[]{:S(2)}) copy-start(bf16[528,128]{1,0:T(8,128)(2,1)S(1)} %collective-permute-done.7.refs_8_) | copy-start | bytes 405508
  34.5 1.4 %collective-permute-start.12 = (bf16[528,128]{1,0:T(8,128)(2,1)S(1)}, bf16[528,128]{1,0:T(8,128)(2,1)S(1)}, u32[]{:S(2)}, u32[]{:S(2)}) collective-permute-start(bf16[528,128]{1,0:T(8,128)(2,1)S(1)} %collective-permute-done.4.refs_5_), channel_id=1, source_target_pairs={{0,1},{1,0},{2,3},{3,2},{4,5},{5,4},{6,7},{7,6},{8,9},{9,8},{10,11... | collective-permute-start | bytes 405512 | tf_op jit(solution)/shard_map/ppermute | solution.py:272
  34.6 1.9 %copy-start.8 = (bf16[528,128]{1,0:T(8,128)(2,1)}, bf16[528,128]{1,0:T(8,128)(2,1)S(1)}, u32[]{:S(2)}) copy-start(bf16[528,128]{1,0:T(8,128)(2,1)S(1)} %collective-permute-done.8.refs_9_) | copy-start | bytes 405508
  34.6 1.5 %collective-permute-start.13 = (bf16[528,128]{1,0:T(8,128)(2,1)S(1)}, bf16[528,128]{1,0:T(8,128)(2,1)S(1)}, u32[]{:S(2)}, u32[]{:S(2)}) collective-permute-start(bf16[528,128]{1,0:T(8,128)(2,1)S(1)} %collective-permute-done.5.refs_6_), channel_id=1, source_target_pairs={{0,1},{1,0},{2,3},{3,2},{4,5},{5,4},{6,7},{7,6},{8,9},{9,8},{10,11... | collective-permute-start | bytes 405512 | tf_op jit(solution)/shard_map/ppermute | solution.py:272
  35.0 1.4 %copy-start.9 = (bf16[528,128]{1,0:T(8,128)(2,1)}, bf16[528,128]{1,0:T(8,128)(2,1)S(1)}, u32[]{:S(2)}) copy-start(bf16[528,128]{1,0:T(8,128)(2,1)S(1)} %collective-permute-done.9.refs_10_) | copy-start | bytes 405508
  35.0 1.4 %collective-permute-start.14 = (bf16[528,128]{1,0:T(8,128)(2,1)S(1)}, bf16[528,128]{1,0:T(8,128)(2,1)S(1)}, u32[]{:S(2)}, u32[]{:S(2)}) collective-permute-start(bf16[528,128]{1,0:T(8,128)(2,1)S(1)} %collective-permute-done.6.refs_7_), channel_id=1, source_target_pairs={{0,1},{1,0},{2,3},{3,2},{4,5},{5,4},{6,7},{7,6},{8,9},{9,8},{10,11... | collective-permute-start | bytes 405512 | tf_op jit(solution)/shard_map/ppermute | solution.py:272
  35.3 1.1 %copy-start.10 = (bf16[528,128]{1,0:T(8,128)(2,1)}, bf16[528,128]{1,0:T(8,128)(2,1)S(1)}, u32[]{:S(2)}) copy-start(bf16[528,128]{1,0:T(8,128)(2,1)S(1)} %collective-permute-done.10.refs_11_) | copy-start | bytes 405508
  35.5 0.9 %copy-start.11 = (bf16[528,128]{1,0:T(8,128)(2,1)}, bf16[528,128]{1,0:T(8,128)(2,1)S(1)}, u32[]{:S(2)}) copy-start(bf16[528,128]{1,0:T(8,128)(2,1)S(1)} %collective-permute-done.11.refs_12_) | copy-start | bytes 405508
  35.8 0.7 copy-start.12
  36.0 0.7 copy-start.13
  36.7 0.7 copy-start.14
  52.4 8.5 %collective-permute-start.15 = (bf16[400,128]{1,0:T(8,128)(2,1)}, bf16[400,128]{1,0:T(8,128)(2,1)S(1)}, u32[]{:S(2)}, u32[]{:S(2)}) collective-permute-start(bf16[400,128]{1,0:T(8,128)(2,1)} %get-tuple-element.33), channel_id=1, source_target_pairs={{0,14},{1,15},{2,12},{3,13},{4,10},{5,11},{6,8},{7,9},{8,6},{9,7},... | collective-permute-start | bytes 307208 | tf_op jit(solution)/shard_map/ppermute | solution.py:269
  54.9 7.8 %collective-permute-start.16 = (bf16[400,128]{1,0:T(8,128)(2,1)}, bf16[400,128]{1,0:T(8,128)(2,1)S(1)}, u32[]{:S(2)}, u32[]{:S(2)}) collective-permute-start(bf16[400,128]{1,0:T(8,128)(2,1)} %get-tuple-element.34), channel_id=1, source_target_pairs={{0,12},{1,13},{2,14},{3,15},{4,8},{5,9},{6,10},{7,11},{8,4},{9,5},... | collective-permute-start | bytes 307208 | tf_op jit(solution)/shard_map/ppermute | solution.py:269
  56.3 15.2 %collective-permute-start.17 = (bf16[400,128]{1,0:T(8,128)(2,1)}, bf16[400,128]{1,0:T(8,128)(2,1)S(1)}, u32[]{:S(2)}, u32[]{:S(2)}) collective-permute-start(bf16[400,128]{1,0:T(8,128)(2,1)} %get-tuple-element.35), channel_id=1, source_target_pairs={{0,10},{1,11},{2,8},{3,9},{4,14},{5,15},{6,12},{7,13},{8,2},{9,3},... | collective-permute-start | bytes 307208 | tf_op jit(solution)/shard_map/ppermute | solution.py:269
  56.3 16.0 %collective-permute-start.18 = (bf16[400,128]{1,0:T(8,128)(2,1)}, bf16[400,128]{1,0:T(8,128)(2,1)S(1)}, u32[]{:S(2)}, u32[]{:S(2)}) collective-permute-start(bf16[400,128]{1,0:T(8,128)(2,1)} %get-tuple-element.36), channel_id=1, source_target_pairs={{0,8},{1,9},{2,10},{3,11},{4,12},{5,13},{6,14},{7,15},{8,0},{9,1},... | collective-permute-start | bytes 307208 | tf_op jit(solution)/shard_map/ppermute | solution.py:269
  60.1 12.2 %collective-permute-start.19 = (bf16[400,128]{1,0:T(8,128)(2,1)}, bf16[400,128]{1,0:T(8,128)(2,1)S(1)}, u32[]{:S(2)}, u32[]{:S(2)}) collective-permute-start(bf16[400,128]{1,0:T(8,128)(2,1)} %get-tuple-element.37), channel_id=1, source_target_pairs={{0,6},{1,7},{2,4},{3,5},{4,2},{5,3},{6,0},{7,1},{8,14},{9,15},{10,... | collective-permute-start | bytes 307208 | tf_op jit(solution)/shard_map/ppermute | solution.py:269
  60.8 11.4 %copy-start.15 = (bf16[400,128]{1,0:T(8,128)(2,1)}, bf16[400,128]{1,0:T(8,128)(2,1)S(1)}, u32[]{:S(2)}) copy-start(bf16[400,128]{1,0:T(8,128)(2,1)S(1)} %collective-permute-done.15.refs_1_) | copy-start | bytes 307204
  60.8 11.4 %collective-permute-start.20 = (bf16[400,128]{1,0:T(8,128)(2,1)}, bf16[400,128]{1,0:T(8,128)(2,1)S(1)}, u32[]{:S(2)}, u32[]{:S(2)}) collective-permute-start(bf16[400,128]{1,0:T(8,128)(2,1)} %get-tuple-element.38), channel_id=1, source_target_pairs={{0,4},{1,5},{2,6},{3,7},{4,0},{5,1},{6,2},{7,3},{8,12},{9,13},{10,... | collective-permute-start | bytes 307208 | tf_op jit(solution)/shard_map/ppermute | solution.py:269
  62.7 9.6 %copy-start.16 = (bf16[400,128]{1,0:T(8,128)(2,1)}, bf16[400,128]{1,0:T(8,128)(2,1)S(1)}, u32[]{:S(2)}) copy-start(bf16[400,128]{1,0:T(8,128)(2,1)S(1)} %collective-permute-done.16.refs_2_) | copy-start | bytes 307204
  62.7 9.5 %collective-permute-start.21 = (bf16[400,128]{1,0:T(8,128)(2,1)}, bf16[400,128]{1,0:T(8,128)(2,1)S(1)}, u32[]{:S(2)}, u32[]{:S(2)}) collective-permute-start(bf16[400,128]{1,0:T(8,128)(2,1)} %get-tuple-element.39), channel_id=1, source_target_pairs={{0,2},{1,3},{2,0},{3,1},{4,6},{5,7},{6,4},{7,5},{8,10},{9,11},{10,... | collective-permute-start | bytes 307208 | tf_op jit(solution)/shard_map/ppermute | solution.py:269
  71.5 0.8 %copy-start.17 = (bf16[400,128]{1,0:T(8,128)(2,1)}, bf16[400,128]{1,0:T(8,128)(2,1)S(1)}, u32[]{:S(2)}) copy-start(bf16[400,128]{1,0:T(8,128)(2,1)S(1)} %collective-permute-done.17.refs_3_) | copy-start | bytes 307204
  72.2 0.6 copy-start.18
  72.2 0.7 copy-start.19
  72.2 0.7 copy-start.20
  72.3 0.7 copy-start.21

commit v3 on v2

--- a/solution.py
+++ b/solution.py
@@ -38,28 +38,39 @@
     return as_row.astype(I32), as_col.astype(I32)
 
 
-def pack_kernel(chip_ref, q_ref, k_ref, v_ref, g_ref, ld_ref, pos_ref, *outs):
-    rows = q_ref.shape[0]
+def pack_kernel(chip_ref, *refs):
+    given, outs, held, built, sems, leaves = refs[:6], refs[6:-9], refs[-9:-3], refs[-3], refs[-2], refs[-1]
+    rows = given[0].shape[0]
     heads = len(outs)
+    copies = [pltpu.make_async_copy(given[n], held[n], sems.at[n]) for n in range(6)]
+    for n in (5, 4, 0, 1, 2, 3):
+        copies[n].start()
     chip = chip_ref[0]
-    pos = pos_ref[...]
+    copies[5].wait()
+    pos = held[5][...]
     rank, _ = order(pos)
     sort = (rank == iota((rows, rows), 0)).astype(BF16)
-    for s in range(heads):
-        head = chip ^ ((heads - s) % heads)
-        at = pl.ds(pl.multiple_of(head * SPAN, SPAN), SPAN)
-        together = jnp.concatenate([ref[:, at] for ref in (q_ref, k_ref, v_ref, g_ref)], axis=1)
-        together = dot(sort, together, NN).astype(BF16)
-        for a in range(4):
-            outs[s][a * rows:(a + 1) * rows, :] = together[:, a * SPAN:(a + 1) * SPAN]
     line = iota((META, rows), 0)
     where = jnp.where(line == 1, (pos // SPAN).astype(F32), jnp.where(line == 2, (pos % SPAN + 1).astype(F32), 0.0))
     where = dot(where.astype(BF16), sort, NT)
-    decay = dot(ld_ref[...], sort, NT)
+    copies[4].wait()
+    decay = dot(held[4][...], sort, NT)
     for s in range(heads):
         head = chip ^ ((heads - s) % heads)
         mine = jnp.sum(jnp.where(iota((heads, rows), 0) == head, decay, 0.0), axis=0, keepdims=True)
-        outs[s][4 * rows:, :] = jnp.where(line == 0, mine, where).astype(BF16)
+        built[s, 4 * rows:, :] = jnp.where(line == 0, mine, where).astype(BF16)
+    for a in range(4):
+        copies[a].wait()
+    for s in range(heads):
+        head = chip ^ ((heads - s) % heads)
+        at = pl.ds(pl.multiple_of(head * SPAN, SPAN), SPAN)
+        together = jnp.concatenate([held[a][:, at] for a in range(4)], axis=1)
+        together = dot(sort, together, NN).astype(BF16)
+        for a in range(4):
+            built[s, a * rows:(a + 1) * rows, :] = together[:, a * SPAN:(a + 1) * SPAN]
+        pltpu.make_async_copy(built.at[s], outs[s], leaves.at[s]).start()
+    for s in range(heads):
+        pltpu.make_async_copy(built.at[s], outs[s], leaves.at[s]).wait()
 
 
 def segments(position, starts):
@@ -72,7 +83,7 @@
 def chain_kernel(heads, lengths_ref, *refs):
     sources = len(refs) - heads - 14
     blocks, outs, scratch = refs[:sources], refs[sources:sources + heads], refs[sources + heads:]
-    (hi_ref, lo_ref, win_ref, at_ref, sem, key_ref, cum_ref, chain_ref, gained_ref, weighted_ref,
+    (hi_ref, lo_ref, win_ref, at_ref, sem, down_ref, cum_ref, chain_ref, gained_ref, weighted_ref,
      carried_ref, pulled_ref, low_ref, tail_ref) = scratch
     rows = (blocks[0].shape[0] - META) // 4
     frames = rows * sources
@@ -111,8 +122,10 @@
     marks = segments(place, starts) - segments(iota((tall, SPAN), 0) * SPAN - 1, starts)
     cum_ref[...] = dot(in_chain, upper, NN) - 128.0 * marks.astype(F32)
     tail_ref[...] = jnp.zeros_like(tail_ref)
-    for ref in outs:
+    for s, ref in enumerate(outs):
         ref[...] = jnp.zeros_like(ref)
+        where = hi_ref[s:s + 1, :] * SPAN + lo_ref[s:s + 1, :] - 1.0
+        down_ref[s * rows:(s + 1) * rows, :] = jnp.transpose(jnp.broadcast_to(where, (SPAN, rows)))
 
     row_i = iota((SPAN, SPAN), 0)
     col_j = iota((SPAN, SPAN), 1)
@@ -136,7 +149,6 @@
                         [blocks[n][pl.ds(a * rows + begin, window), :] for a in range(4)], axis=1))
                 parts.append(row)
             row = jnp.concatenate(parts, axis=1)
-            key_ref[pl.ds(b, 1), n0 * window:(n0 + 2 * per) * window] = row
             hot = (row == (iota((SPAN, 2 * per * window), 0) + 1).astype(F32)).astype(BF16)
             chain = chain + dot(hot, jnp.concatenate(found, axis=0), NN)
         chain = chain.astype(BF16)
@@ -175,17 +187,17 @@
         seg_j = segments(base + iota((1, SPAN), 1), starts)
         lower = (seg_i == seg_j) & (row_i >= col_j)
         tail_ref[pl.ds(b, 1), :] = jnp.sum(jnp.where(lower, term, 0.0), axis=0, keepdims=True)
-        key = key_ref[pl.ds(b, 1), 0:heads * window]
-        hot = (key == (iota((SPAN, heads * window), 0) + 1).astype(F32)).astype(BF16)
+        begins = [pl.multiple_of(at_ref[s, b], 16) for s in range(heads)]
+        there = jnp.concatenate([down_ref[pl.ds(s * rows + begins[s], window), :] for s in range(heads)], axis=0)
+        hot = (there == (base + iota((heads * window, SPAN), 1)).astype(F32)).astype(BF16)
         three = jnp.concatenate([dq.astype(BF16), dk.astype(BF16), dv.astype(BF16)], axis=1)
-        back = dot(hot, three, TN).astype(BF16)
+        back = dot(hot, three, NN).astype(BF16)
         for s in range(heads):
-            begin = pl.multiple_of(at_ref[s, b], 16)
             for a in range(3):
-                to = pl.ds(a * rows + begin, window)
+                to = pl.ds(a * rows + begins[s], window)
                 outs[s][to, :] += back[s * window:(s + 1) * window, a * SPAN:(a + 1) * SPAN]
 
-    step = max(1, 64 // sources)
+    step = max(1, 128 // sources)
 
     @pl.loop(0, spans // step)
     def _(turn):
@@ -274,8 +286,12 @@
     packets = pl.pallas_call(
         pack_kernel,
         out_shape=[jax.ShapeDtypeStruct((4 * rows + META, SPAN), BF16)] * heads,
-        in_specs=[SMEM] + [VMEM] * 6,
-        out_specs=[VMEM] * heads,
+        in_specs=[SMEM] + [pl.BlockSpec(memory_space=pltpu.HBM)] * 6,
+        out_specs=[pl.BlockSpec(memory_space=pltpu.HBM)] * heads,
+        scratch_shapes=[pltpu.VMEM((rows, width), BF16)] * 4
+        + [pltpu.VMEM((heads, rows), BF16), pltpu.VMEM((1, rows), I32), pltpu.VMEM((heads, 4 * rows + META, SPAN), BF16)]
+        + [pltpu.SemaphoreType.DMA((6,)), pltpu.SemaphoreType.DMA((heads,))],
+        compiler_params=pltpu.CompilerParams(vmem_limit_bytes=60 * 2**20),
         name="pack",
     )(chip, queries, keys, values, out_grad, log_decay.T, frame_pos.reshape(1, rows))
     got = [packets[0]] + [across(packets[s], heads - s) for s in range(1, heads)]
@@ -295,7 +311,7 @@
             pltpu.VMEM((peers, SPAN), I32),
             pltpu.SMEM((peers, SPAN), I32),
             pltpu.SemaphoreType.DMA,
-            pltpu.VMEM((spans, peers * (16 * pl.cdiv(2 * rows // peers, 16) + 16)), F32),
+            pltpu.VMEM((heads * rows, SPAN), F32),
             pltpu.VMEM((tall, SPAN), F32),
             pltpu.VMEM((frames, 4 * SPAN), BF16),
             pltpu.VMEM((frames, 3 * SPAN), BF16),
@@ -305,7 +321,7 @@
             pltpu.VMEM((frames, 2 * SPAN), BF16),
             pltpu.VMEM((SPAN, SPAN), F32),
         ],
-        compiler_params=pltpu.CompilerParams(vmem_limit_bytes=60 * 2**20),
+        compiler_params=pltpu.CompilerParams(vmem_limit_bytes=frames * 6 * 2**10 + 8 * 2**20),
         name="chain",
     )(trial_lengths, *everything)
     returned = [back[0]] + [across(back[s], heads - s) for s in range(1, heads)]
@@ -315,6 +331,7 @@
         out_shape=[jax.ShapeDtypeStruct((rows, width), BF16)] * 3 + [jax.ShapeDtypeStruct((heads, rows), BF16)],
         in_specs=[SMEM] + [VMEM] * (1 + heads),
         out_specs=[VMEM] * 4,
+        compiler_params=pltpu.CompilerParams(vmem_limit_bytes=12 * 2**20),
         name="unpack",
     )(chip, frame_pos.reshape(1, rows), *returned)
     return (*grads, tails.T)

time: 75.9 us -> 71.7 us (0.945)
  starting transfers between devices: 35.7 us -> 40 us
  Pallas kernels: 20.4 us -> 16.3 us
  waiting for transfers between devices: 17.1 us -> 13.7 us
    ppermute x14, starting transfers between devices: 34.1 us -> 38.4 us  [across(): return lax.ppermute(x, 'ctx', [(p, p ^ s * cores) for p in range(peers)])]
    ppermute x14, waiting for transfers between devices: 15.8 us -> 12.4 us  [across(): return lax.ppermute(x, 'ctx', [(p, p ^ s * cores) for p in range(peers)])]
    pallas_call x1, Pallas kernels: 15 us -> 12.3 us  [body(): pl.pallas_call(functools.partial(chain_kernel, heads), out_shape=[jax.Sha...]
    pallas_call x1, Pallas kernels: 2.67 us -> 1.42 us  [body(): pl.pallas_call(unpack_kernel, out_shape=[jax.ShapeDtypeStruct((rows, widt...]
    unnamed x44 -> x6, local copies, waits for them, and re-layouts: 1.63 us -> 0.91 us
where the time goes in v3:
time: 71.7 us; the launch traced here: 71.5 us
  starting transfers between devices  40 us (56%)
  Pallas kernels  16.3 us (23%)
  waiting for transfers between devices  13.7 us (19%)
  local copies, waits for them, and re-layouts  0.91 us (1%)
    ppermute x14, starting transfers between devices, across(): return lax.ppermute(x, 'ctx', [(p, p ^ s * cores) for p in range(peers)])  38.4 us
    ppermute x14, waiting for transfers between devices, across(): return lax.ppermute(x, 'ctx', [(p, p ^ s * cores) for p in range(peers)])  12.4 us
    pallas_call x1, Pallas kernels, body(): pl.pallas_call(functools.partial(chain_kernel, heads), out_shape=[jax.Sha...  12.3 us
    pallas_call x1, Pallas kernels, body(): pl.pallas_call(pack_kernel, out_shape=[jax.ShapeDtypeStruct((4 * rows + M...  2.52 us
    ppermute x8, starting transfers between devices, beside(): return lax.ppermute(x, 'ctx', [(p, p ^ t) for p in range(peers)])  1.6 us
  transfers between devices with their start and end apart: 22, of which 12 were waited for; matrix products, arithmetic and copies ran while one was open for 0% of the time, Pallas kernels for 0%

profile of v3, /device:TPU:0, one launch (start us, length us, event | category | flops | bytes accessed | tf_op | source)
XLA Modules:
  0.0 71.5 jit_solution(15822201601972961116)
XLA Ops:
  0.6 2.5 %pack.1 = (bf16[528,128]{1,0:T(8,128)(2,1)}, bf16[528,128]{1,0:T(8,128)(2,1)}, bf16[528,128]{1,0:T(8,128)(2,1)}, bf16[528,128]{1,0:T(8,128)(2,1)}, bf16[528,128]...) custom-call(s32[1]{0:T(128)} %bitcast.chip_ref, ...), custom_call_target="tpu_custom_call" | custom-call | tf_op jit(solution)/shard_map/pack/pallas_call | solution.py:286
  3.2 6.1 %collective-permute-start = (bf16[528,128]{1,0:T(8,128)(2,1)}, bf16[528,128]{1,0:T(8,128)(2,1)S(1)}, u32[]{:S(2)}, u32[]{:S(2)}) collective-permute-start(bf16[528,128]{1,0:T(8,128)(2,1)} %get-tuple-element.25), channel_id=1, source_target_pairs={{0,14},{1,15},{2,12},{3,13},{4,10},{5,11},{6,8},{7,9},{8,6},{9,7},... | collective-permute-start | bytes 405512 | tf_op jit(solution)/shard_map/ppermute | solution.py:281
  9.3 0.2 collective-permute-start.1
  9.5 0.7 %collective-permute-start.2 = (bf16[528,128]{1,0:T(8,128)(2,1)}, bf16[528,128]{1,0:T(8,128)(2,1)S(1)}, u32[]{:S(2)}, u32[]{:S(2)}) collective-permute-start(bf16[528,128]{1,0:T(8,128)(2,1)} %get-tuple-element.27), channel_id=1, source_target_pairs={{0,10},{1,11},{2,8},{3,9},{4,14},{5,15},{6,12},{7,13},{8,2},{9,3},... | collective-permute-start | bytes 405512 | tf_op jit(solution)/shard_map/ppermute | solution.py:281
  10.2 2.0 %collective-permute-start.3 = (bf16[528,128]{1,0:T(8,128)(2,1)}, bf16[528,128]{1,0:T(8,128)(2,1)S(1)}, u32[]{:S(2)}, u32[]{:S(2)}) collective-permute-start(bf16[528,128]{1,0:T(8,128)(2,1)} %get-tuple-element.28), channel_id=1, source_target_pairs={{0,8},{1,9},{2,10},{3,11},{4,12},{5,13},{6,14},{7,15},{8,0},{9,1},... | collective-permute-start | bytes 405512 | tf_op jit(solution)/shard_map/ppermute | solution.py:281
  12.3 2.3 %collective-permute-start.4 = (bf16[528,128]{1,0:T(8,128)(2,1)}, bf16[528,128]{1,0:T(8,128)(2,1)S(1)}, u32[]{:S(2)}, u32[]{:S(2)}) collective-permute-start(bf16[528,128]{1,0:T(8,128)(2,1)} %get-tuple-element.29), channel_id=1, source_target_pairs={{0,6},{1,7},{2,4},{3,5},{4,2},{5,3},{6,0},{7,1},{8,14},{9,15},{10,... | collective-permute-start | bytes 405512 | tf_op jit(solution)/shard_map/ppermute | solution.py:281
  14.5 0.0 collective-permute-done.refs_1_
  14.5 11.1 %collective-permute-start.5 = (bf16[528,128]{1,0:T(8,128)(2,1)}, bf16[528,128]{1,0:T(8,128)(2,1)S(1)}, u32[]{:S(2)}, u32[]{:S(2)}) collective-permute-start(bf16[528,128]{1,0:T(8,128)(2,1)} %get-tuple-element.30), channel_id=1, source_target_pairs={{0,4},{1,5},{2,6},{3,7},{4,0},{5,1},{6,2},{7,3},{8,12},{9,13},{10,... | collective-permute-start | bytes 405512 | tf_op jit(solution)/shard_map/ppermute | solution.py:281
  25.7 0.0 collective-permute-done.1.refs_2_
  25.7 0.0 copy-start.2
  25.7 1.3 %collective-permute-start.6 = (bf16[528,128]{1,0:T(8,128)(2,1)}, bf16[528,128]{1,0:T(8,128)(2,1)S(1)}, u32[]{:S(2)}, u32[]{:S(2)}) collective-permute-start(bf16[528,128]{1,0:T(8,128)(2,1)} %get-tuple-element.31), channel_id=1, source_target_pairs={{0,2},{1,3},{2,0},{3,1},{4,6},{5,7},{6,4},{7,5},{8,10},{9,11},{10,... | collective-permute-start | bytes 405512 | tf_op jit(solution)/shard_map/ppermute | solution.py:281
  27.0 3.6 %collective-permute-done.2.refs_3_ = bf16[528,128]{1,0:T(8,128)(2,1)S(1)} collective-permute-done((bf16[528,128]{1,0:T(8,128)(2,1)}, bf16[528,128]{1,0:T(8,128)(2,1)S(1)}, u32[]{:S(2)}, u32[]{:S(2)}) %collective-permute-start.2) | collective-permute-done | bytes 135200 | tf_op jit(solution)/shard_map/ppermute | solution.py:281
  30.6 0.0 collective-permute-start.7
  30.6 1.9 %collective-permute-done.3.refs_4_ = bf16[528,128]{1,0:T(8,128)(2,1)S(1)} collective-permute-done((bf16[528,128]{1,0:T(8,128)(2,1)}, bf16[528,128]{1,0:T(8,128)(2,1)S(1)}, u32[]{:S(2)}, u32[]{:S(2)}) %collective-permute-start.3) | collective-permute-done | bytes 135200 | tf_op jit(solution)/shard_map/ppermute | solution.py:281
  32.6 0.0 collective-permute-start.8
  32.6 0.0 collective-permute-done.4.refs_5_
  32.6 0.5 collective-permute-start.9
  33.1 0.8 %collective-permute-done.5.refs_6_ = bf16[528,128]{1,0:T(8,128)(2,1)S(1)} collective-permute-done((bf16[528,128]{1,0:T(8,128)(2,1)}, bf16[528,128]{1,0:T(8,128)(2,1)S(1)}, u32[]{:S(2)}, u32[]{:S(2)}) %collective-permute-start.5) | collective-permute-done | bytes 135200 | tf_op jit(solution)/shard_map/ppermute | solution.py:281
  33.9 0.0 collective-permute-start.10
  33.9 0.0 collective-permute-done.6.refs_7_
  33.9 0.5 collective-permute-start.11
  34.4 0.0 collective-permute-done.7.refs_8_
  34.4 0.1 collective-permute-start.12
  34.4 0.0 collective-permute-done.8.refs_9_
  34.4 0.4 collective-permute-start.13
  34.9 0.0 collective-permute-done.9.refs_10_
  34.9 0.1 collective-permute-start.14
  35.0 0.2 collective-permute-done.10.refs_11_
  35.2 0.2 collective-permute-done.11.refs_12_
  35.4 0.3 collective-permute-done.12.refs_13_
  35.7 0.2 collective-permute-done.13.refs_14_
  35.9 0.3 collective-permute-done.14.refs_15_
  36.2 0.0 copy-done.2
  36.2 0.0 copy-start
  36.2 0.9 %copy-done = bf16[528,128]{1,0:T(8,128)(2,1)S(1)} copy-done((bf16[528,128]{1,0:T(8,128)(2,1)S(1)}, bf16[528,128]{1,0:T(8,128)(2,1)}, u32[]{:S(2)}) %copy-start) | copy-done | bytes 135192
  37.2 12.3 %chain.1 = (bf16[400,128]{1,0:T(8,128)(2,1)S(1)}, bf16[400,128]{1,0:T(8,128)(2,1)S(1)}, bf16[400,128]{1,0:T(8,128)(2,1)S(1)}, bf16[400,128]{1,0:T(8,128)(2,1)S(1...) custom-call(s32[8]{0:T(128)S(1)} %copy-done.2, ...), custom_call_target="tpu_custom_call" | custom-call | tf_op jit(solution)/shard_map/chain/pallas_call | solution.py:303
  49.5 2.5 %collective-permute-start.15 = (bf16[400,128]{1,0:T(8,128)(2,1)S(1)}, bf16[400,128]{1,0:T(8,128)(2,1)S(1)}, u32[]{:S(2)}, u32[]{:S(2)}) collective-permute-start(bf16[400,128]{1,0:T(8,128)(2,1)S(1)} %get-tuple-element.33), channel_id=1, source_target_pairs={{0,14},{1,15},{2,12},{3,13},{4,10},{5,11},{6,8},{7,9},{8,6},{9,7},... | collective-permute-start | bytes 307208 | tf_op jit(solution)/shard_map/ppermute | solution.py:281
  52.0 1.3 %collective-permute-start.16 = (bf16[400,128]{1,0:T(8,128)(2,1)S(1)}, bf16[400,128]{1,0:T(8,128)(2,1)S(1)}, u32[]{:S(2)}, u32[]{:S(2)}) collective-permute-start(bf16[400,128]{1,0:T(8,128)(2,1)S(1)} %get-tuple-element.34), channel_id=1, source_target_pairs={{0,12},{1,13},{2,14},{3,15},{4,8},{5,9},{6,10},{7,11},{8,4},{9,5},... | collective-permute-start | bytes 307208 | tf_op jit(solution)/shard_map/ppermute | solution.py:281
  53.4 0.0 collective-permute-start.17
  53.4 3.8 %collective-permute-start.18 = (bf16[400,128]{1,0:T(8,128)(2,1)S(1)}, bf16[400,128]{1,0:T(8,128)(2,1)S(1)}, u32[]{:S(2)}, u32[]{:S(2)}) collective-permute-start(bf16[400,128]{1,0:T(8,128)(2,1)S(1)} %get-tuple-element.36), channel_id=1, source_target_pairs={{0,8},{1,9},{2,10},{3,11},{4,12},{5,13},{6,14},{7,15},{8,0},{9,1},... | collective-permute-start | bytes 307208 | tf_op jit(solution)/shard_map/ppermute | solution.py:281
  57.2 0.1 collective-permute-start.19
  57.3 0.2 collective-permute-done.15.refs_1_
  57.6 6.5 %collective-permute-start.20 = (bf16[400,128]{1,0:T(8,128)(2,1)S(1)}, bf16[400,128]{1,0:T(8,128)(2,1)S(1)}, u32[]{:S(2)}, u32[]{:S(2)}) collective-permute-start(bf16[400,128]{1,0:T(8,128)(2,1)S(1)} %get-tuple-element.38), channel_id=1, source_target_pairs={{0,4},{1,5},{2,6},{3,7},{4,0},{5,1},{6,2},{7,3},{8,12},{9,13},{10,... | collective-permute-start | bytes 307208 | tf_op jit(solution)/shard_map/ppermute | solution.py:281
  64.0 0.0 collective-permute-done.16.refs_2_
  64.0 0.0 copy-start.1
  64.0 0.3 collective-permute-start.21
  64.3 4.2 %collective-permute-done.17.refs_3_ = bf16[400,128]{1,0:T(8,128)(2,1)S(1)} collective-permute-done((bf16[400,128]{1,0:T(8,128)(2,1)S(1)}, bf16[400,128]{1,0:T(8,128)(2,1)S(1)}, u32[]{:S(2)}, u32[]{:S(2)}) %collective-permute-start.17) | collective-permute-done | bytes 102432 | tf_op jit(solution)/shard_map/ppermute | solution.py:281
  68.5 0.6 collective-permute-done.18.refs_4_
  69.1 0.0 collective-permute-done.19.refs_5_
  69.1 1.0 %collective-permute-done.20.refs_6_ = bf16[400,128]{1,0:T(8,128)(2,1)S(1)} collective-permute-done((bf16[400,128]{1,0:T(8,128)(2,1)S(1)}, bf16[400,128]{1,0:T(8,128)(2,1)S(1)}, u32[]{:S(2)}, u32[]{:S(2)}) %collective-permute-start.20) | collective-permute-done | bytes 102432 | tf_op jit(solution)/shard_map/ppermute | solution.py:281
  70.1 0.0 collective-permute-done.21.refs_7_
  70.1 0.0 copy-done.1
  70.1 1.4 %unpack.1 = (bf16[128,1024]{1,0:T(8,128)(2,1)}, bf16[128,1024]{1,0:T(8,128)(2,1)}, bf16[128,1024]{1,0:T(8,128)(2,1)}, bf16[8,128]{1,0:T(8,128)(2,1)}) custom-call(s32[1]{0:T(128)} %bitcast.chip_ref, s32[1,128]{1,0:T(1,128)S(1)} %bitcast.5, bf16[400,128]{1,0:T(8,128)(2,1)S(1)} %get-tuple-element.32.refs_0_, ...), custom_call_target="tpu_custom_call" | custom-call | tf_op jit(solution)/shard_map/unpack/pallas_call | solution.py:329
Async XLA Ops:
  3.2 11.4 %collective-permute-start = (bf16[528,128]{1,0:T(8,128)(2,1)}, bf16[528,128]{1,0:T(8,128)(2,1)S(1)}, u32[]{:S(2)}, u32[]{:S(2)}) collective-permute-start(bf16[528,128]{1,0:T(8,128)(2,1)} %get-tuple-element.25), channel_id=1, source_target_pairs={{0,14},{1,15},{2,12},{3,13},{4,10},{5,11},{6,8},{7,9},{8,6},{9,7},... | collective-permute-start | bytes 405512 | tf_op jit(solution)/shard_map/ppermute | solution.py:281
  9.3 16.4 %collective-permute-start.1 = (bf16[528,128]{1,0:T(8,128)(2,1)}, bf16[528,128]{1,0:T(8,128)(2,1)S(1)}, u32[]{:S(2)}, u32[]{:S(2)}) collective-permute-start(bf16[528,128]{1,0:T(8,128)(2,1)} %get-tuple-element.26), channel_id=1, source_target_pairs={{0,12},{1,13},{2,14},{3,15},{4,8},{5,9},{6,10},{7,11},{8,4},{9,5},... | collective-permute-start | bytes 405512 | tf_op jit(solution)/shard_map/ppermute | solution.py:281
  9.5 21.2 %collective-permute-start.2 = (bf16[528,128]{1,0:T(8,128)(2,1)}, bf16[528,128]{1,0:T(8,128)(2,1)S(1)}, u32[]{:S(2)}, u32[]{:S(2)}) collective-permute-start(bf16[528,128]{1,0:T(8,128)(2,1)} %get-tuple-element.27), channel_id=1, source_target_pairs={{0,10},{1,11},{2,8},{3,9},{4,14},{5,15},{6,12},{7,13},{8,2},{9,3},... | collective-permute-start | bytes 405512 | tf_op jit(solution)/shard_map/ppermute | solution.py:281
  10.2 22.4 %collective-permute-start.3 = (bf16[528,128]{1,0:T(8,128)(2,1)}, bf16[528,128]{1,0:T(8,128)(2,1)S(1)}, u32[]{:S(2)}, u32[]{:S(2)}) collective-permute-start(bf16[528,128]{1,0:T(8,128)(2,1)} %get-tuple-element.28), channel_id=1, source_target_pairs={{0,8},{1,9},{2,10},{3,11},{4,12},{5,13},{6,14},{7,15},{8,0},{9,1},... | collective-permute-start | bytes 405512 | tf_op jit(solution)/shard_map/ppermute | solution.py:281
  12.3 20.3 %collective-permute-start.4 = (bf16[528,128]{1,0:T(8,128)(2,1)}, bf16[528,128]{1,0:T(8,128)(2,1)S(1)}, u32[]{:S(2)}, u32[]{:S(2)}) collective-permute-start(bf16[528,128]{1,0:T(8,128)(2,1)} %get-tuple-element.29), channel_id=1, source_target_pairs={{0,6},{1,7},{2,4},{3,5},{4,2},{5,3},{6,0},{7,1},{8,14},{9,15},{10,... | collective-permute-start | bytes 405512 | tf_op jit(solution)/shard_map/ppermute | solution.py:281
  14.5 19.3 %collective-permute-start.5 = (bf16[528,128]{1,0:T(8,128)(2,1)}, bf16[528,128]{1,0:T(8,128)(2,1)S(1)}, u32[]{:S(2)}, u32[]{:S(2)}) collective-permute-start(bf16[528,128]{1,0:T(8,128)(2,1)} %get-tuple-element.30), channel_id=1, source_target_pairs={{0,4},{1,5},{2,6},{3,7},{4,0},{5,1},{6,2},{7,3},{8,12},{9,13},{10,... | collective-permute-start | bytes 405512 | tf_op jit(solution)/shard_map/ppermute | solution.py:281
  25.7 10.6 %copy-start.2 = (s32[8]{0:T(128)S(1)}, s32[8]{0:T(128)}, u32[]{:S(2)}) copy-start(s32[8]{0:T(128)} %lengths_ref.1) | copy-start | bytes 100
  25.7 8.2 %collective-permute-start.6 = (bf16[528,128]{1,0:T(8,128)(2,1)}, bf16[528,128]{1,0:T(8,128)(2,1)S(1)}, u32[]{:S(2)}, u32[]{:S(2)}) collective-permute-start(bf16[528,128]{1,0:T(8,128)(2,1)} %get-tuple-element.31), channel_id=1, source_target_pairs={{0,2},{1,3},{2,0},{3,1},{4,6},{5,7},{6,4},{7,5},{8,10},{9,11},{10,... | collective-permute-start | bytes 405512 | tf_op jit(solution)/shard_map/ppermute | solution.py:281
  30.6 3.7 %collective-permute-start.7 = (bf16[528,128]{1,0:T(8,128)(2,1)}, bf16[528,128]{1,0:T(8,128)(2,1)S(1)}, u32[]{:S(2)}, u32[]{:S(2)}) collective-permute-start(bf16[528,128]{1,0:T(8,128)(2,1)} %get-tuple-element.24.refs_0_), channel_id=1, source_target_pairs={{0,1},{1,0},{2,3},{3,2},{4,5},{5,4},{6,7},{7,6},{8,9},{9,8},{10,11... | collective-permute-start | bytes 405512 | tf_op jit(solution)/shard_map/ppermute | solution.py:284
  32.6 1.9 %collective-permute-start.8 = (bf16[528,128]{1,0:T(8,128)(2,1)S(1)}, bf16[528,128]{1,0:T(8,128)(2,1)S(1)}, u32[]{:S(2)}, u32[]{:S(2)}) collective-permute-start(bf16[528,128]{1,0:T(8,128)(2,1)S(1)} %collective-permute-done.refs_1_), channel_id=1, source_target_pairs={{0,1},{1,0},{2,3},{3,2},{4,5},{5,4},{6,7},{7,6},{8,9},{9,8},{10,11... | collective-permute-start | bytes 405512 | tf_op jit(solution)/shard_map/ppermute | solution.py:284
  32.6 2.3 %collective-permute-start.9 = (bf16[528,128]{1,0:T(8,128)(2,1)S(1)}, bf16[528,128]{1,0:T(8,128)(2,1)S(1)}, u32[]{:S(2)}, u32[]{:S(2)}) collective-permute-start(bf16[528,128]{1,0:T(8,128)(2,1)S(1)} %collective-permute-done.1.refs_2_), channel_id=1, source_target_pairs={{0,1},{1,0},{2,3},{3,2},{4,5},{5,4},{6,7},{7,6},{8,9},{9,8},{10,11... | collective-permute-start | bytes 405512 | tf_op jit(solution)/shard_map/ppermute | solution.py:284
  33.9 1.4 %collective-permute-start.10 = (bf16[528,128]{1,0:T(8,128)(2,1)S(1)}, bf16[528,128]{1,0:T(8,128)(2,1)S(1)}, u32[]{:S(2)}, u32[]{:S(2)}) collective-permute-start(bf16[528,128]{1,0:T(8,128)(2,1)S(1)} %collective-permute-done.2.refs_3_), channel_id=1, source_target_pairs={{0,1},{1,0},{2,3},{3,2},{4,5},{5,4},{6,7},{7,6},{8,9},{9,8},{10,11... | collective-permute-start | bytes 405512 | tf_op jit(solution)/shard_map/ppermute | solution.py:284
  33.9 1.5 %collective-permute-start.11 = (bf16[528,128]{1,0:T(8,128)(2,1)S(1)}, bf16[528,128]{1,0:T(8,128)(2,1)S(1)}, u32[]{:S(2)}, u32[]{:S(2)}) collective-permute-start(bf16[528,128]{1,0:T(8,128)(2,1)S(1)} %collective-permute-done.3.refs_4_), channel_id=1, source_target_pairs={{0,1},{1,0},{2,3},{3,2},{4,5},{5,4},{6,7},{7,6},{8,9},{9,8},{10,11... | collective-permute-start | bytes 405512 | tf_op jit(solution)/shard_map/ppermute | solution.py:284
  34.4 1.4 %collective-permute-start.12 = (bf16[528,128]{1,0:T(8,128)(2,1)S(1)}, bf16[528,128]{1,0:T(8,128)(2,1)S(1)}, u32[]{:S(2)}, u32[]{:S(2)}) collective-permute-start(bf16[528,128]{1,0:T(8,128)(2,1)S(1)} %collective-permute-done.4.refs_5_), channel_id=1, source_target_pairs={{0,1},{1,0},{2,3},{3,2},{4,5},{5,4},{6,7},{7,6},{8,9},{9,8},{10,11... | collective-permute-start | bytes 405512 | tf_op jit(solution)/shard_map/ppermute | solution.py:284
  34.4 1.5 %collective-permute-start.13 = (bf16[528,128]{1,0:T(8,128)(2,1)S(1)}, bf16[528,128]{1,0:T(8,128)(2,1)S(1)}, u32[]{:S(2)}, u32[]{:S(2)}) collective-permute-start(bf16[528,128]{1,0:T(8,128)(2,1)S(1)} %collective-permute-done.5.refs_6_), channel_id=1, source_target_pairs={{0,1},{1,0},{2,3},{3,2},{4,5},{5,4},{6,7},{7,6},{8,9},{9,8},{10,11... | collective-permute-start | bytes 405512 | tf_op jit(solution)/shard_map/ppermute | solution.py:284
  34.9 1.4 %collective-permute-start.14 = (bf16[528,128]{1,0:T(8,128)(2,1)S(1)}, bf16[528,128]{1,0:T(8,128)(2,1)S(1)}, u32[]{:S(2)}, u32[]{:S(2)}) collective-permute-start(bf16[528,128]{1,0:T(8,128)(2,1)S(1)} %collective-permute-done.6.refs_7_), channel_id=1, source_target_pairs={{0,1},{1,0},{2,3},{3,2},{4,5},{5,4},{6,7},{7,6},{8,9},{9,8},{10,11... | collective-permute-start | bytes 405512 | tf_op jit(solution)/shard_map/ppermute | solution.py:284
  36.2 0.9 %copy-start = (bf16[528,128]{1,0:T(8,128)(2,1)S(1)}, bf16[528,128]{1,0:T(8,128)(2,1)}, u32[]{:S(2)}) copy-start(bf16[528,128]{1,0:T(8,128)(2,1)} %get-tuple-element.24.refs_0_) | copy-start | bytes 405508
  49.5 8.1 %collective-permute-start.15 = (bf16[400,128]{1,0:T(8,128)(2,1)S(1)}, bf16[400,128]{1,0:T(8,128)(2,1)S(1)}, u32[]{:S(2)}, u32[]{:S(2)}) collective-permute-start(bf16[400,128]{1,0:T(8,128)(2,1)S(1)} %get-tuple-element.33), channel_id=1, source_target_pairs={{0,14},{1,15},{2,12},{3,13},{4,10},{5,11},{6,8},{7,9},{8,6},{9,7},... | collective-permute-start | bytes 307208 | tf_op jit(solution)/shard_map/ppermute | solution.py:281
  52.0 12.0 %collective-permute-start.16 = (bf16[400,128]{1,0:T(8,128)(2,1)S(1)}, bf16[400,128]{1,0:T(8,128)(2,1)S(1)}, u32[]{:S(2)}, u32[]{:S(2)}) collective-permute-start(bf16[400,128]{1,0:T(8,128)(2,1)S(1)} %get-tuple-element.34), channel_id=1, source_target_pairs={{0,12},{1,13},{2,14},{3,15},{4,8},{5,9},{6,10},{7,11},{8,4},{9,5},... | collective-permute-start | bytes 307208 | tf_op jit(solution)/shard_map/ppermute | solution.py:281
  53.4 15.1 %collective-permute-start.17 = (bf16[400,128]{1,0:T(8,128)(2,1)S(1)}, bf16[400,128]{1,0:T(8,128)(2,1)S(1)}, u32[]{:S(2)}, u32[]{:S(2)}) collective-permute-start(bf16[400,128]{1,0:T(8,128)(2,1)S(1)} %get-tuple-element.35), channel_id=1, source_target_pairs={{0,10},{1,11},{2,8},{3,9},{4,14},{5,15},{6,12},{7,13},{8,2},{9,3},... | collective-permute-start | bytes 307208 | tf_op jit(solution)/shard_map/ppermute | solution.py:281
  53.4 15.7 %collective-permute-start.18 = (bf16[400,128]{1,0:T(8,128)(2,1)S(1)}, bf16[400,128]{1,0:T(8,128)(2,1)S(1)}, u32[]{:S(2)}, u32[]{:S(2)}) collective-permute-start(bf16[400,128]{1,0:T(8,128)(2,1)S(1)} %get-tuple-element.36), channel_id=1, source_target_pairs={{0,8},{1,9},{2,10},{3,11},{4,12},{5,13},{6,14},{7,15},{8,0},{9,1},... | collective-permute-start | bytes 307208 | tf_op jit(solution)/shard_map/ppermute | solution.py:281
  57.2 11.9 %collective-permute-start.19 = (bf16[400,128]{1,0:T(8,128)(2,1)S(1)}, bf16[400,128]{1,0:T(8,128)(2,1)S(1)}, u32[]{:S(2)}, u32[]{:S(2)}) collective-permute-start(bf16[400,128]{1,0:T(8,128)(2,1)S(1)} %get-tuple-element.37), channel_id=1, source_target_pairs={{0,6},{1,7},{2,4},{3,5},{4,2},{5,3},{6,0},{7,1},{8,14},{9,15},{10,... | collective-permute-start | bytes 307208 | tf_op jit(solution)/shard_map/ppermute | solution.py:281
  57.6 12.5 %collective-permute-start.20 = (bf16[400,128]{1,0:T(8,128)(2,1)S(1)}, bf16[400,128]{1,0:T(8,128)(2,1)S(1)}, u32[]{:S(2)}, u32[]{:S(2)}) collective-permute-start(bf16[400,128]{1,0:T(8,128)(2,1)S(1)} %get-tuple-element.38), channel_id=1, source_target_pairs={{0,4},{1,5},{2,6},{3,7},{4,0},{5,1},{6,2},{7,3},{8,12},{9,13},{10,... | collective-permute-start | bytes 307208 | tf_op jit(solution)/shard_map/ppermute | solution.py:281
  64.0 6.1 %copy-start.1 = (s32[128]{0:T(128)S(1)}, s32[128]{0:T(128)}, u32[]{:S(2)}) copy-start(s32[128]{0:T(128)} %param.12) | copy-start | bytes 1540
  64.0 6.1 %collective-permute-start.21 = (bf16[400,128]{1,0:T(8,128)(2,1)S(1)}, bf16[400,128]{1,0:T(8,128)(2,1)S(1)}, u32[]{:S(2)}, u32[]{:S(2)}) collective-permute-start(bf16[400,128]{1,0:T(8,128)(2,1)S(1)} %get-tuple-element.39), channel_id=1, source_target_pairs={{0,2},{1,3},{2,0},{3,1},{4,6},{5,7},{6,4},{7,5},{8,10},{9,11},{10,... | collective-permute-start | bytes 307208 | tf_op jit(solution)/shard_map/ppermute | solution.py:281

commit v4 on v3

--- a/solution.py
+++ b/solution.py
@@ -9,6 +9,9 @@
 
 SPAN = 128
 META = 16
+COMING = (0, 1, 2, 6, 7, 4, 5, 3)
+GOING = (0, 7, 6, 5, 4, 3, 2, 1)
+TOGETHER = 3
 F32 = jnp.float32
 BF16 = jnp.bfloat16
 I32 = jnp.int32
@@ -56,13 +59,13 @@
     copies[4].wait()
     decay = dot(held[4][...], sort, NT)
     for s in range(heads):
-        head = chip ^ ((heads - s) % heads)
+        head = chip ^ COMING[s]
         mine = jnp.sum(jnp.where(iota((heads, rows), 0) == head, decay, 0.0), axis=0, keepdims=True)
         built[s, 4 * rows:, :] = jnp.where(line == 0, mine, where).astype(BF16)
     for a in range(4):
         copies[a].wait()
     for s in range(heads):
-        head = chip ^ ((heads - s) % heads)
+        head = chip ^ COMING[s]
         at = pl.ds(pl.multiple_of(head * SPAN, SPAN), SPAN)
         together = jnp.concatenate([held[a][:, at] for a in range(4)], axis=1)
         together = dot(sort, together, NN).astype(BF16)
@@ -81,11 +84,14 @@
 
 
 def chain_kernel(heads, lengths_ref, *refs):
-    sources = len(refs) - heads - 14
-    blocks, outs, scratch = refs[:sources], refs[sources:sources + heads], refs[sources + heads:]
+    given, answers, scratch = refs[:-heads - 14], refs[-heads - 14:-14], refs[-14:]
+    size = min(ref.shape[0] for ref in given)
+    blocks = [ref.at[at:at + size] for ref in given for at in range(0, ref.shape[0], size)]
+    outs = [answers[GOING.index(s)] for s in COMING]
+    sources = len(blocks)
     (hi_ref, lo_ref, win_ref, at_ref, sem, down_ref, cum_ref, chain_ref, gained_ref, weighted_ref,
      carried_ref, pulled_ref, low_ref, tail_ref) = scratch
-    rows = (blocks[0].shape[0] - META) // 4
+    rows = (size - META) // 4
     frames = rows * sources
     spans = frames // SPAN
     window = 16 * pl.cdiv(2 * rows // sources, 16) + 16
@@ -248,6 +254,12 @@
         outs[s][3 * rows:, :] = jnp.broadcast_to(found, (META, rows)).astype(BF16)
 
 
+def join_kernel(*refs):
+    size = refs[0].shape[0]
+    for n, ref in enumerate(refs[:-1]):
+        refs[-1][n * size:(n + 1) * size, :] = ref[...]
+
+
 def unpack_kernel(chip_ref, pos_ref, *refs):
     heads = len(refs) - 4
     blocks, outs = refs[:heads], refs[heads:]
@@ -258,7 +270,7 @@
     line = iota((META, rows), 0)
     tails = jnp.zeros((META, rows), F32)
     for s in range(heads):
-        head = chip ^ ((heads - s) % heads)
+        head = chip ^ GOING[s]
         at = pl.ds(pl.multiple_of(head * SPAN, SPAN), SPAN)
         together = jnp.concatenate([blocks[s][a * rows:(a + 1) * rows, :] for a in range(3)], axis=1)
         together = dot(loose, together, NN).astype(BF16)
@@ -294,7 +306,18 @@
         compiler_params=pltpu.CompilerParams(vmem_limit_bytes=60 * 2**20),
         name="pack",
     )(chip, queries, keys, values, out_grad, log_decay.T, frame_pos.reshape(1, rows))
-    got = [packets[0]] + [across(packets[s], heads - s) for s in range(1, heads)]
+    got = [packets[0]] + [across(packets[s], COMING[s]) for s in range(1, heads)]
+    size = 4 * rows + META
+    joined = pl.pallas_call(
+        join_kernel,
+        out_shape=jax.ShapeDtypeStruct((TOGETHER * size, SPAN), BF16),
+        in_specs=[VMEM] * TOGETHER,
+        out_specs=VMEM,
+        compiler_params=pltpu.CompilerParams(vmem_limit_bytes=4 * 2**20),
+        cost_estimate=pl.CostEstimate(flops=2**30, bytes_accessed=2**18, transcendentals=0),
+        name="join",
+    )(*got[:TOGETHER])
+    got = [joined, *got[TOGETHER:]]
     everything = list(got)
     for t in range(1, cores):
         everything += [beside(x, t) for x in got]
@@ -303,7 +326,7 @@
     back = pl.pallas_call(
         functools.partial(chain_kernel, heads),
         out_shape=[jax.ShapeDtypeStruct((3 * rows + META, SPAN), BF16)] * heads,
-        in_specs=[SMEM] + [VMEM] * peers,
+        in_specs=[SMEM] + [VMEM] * len(everything),
         out_specs=[VMEM] * heads,
         scratch_shapes=[
             pltpu.VMEM((peers, SPAN), F32),
@@ -324,7 +347,7 @@
         compiler_params=pltpu.CompilerParams(vmem_limit_bytes=frames * 6 * 2**10 + 8 * 2**20),
         name="chain",
     )(trial_lengths, *everything)
-    returned = [back[0]] + [across(back[s], heads - s) for s in range(1, heads)]
+    returned = [back[0]] + [across(back[s], GOING[s]) for s in range(1, heads)]
 
     *grads, tails = pl.pallas_call(
         unpack_kernel,

time: 71.7 us -> 70 us (0.976)
  starting transfers between devices: 40 us -> 33.6 us
  waiting for transfers between devices: 13.7 us -> 17.5 us
  local copies, waits for them, and re-layouts: 0.91 us -> 1.71 us
    ppermute x14, starting transfers between devices: 38.4 us -> 32.9 us  [across(): return lax.ppermute(x, 'ctx', [(p, p ^ s * cores) for p in range(peers)])]
    ppermute x14, waiting for transfers between devices: 12.4 us -> 16.2 us  [across(): return lax.ppermute(x, 'ctx', [(p, p ^ s * cores) for p in range(peers)])]
    ppermute x8 -> x6, starting transfers between devices: 1.6 us -> 0.66 us  [beside(): return lax.ppermute(x, 'ctx', [(p, p ^ t) for p in range(peers)])]
    unnamed x6 -> x12, local copies, waits for them, and re-layouts: 0.91 us -> 1.71 us
  transfers between devices with their start and end apart: 22 -> 20, of which waited for: 12 -> 10; matrix products, arithmetic and copies ran while one was open for 0% -> 0% of each run, Pallas kernels for 0% -> 0%
where the time goes in v4:
time: 70 us; the launch traced here: 69.8 us
  starting transfers between devices  33.6 us (48%)
  waiting for transfers between devices  17.5 us (25%)
  Pallas kernels  16.2 us (23%)
  local copies, waits for them, and re-layouts  1.71 us (2%)
  between operations  0.71 us (1%)
    ppermute x14, starting transfers between devices, across(): return lax.ppermute(x, 'ctx', [(p, p ^ s * cores) for p in range(peers)])  32.9 us
    ppermute x14, waiting for transfers between devices, across(): return lax.ppermute(x, 'ctx', [(p, p ^ s * cores) for p in range(peers)])  16.2 us
    pallas_call x1, Pallas kernels, body(): pl.pallas_call(functools.partial(chain_kernel, heads), out_shape=[jax.Sha...  12.3 us
    pallas_call x1, Pallas kernels, body(): pl.pallas_call(pack_kernel, out_shape=[jax.ShapeDtypeStruct((4 * rows + M...  2.51 us
    unnamed x12, local copies, waits for them, and re-layouts  1.71 us
    pallas_call x1, Pallas kernels, body(): pl.pallas_call(unpack_kernel, out_shape=[jax.ShapeDtypeStruct((rows, widt...  1.43 us
  transfers between devices with their start and end apart: 20, of which 10 were waited for; matrix products, arithmetic and copies ran while one was open for 0% of the time, Pallas kernels for 0%

profile of v4, /device:TPU:0, one launch (start us, length us, event | category | flops | bytes accessed | tf_op | source)
XLA Modules:
  0.0 69.8 jit_solution(5413832182448233008)
XLA Ops:
  0.6 2.5 %pack.1 = (bf16[528,128]{1,0:T(8,128)(2,1)}, bf16[528,128]{1,0:T(8,128)(2,1)}, bf16[528,128]{1,0:T(8,128)(2,1)}, bf16[528,128]{1,0:T(8,128)(2,1)}, bf16[528,128]...) custom-call(s32[1]{0:T(128)} %bitcast.chip_ref, ...), custom_call_target="tpu_custom_call" | custom-call | tf_op jit(solution)/shard_map/pack/pallas_call | solution.py:298
  3.2 3.0 %collective-permute-start = (bf16[528,128]{1,0:T(8,128)(2,1)}, bf16[528,128]{1,0:T(8,128)(2,1)S(1)}, u32[]{:S(2)}, u32[]{:S(2)}) collective-permute-start(bf16[528,128]{1,0:T(8,128)(2,1)} %get-tuple-element.25), channel_id=1, source_target_pairs={{0,2},{1,3},{2,0},{3,1},{4,6},{5,7},{6,4},{7,5},{8,10},{9,11},{10,... | collective-permute-start | bytes 405512 | tf_op jit(solution)/shard_map/ppermute | solution.py:293
  6.2 1.6 %collective-permute-start.1 = (bf16[528,128]{1,0:T(8,128)(2,1)}, bf16[528,128]{1,0:T(8,128)(2,1)S(1)}, u32[]{:S(2)}, u32[]{:S(2)}) collective-permute-start(bf16[528,128]{1,0:T(8,128)(2,1)} %get-tuple-element.26), channel_id=1, source_target_pairs={{0,4},{1,5},{2,6},{3,7},{4,0},{5,1},{6,2},{7,3},{8,12},{9,13},{10,... | collective-permute-start | bytes 405512 | tf_op jit(solution)/shard_map/ppermute | solution.py:293
  7.8 2.5 %collective-permute-start.2 = (bf16[528,128]{1,0:T(8,128)(2,1)}, bf16[528,128]{1,0:T(8,128)(2,1)S(1)}, u32[]{:S(2)}, u32[]{:S(2)}) collective-permute-start(bf16[528,128]{1,0:T(8,128)(2,1)} %get-tuple-element.27), channel_id=1, source_target_pairs={{0,12},{1,13},{2,14},{3,15},{4,8},{5,9},{6,10},{7,11},{8,4},{9,5},... | collective-permute-start | bytes 405512 | tf_op jit(solution)/shard_map/ppermute | solution.py:293
  10.3 1.3 %collective-permute-start.3 = (bf16[528,128]{1,0:T(8,128)(2,1)}, bf16[528,128]{1,0:T(8,128)(2,1)S(1)}, u32[]{:S(2)}, u32[]{:S(2)}) collective-permute-start(bf16[528,128]{1,0:T(8,128)(2,1)} %get-tuple-element.28), channel_id=1, source_target_pairs={{0,14},{1,15},{2,12},{3,13},{4,10},{5,11},{6,8},{7,9},{8,6},{9,7},... | collective-permute-start | bytes 405512 | tf_op jit(solution)/shard_map/ppermute | solution.py:293
  11.5 0.0 collective-permute-done.refs_1_
  11.5 0.0 collective-permute-done.1.refs_2_
  11.6 0.0 copy-start.2
  11.6 0.9 %copy-done.2 = bf16[528,128]{1,0:T(8,128)(2,1)S(1)} copy-done((bf16[528,128]{1,0:T(8,128)(2,1)S(1)}, bf16[528,128]{1,0:T(8,128)(2,1)}, u32[]{:S(2)}) %copy-start.2) | copy-done | bytes 135192
  12.5 0.0 copy-start.5
  12.5 0.0 copy-start.4
  12.5 0.0 copy-start.3
  12.5 0.1 collective-permute-start.7
  12.6 0.8 %copy-done.5 = bf16[528,128]{1,0:T(8,128)(2,1)S(1)} copy-done((bf16[528,128]{1,0:T(8,128)(2,1)S(1)}, bf16[528,128]{1,0:T(8,128)(2,1)}, u32[]{:S(2)}) %copy-start.5) | copy-done | bytes 135192
  13.4 4.0 %collective-permute-start.4 = (bf16[528,128]{1,0:T(8,128)(2,1)S(1)}, bf16[528,128]{1,0:T(8,128)(2,1)S(1)}, u32[]{:S(2)}, u32[]{:S(2)}) collective-permute-start(bf16[528,128]{1,0:T(8,128)(2,1)S(1)} %copy-done.5), channel_id=1, source_target_pairs={{0,8},{1,9},{2,10},{3,11},{4,12},{5,13},{6,14},{7,15},{8,0},{9,1},... | collective-permute-start | bytes 405512 | tf_op jit(solution)/shard_map/ppermute | solution.py:293
  17.3 0.0 copy-done.4
  17.3 0.0 copy-start.1
  17.3 0.0 collective-permute-start.5
  17.3 0.5 collective-permute-done.2.refs_1_
  17.8 0.0 copy-done.3
  17.8 8.5 %collective-permute-start.6 = (bf16[528,128]{1,0:T(8,128)(2,1)S(1)}, bf16[528,128]{1,0:T(8,128)(2,1)S(1)}, u32[]{:S(2)}, u32[]{:S(2)}) collective-permute-start(bf16[528,128]{1,0:T(8,128)(2,1)S(1)} %copy-done.3), channel_id=1, source_target_pairs={{0,6},{1,7},{2,4},{3,5},{4,2},{5,3},{6,0},{7,1},{8,14},{9,15},{10,... | collective-permute-start | bytes 405512 | tf_op jit(solution)/shard_map/ppermute | solution.py:293
  26.4 0.0 collective-permute-done.3.refs_2_
  26.4 0.0 collective-permute-start.8
  26.4 6.9 %collective-permute-done.4.refs_3_ = bf16[528,128]{1,0:T(8,128)(2,1)S(1)} collective-permute-done((bf16[528,128]{1,0:T(8,128)(2,1)S(1)}, bf16[528,128]{1,0:T(8,128)(2,1)S(1)}, u32[]{:S(2)}, u32[]{:S(2)}) %collective-permute-start.4) | collective-permute-done | bytes 135200 | tf_op jit(solution)/shard_map/ppermute | solution.py:293
  33.3 0.0 collective-permute-start.9
  33.3 0.6 collective-permute-done.5.refs_4_
  33.8 0.0 collective-permute-start.10
  33.8 0.0 collective-permute-done.6.refs_5_
  33.8 0.5 collective-permute-start.11
  34.3 0.0 collective-permute-done.8.refs_7_
  34.3 0.1 collective-permute-start.12
  34.4 0.2 collective-permute-done.9.refs_8_
  34.6 0.6 collective-permute-done.10.refs_9_
  35.2 0.2 collective-permute-done.11.refs_10_
  35.4 0.3 collective-permute-done.12.refs_11_
  35.7 0.0 collective-permute-done.7.refs_6_
  35.7 0.0 copy-done.1
  35.7 12.3 %chain.1 = (bf16[400,128]{1,0:T(8,128)(2,1)S(1)}, bf16[400,128]{1,0:T(8,128)(2,1)S(1)}, bf16[400,128]{1,0:T(8,128)(2,1)S(1)}, bf16[400,128]{1,0:T(8,128)(2,1)S(1...) custom-call(s32[8]{0:T(128)S(1)} %copy-done.1, ...), custom_call_target="tpu_custom_call" | custom-call | tf_op jit(solution)/shard_map/chain/pallas_call | solution.py:326
  48.0 4.4 %collective-permute-start.13 = (bf16[400,128]{1,0:T(8,128)(2,1)S(1)}, bf16[400,128]{1,0:T(8,128)(2,1)S(1)}, u32[]{:S(2)}, u32[]{:S(2)}) collective-permute-start(bf16[400,128]{1,0:T(8,128)(2,1)S(1)} %get-tuple-element.33), channel_id=1, source_target_pairs={{0,14},{1,15},{2,12},{3,13},{4,10},{5,11},{6,8},{7,9},{8,6},{9,7},... | collective-permute-start | bytes 307208 | tf_op jit(solution)/shard_map/ppermute | solution.py:293
  52.4 1.3 %collective-permute-start.14 = (bf16[400,128]{1,0:T(8,128)(2,1)S(1)}, bf16[400,128]{1,0:T(8,128)(2,1)S(1)}, u32[]{:S(2)}, u32[]{:S(2)}) collective-permute-start(bf16[400,128]{1,0:T(8,128)(2,1)S(1)} %get-tuple-element.34), channel_id=1, source_target_pairs={{0,12},{1,13},{2,14},{3,15},{4,8},{5,9},{6,10},{7,11},{8,4},{9,5},... | collective-permute-start | bytes 307208 | tf_op jit(solution)/shard_map/ppermute | solution.py:293
  53.7 0.0 collective-permute-start.15
  53.7 2.0 %collective-permute-start.16 = (bf16[400,128]{1,0:T(8,128)(2,1)S(1)}, bf16[400,128]{1,0:T(8,128)(2,1)S(1)}, u32[]{:S(2)}, u32[]{:S(2)}) collective-permute-start(bf16[400,128]{1,0:T(8,128)(2,1)S(1)} %get-tuple-element.36), channel_id=1, source_target_pairs={{0,8},{1,9},{2,10},{3,11},{4,12},{5,13},{6,14},{7,15},{8,0},{9,1},... | collective-permute-start | bytes 307208 | tf_op jit(solution)/shard_map/ppermute | solution.py:293
  55.7 2.0 %collective-permute-start.17 = (bf16[400,128]{1,0:T(8,128)(2,1)S(1)}, bf16[400,128]{1,0:T(8,128)(2,1)S(1)}, u32[]{:S(2)}, u32[]{:S(2)}) collective-permute-start(bf16[400,128]{1,0:T(8,128)(2,1)S(1)} %get-tuple-element.37), channel_id=1, source_target_pairs={{0,6},{1,7},{2,4},{3,5},{4,2},{5,3},{6,0},{7,1},{8,14},{9,15},{10,... | collective-permute-start | bytes 307208 | tf_op jit(solution)/shard_map/ppermute | solution.py:293
  57.7 0.0 collective-permute-done.13.refs_1_
  57.7 1.8 %collective-permute-start.18 = (bf16[400,128]{1,0:T(8,128)(2,1)S(1)}, bf16[400,128]{1,0:T(8,128)(2,1)S(1)}, u32[]{:S(2)}, u32[]{:S(2)}) collective-permute-start(bf16[400,128]{1,0:T(8,128)(2,1)S(1)} %get-tuple-element.38), channel_id=1, source_target_pairs={{0,4},{1,5},{2,6},{3,7},{4,0},{5,1},{6,2},{7,3},{8,12},{9,13},{10,... | collective-permute-start | bytes 307208 | tf_op jit(solution)/shard_map/ppermute | solution.py:293
  59.5 0.5 collective-permute-done.14.refs_2_
  60.0 0.0 copy-start
  60.0 0.6 collective-permute-start.19
  60.5 6.3 %collective-permute-done.15.refs_3_ = bf16[400,128]{1,0:T(8,128)(2,1)S(1)} collective-permute-done((bf16[400,128]{1,0:T(8,128)(2,1)S(1)}, bf16[400,128]{1,0:T(8,128)(2,1)S(1)}, u32[]{:S(2)}, u32[]{:S(2)}) %collective-permute-start.15) | collective-permute-done | bytes 102432 | tf_op jit(solution)/shard_map/ppermute | solution.py:293
  66.8 1.5 %collective-permute-done.16.refs_4_ = bf16[400,128]{1,0:T(8,128)(2,1)S(1)} collective-permute-done((bf16[400,128]{1,0:T(8,128)(2,1)S(1)}, bf16[400,128]{1,0:T(8,128)(2,1)S(1)}, u32[]{:S(2)}, u32[]{:S(2)}) %collective-permute-start.16) | collective-permute-done | bytes 102432 | tf_op jit(solution)/shard_map/ppermute | solution.py:293
  68.3 0.0 collective-permute-done.17.refs_5_
  68.3 0.0 collective-permute-done.18.refs_6_
  68.3 0.0 collective-permute-done.19.refs_7_
  68.3 0.0 copy-done
  68.4 1.4 %unpack.1 = (bf16[128,1024]{1,0:T(8,128)(2,1)}, bf16[128,1024]{1,0:T(8,128)(2,1)}, bf16[128,1024]{1,0:T(8,128)(2,1)}, bf16[8,128]{1,0:T(8,128)(2,1)}) custom-call(s32[1]{0:T(128)} %bitcast.chip_ref, s32[1,128]{1,0:T(1,128)S(1)} %bitcast.5, bf16[400,128]{1,0:T(8,128)(2,1)S(1)} %get-tuple-element.32.refs_0_, ...), custom_call_target="tpu_custom_call" | custom-call | tf_op jit(solution)/shard_map/unpack/pallas_call | solution.py:352
  (1 shorter events, 0.0 us)
Async XLA Ops:
  3.2 8.4 %collective-permute-start = (bf16[528,128]{1,0:T(8,128)(2,1)}, bf16[528,128]{1,0:T(8,128)(2,1)S(1)}, u32[]{:S(2)}, u32[]{:S(2)}) collective-permute-start(bf16[528,128]{1,0:T(8,128)(2,1)} %get-tuple-element.25), channel_id=1, source_target_pairs={{0,2},{1,3},{2,0},{3,1},{4,6},{5,7},{6,4},{7,5},{8,10},{9,11},{10,... | collective-permute-start | bytes 405512 | tf_op jit(solution)/shard_map/ppermute | solution.py:293
  6.2 5.4 %collective-permute-start.1 = (bf16[528,128]{1,0:T(8,128)(2,1)}, bf16[528,128]{1,0:T(8,128)(2,1)S(1)}, u32[]{:S(2)}, u32[]{:S(2)}) collective-permute-start(bf16[528,128]{1,0:T(8,128)(2,1)} %get-tuple-element.26), channel_id=1, source_target_pairs={{0,4},{1,5},{2,6},{3,7},{4,0},{5,1},{6,2},{7,3},{8,12},{9,13},{10,... | collective-permute-start | bytes 405512 | tf_op jit(solution)/shard_map/ppermute | solution.py:293
  7.8 10.1 %collective-permute-start.2 = (bf16[528,128]{1,0:T(8,128)(2,1)}, bf16[528,128]{1,0:T(8,128)(2,1)S(1)}, u32[]{:S(2)}, u32[]{:S(2)}) collective-permute-start(bf16[528,128]{1,0:T(8,128)(2,1)} %get-tuple-element.27), channel_id=1, source_target_pairs={{0,12},{1,13},{2,14},{3,15},{4,8},{5,9},{6,10},{7,11},{8,4},{9,5},... | collective-permute-start | bytes 405512 | tf_op jit(solution)/shard_map/ppermute | solution.py:293
  10.3 16.1 %collective-permute-start.3 = (bf16[528,128]{1,0:T(8,128)(2,1)}, bf16[528,128]{1,0:T(8,128)(2,1)S(1)}, u32[]{:S(2)}, u32[]{:S(2)}) collective-permute-start(bf16[528,128]{1,0:T(8,128)(2,1)} %get-tuple-element.28), channel_id=1, source_target_pairs={{0,14},{1,15},{2,12},{3,13},{4,10},{5,11},{6,8},{7,9},{8,6},{9,7},... | collective-permute-start | bytes 405512 | tf_op jit(solution)/shard_map/ppermute | solution.py:293
  11.6 0.9 %copy-start.2 = (bf16[528,128]{1,0:T(8,128)(2,1)S(1)}, bf16[528,128]{1,0:T(8,128)(2,1)}, u32[]{:S(2)}) copy-start(bf16[528,128]{1,0:T(8,128)(2,1)} %get-tuple-element.24.refs_0_) | copy-start | bytes 405508
  12.5 0.9 %copy-start.5 = (bf16[528,128]{1,0:T(8,128)(2,1)S(1)}, bf16[528,128]{1,0:T(8,128)(2,1)}, u32[]{:S(2)}) copy-start(bf16[528,128]{1,0:T(8,128)(2,1)} %get-tuple-element.29) | copy-start | bytes 405508
  12.5 4.9 %copy-start.4 = (bf16[528,128]{1,0:T(8,128)(2,1)S(1)}, bf16[528,128]{1,0:T(8,128)(2,1)}, u32[]{:S(2)}) copy-start(bf16[528,128]{1,0:T(8,128)(2,1)} %get-tuple-element.30) | copy-start | bytes 405508
  12.5 5.4 %copy-start.3 = (bf16[528,128]{1,0:T(8,128)(2,1)S(1)}, bf16[528,128]{1,0:T(8,128)(2,1)}, u32[]{:S(2)}) copy-start(bf16[528,128]{1,0:T(8,128)(2,1)} %get-tuple-element.31) | copy-start | bytes 405508
  12.5 23.2 %collective-permute-start.7 = (bf16[1584,128]{1,0:T(8,128)(2,1)S(1)}, bf16[1584,128]{1,0:T(8,128)(2,1)S(1)}, u32[]{:S(2)}, u32[]{:S(2)}) collective-permute-start(bf16[1584,128]{1,0:T(8,128)(2,1)S(1)} %join.1.refs_0_), channel_id=1, source_target_pairs={{0,1},{1,0},{2,3},{3,2},{4,5},{5,4},{6,7},{7,6},{8,9},{9,8},{10,11... | collective-permute-start | bytes 1216520 | tf_op jit(solution)/shard_map/ppermute | solution.py:296
  13.4 19.9 %collective-permute-start.4 = (bf16[528,128]{1,0:T(8,128)(2,1)S(1)}, bf16[528,128]{1,0:T(8,128)(2,1)S(1)}, u32[]{:S(2)}, u32[]{:S(2)}) collective-permute-start(bf16[528,128]{1,0:T(8,128)(2,1)S(1)} %copy-done.5), channel_id=1, source_target_pairs={{0,8},{1,9},{2,10},{3,11},{4,12},{5,13},{6,14},{7,15},{8,0},{9,1},... | collective-permute-start | bytes 405512 | tf_op jit(solution)/shard_map/ppermute | solution.py:293
  17.3 18.4 %copy-start.1 = (s32[8]{0:T(128)S(1)}, s32[8]{0:T(128)}, u32[]{:S(2)}) copy-start(s32[8]{0:T(128)} %lengths_ref.1) | copy-start | bytes 100
  17.3 16.5 %collective-permute-start.5 = (bf16[528,128]{1,0:T(8,128)(2,1)S(1)}, bf16[528,128]{1,0:T(8,128)(2,1)S(1)}, u32[]{:S(2)}, u32[]{:S(2)}) collective-permute-start(bf16[528,128]{1,0:T(8,128)(2,1)S(1)} %copy-done.4), channel_id=1, source_target_pairs={{0,10},{1,11},{2,8},{3,9},{4,14},{5,15},{6,12},{7,13},{8,2},{9,3},... | collective-permute-start | bytes 405512 | tf_op jit(solution)/shard_map/ppermute | solution.py:293
  17.8 16.0 %collective-permute-start.6 = (bf16[528,128]{1,0:T(8,128)(2,1)S(1)}, bf16[528,128]{1,0:T(8,128)(2,1)S(1)}, u32[]{:S(2)}, u32[]{:S(2)}) collective-permute-start(bf16[528,128]{1,0:T(8,128)(2,1)S(1)} %copy-done.3), channel_id=1, source_target_pairs={{0,6},{1,7},{2,4},{3,5},{4,2},{5,3},{6,0},{7,1},{8,14},{9,15},{10,... | collective-permute-start | bytes 405512 | tf_op jit(solution)/shard_map/ppermute | solution.py:293
  26.4 8.0 %collective-permute-start.8 = (bf16[528,128]{1,0:T(8,128)(2,1)S(1)}, bf16[528,128]{1,0:T(8,128)(2,1)S(1)}, u32[]{:S(2)}, u32[]{:S(2)}) collective-permute-start(bf16[528,128]{1,0:T(8,128)(2,1)S(1)} %collective-permute-done.2.refs_1_), channel_id=1, source_target_pairs={{0,1},{1,0},{2,3},{3,2},{4,5},{5,4},{6,7},{7,6},{8,9},{9,8},{10,11... | collective-permute-start | bytes 405512 | tf_op jit(solution)/shard_map/ppermute | solution.py:296
  33.3 1.4 %collective-permute-start.9 = (bf16[528,128]{1,0:T(8,128)(2,1)S(1)}, bf16[528,128]{1,0:T(8,128)(2,1)S(1)}, u32[]{:S(2)}, u32[]{:S(2)}) collective-permute-start(bf16[528,128]{1,0:T(8,128)(2,1)S(1)} %collective-permute-done.3.refs_2_), channel_id=1, source_target_pairs={{0,1},{1,0},{2,3},{3,2},{4,5},{5,4},{6,7},{7,6},{8,9},{9,8},{10,11... | collective-permute-start | bytes 405512 | tf_op jit(solution)/shard_map/ppermute | solution.py:296
  33.8 1.4 %collective-permute-start.10 = (bf16[528,128]{1,0:T(8,128)(2,1)S(1)}, bf16[528,128]{1,0:T(8,128)(2,1)S(1)}, u32[]{:S(2)}, u32[]{:S(2)}) collective-permute-start(bf16[528,128]{1,0:T(8,128)(2,1)S(1)} %collective-permute-done.4.refs_3_), channel_id=1, source_target_pairs={{0,1},{1,0},{2,3},{3,2},{4,5},{5,4},{6,7},{7,6},{8,9},{9,8},{10,11... | collective-permute-start | bytes 405512 | tf_op jit(solution)/shard_map/ppermute | solution.py:296
  33.8 1.5 %collective-permute-start.11 = (bf16[528,128]{1,0:T(8,128)(2,1)S(1)}, bf16[528,128]{1,0:T(8,128)(2,1)S(1)}, u32[]{:S(2)}, u32[]{:S(2)}) collective-permute-start(bf16[528,128]{1,0:T(8,128)(2,1)S(1)} %collective-permute-done.5.refs_4_), channel_id=1, source_target_pairs={{0,1},{1,0},{2,3},{3,2},{4,5},{5,4},{6,7},{7,6},{8,9},{9,8},{10,11... | collective-permute-start | bytes 405512 | tf_op jit(solution)/shard_map/ppermute | solution.py:296
  34.3 1.4 %collective-permute-start.12 = (bf16[528,128]{1,0:T(8,128)(2,1)S(1)}, bf16[528,128]{1,0:T(8,128)(2,1)S(1)}, u32[]{:S(2)}, u32[]{:S(2)}) collective-permute-start(bf16[528,128]{1,0:T(8,128)(2,1)S(1)} %collective-permute-done.6.refs_5_), channel_id=1, source_target_pairs={{0,1},{1,0},{2,3},{3,2},{4,5},{5,4},{6,7},{7,6},{8,9},{9,8},{10,11... | collective-permute-start | bytes 405512 | tf_op jit(solution)/shard_map/ppermute | solution.py:296
  48.0 9.7 %collective-permute-start.13 = (bf16[400,128]{1,0:T(8,128)(2,1)S(1)}, bf16[400,128]{1,0:T(8,128)(2,1)S(1)}, u32[]{:S(2)}, u32[]{:S(2)}) collective-permute-start(bf16[400,128]{1,0:T(8,128)(2,1)S(1)} %get-tuple-element.33), channel_id=1, source_target_pairs={{0,14},{1,15},{2,12},{3,13},{4,10},{5,11},{6,8},{7,9},{8,6},{9,7},... | collective-permute-start | bytes 307208 | tf_op jit(solution)/shard_map/ppermute | solution.py:293
  52.4 7.6 %collective-permute-start.14 = (bf16[400,128]{1,0:T(8,128)(2,1)S(1)}, bf16[400,128]{1,0:T(8,128)(2,1)S(1)}, u32[]{:S(2)}, u32[]{:S(2)}) collective-permute-start(bf16[400,128]{1,0:T(8,128)(2,1)S(1)} %get-tuple-element.34), channel_id=1, source_target_pairs={{0,12},{1,13},{2,14},{3,15},{4,8},{5,9},{6,10},{7,11},{8,4},{9,5},... | collective-permute-start | bytes 307208 | tf_op jit(solution)/shard_map/ppermute | solution.py:293
  53.7 13.2 %collective-permute-start.15 = (bf16[400,128]{1,0:T(8,128)(2,1)S(1)}, bf16[400,128]{1,0:T(8,128)(2,1)S(1)}, u32[]{:S(2)}, u32[]{:S(2)}) collective-permute-start(bf16[400,128]{1,0:T(8,128)(2,1)S(1)} %get-tuple-element.35), channel_id=1, source_target_pairs={{0,10},{1,11},{2,8},{3,9},{4,14},{5,15},{6,12},{7,13},{8,2},{9,3},... | collective-permute-start | bytes 307208 | tf_op jit(solution)/shard_map/ppermute | solution.py:293
  53.7 14.7 %collective-permute-start.16 = (bf16[400,128]{1,0:T(8,128)(2,1)S(1)}, bf16[400,128]{1,0:T(8,128)(2,1)S(1)}, u32[]{:S(2)}, u32[]{:S(2)}) collective-permute-start(bf16[400,128]{1,0:T(8,128)(2,1)S(1)} %get-tuple-element.36), channel_id=1, source_target_pairs={{0,8},{1,9},{2,10},{3,11},{4,12},{5,13},{6,14},{7,15},{8,0},{9,1},... | collective-permute-start | bytes 307208 | tf_op jit(solution)/shard_map/ppermute | solution.py:293
  55.7 12.6 %collective-permute-start.17 = (bf16[400,128]{1,0:T(8,128)(2,1)S(1)}, bf16[400,128]{1,0:T(8,128)(2,1)S(1)}, u32[]{:S(2)}, u32[]{:S(2)}) collective-permute-start(bf16[400,128]{1,0:T(8,128)(2,1)S(1)} %get-tuple-element.37), channel_id=1, source_target_pairs={{0,6},{1,7},{2,4},{3,5},{4,2},{5,3},{6,0},{7,1},{8,14},{9,15},{10,... | collective-permute-start | bytes 307208 | tf_op jit(solution)/shard_map/ppermute | solution.py:293
  57.7 10.7 %collective-permute-start.18 = (bf16[400,128]{1,0:T(8,128)(2,1)S(1)}, bf16[400,128]{1,0:T(8,128)(2,1)S(1)}, u32[]{:S(2)}, u32[]{:S(2)}) collective-permute-start(bf16[400,128]{1,0:T(8,128)(2,1)S(1)} %get-tuple-element.38), channel_id=1, source_target_pairs={{0,4},{1,5},{2,6},{3,7},{4,0},{5,1},{6,2},{7,3},{8,12},{9,13},{10,... | collective-permute-start | bytes 307208 | tf_op jit(solution)/shard_map/ppermute | solution.py:293
  60.0 8.4 %copy-start = (s32[128]{0:T(128)S(1)}, s32[128]{0:T(128)}, u32[]{:S(2)}) copy-start(s32[128]{0:T(128)} %param.12) | copy-start | bytes 1540
  60.0 8.4 %collective-permute-start.19 = (bf16[400,128]{1,0:T(8,128)(2,1)S(1)}, bf16[400,128]{1,0:T(8,128)(2,1)S(1)}, u32[]{:S(2)}, u32[]{:S(2)}) collective-permute-start(bf16[400,128]{1,0:T(8,128)(2,1)S(1)} %get-tuple-element.39), channel_id=1, source_target_pairs={{0,2},{1,3},{2,0},{3,1},{4,6},{5,7},{6,4},{7,5},{8,10},{9,11},{10,... | collective-permute-start | bytes 307208 | tf_op jit(solution)/shard_map/ppermute | solution.py:293

commit v5 on v4

--- a/solution.py
+++ b/solution.py
@@ -84,13 +84,13 @@
 
 
 def chain_kernel(heads, lengths_ref, *refs):
-    given, answers, scratch = refs[:-heads - 14], refs[-heads - 14:-14], refs[-14:]
+    given, answers, scratch = refs[:-heads - 13], refs[-heads - 13:-13], refs[-13:]
     size = min(ref.shape[0] for ref in given)
     blocks = [ref.at[at:at + size] for ref in given for at in range(0, ref.shape[0], size)]
     outs = [answers[GOING.index(s)] for s in COMING]
     sources = len(blocks)
     (hi_ref, lo_ref, win_ref, at_ref, sem, down_ref, cum_ref, chain_ref, gained_ref, weighted_ref,
-     carried_ref, pulled_ref, low_ref, tail_ref) = scratch
+     pulled_ref, state_ref, tail_ref) = scratch
     rows = (size - META) // 4
     frames = rows * sources
     spans = frames // SPAN
@@ -138,7 +138,10 @@
     per = SPAN // window
     copy.wait()
 
-    def first(b):
+    def fade(b):
+        return jnp.exp(cum_ref[pl.ds(b, 1), SPAN - 1:])
+
+    def first(b, state):
         base = b * SPAN
         at = pl.ds(pl.multiple_of(base, SPAN), SPAN)
         keys = jnp.where(hi_ref[...] == b.astype(F32), lo_ref[...], 0.0)
@@ -173,18 +176,20 @@
         gained_ref[at, 0:SPAN] = (g.astype(F32) * query_gain).astype(BF16)
         gained_ref[at, SPAN:2 * SPAN] = (v.astype(F32) * key_gain).astype(BF16)
         gained_ref[at, 2 * SPAN:] = key_end
-        carried_ref[at, :] = dot(key_end, v, TN)
+        state_ref[at, :] = state.astype(BF16)
+        state = fade(b) * state + dot(key_end, v, TN)
         pulled_ref[at, :] = dot(query_start, g, TN)
         weighted_ref[at, 0:SPAN] = (dot(g, v, NT) * weight).astype(BF16)
         weighted_ref[at, SPAN:2 * SPAN] = (dot(v, g, NT) * weight_t).astype(BF16)
         weighted_ref[at, 2 * SPAN:] = (dot(k, q, NT) * weight_t).astype(BF16)
-
-    def second(b):
+        return state
+
+    def second(b, held):
         base = b * SPAN
         at = pl.ds(pl.multiple_of(base, SPAN), SPAN)
         q, k, v, g = (chain_ref[at, a * SPAN:(a + 1) * SPAN] for a in range(4))
-        state = low_ref[at, 0:SPAN]
-        grad = low_ref[at, SPAN:]
+        state = state_ref[at, :]
+        grad = held.astype(BF16)
         dq = dot(weighted_ref[at, 0:SPAN], k, NN) + dot(gained_ref[at, 0:SPAN], state, NT)
         dk = dot(weighted_ref[at, SPAN:2 * SPAN], q, NN) + dot(gained_ref[at, SPAN:2 * SPAN], grad, NT)
         dv = dot(weighted_ref[at, 2 * SPAN:], g, NN) + dot(gained_ref[at, 2 * SPAN:], grad, NN)
@@ -203,37 +208,23 @@
                 to = pl.ds(a * rows + begins[s], window)
                 outs[s][to, :] += back[s * window:(s + 1) * window, a * SPAN:(a + 1) * SPAN]
 
+        return fade(b) * held + pulled_ref[at, :]
+
     step = max(1, 128 // sources)
-
-    @pl.loop(0, spans // step)
-    def _(turn):
+    empty = jnp.zeros((SPAN, SPAN), F32)
+
+    def forward(turn, state):
         for u in range(step):
-            first(turn * step + u)
-
-    def scan(turn, held):
-        state, grad = held
-        b, c = turn, spans - 1 - turn
-        at_b = pl.ds(pl.multiple_of(b * SPAN, SPAN), SPAN)
-        at_c = pl.ds(pl.multiple_of(c * SPAN, SPAN), SPAN)
-        low_ref[at_b, 0:SPAN] = state.astype(BF16)
-        low_ref[at_c, SPAN:] = grad.astype(BF16)
-        fade_b = jnp.exp(cum_ref[pl.ds(b, 1), SPAN - 1:])
-        fade_c = jnp.exp(cum_ref[pl.ds(c, 1), SPAN - 1:])
-        return fade_b * state + carried_ref[at_b, :], fade_c * grad + pulled_ref[at_c, :]
-
-    empty = jnp.zeros((SPAN, SPAN), F32)
-
-    def scans(turn, held):
-        for u in range(4):
-            held = scan(turn * 4 + u, held)
-        return held
-
-    lax.fori_loop(0, spans // 4, scans, (empty, empty))
-
-    @pl.loop(0, spans // step)
-    def _(turn):
+            state = first(turn * step + u, state)
+        return state
+
+    def backward(turn, grad):
         for u in range(step):
-            second(turn * step + u)
+            grad = second(spans - 1 - turn * step - u, grad)
+        return grad
+
+    lax.fori_loop(0, spans // step, forward, empty)
+    lax.fori_loop(0, spans // step, backward, empty)
 
     firsts = jnp.transpose(tail_ref[...])[0:1, :]
     local = tail_ref[0:tall, :]
@@ -340,8 +331,7 @@
             pltpu.VMEM((frames, 3 * SPAN), BF16),
             pltpu.VMEM((frames, 3 * SPAN), BF16),
             pltpu.VMEM((frames, SPAN), F32),
-            pltpu.VMEM((frames, SPAN), F32),
-            pltpu.VMEM((frames, 2 * SPAN), BF16),
+            pltpu.VMEM((frames, SPAN), BF16),
             pltpu.VMEM((SPAN, SPAN), F32),
         ],
         compiler_params=pltpu.CompilerParams(vmem_limit_bytes=frames * 6 * 2**10 + 8 * 2**20),

time: 70 us -> 69.3 us (0.990)
  no operation moved by 1% of the time
where the time goes in v5:
time: 69.3 us; the launch traced here: 69.1 us
  starting transfers between devices  33.6 us (48%)
  waiting for transfers between devices  17.5 us (25%)
  Pallas kernels  15.6 us (23%)
  local copies, waits for them, and re-layouts  1.71 us (2%)
  between operations  0.71 us (1%)
    ppermute x14, starting transfers between devices, across(): return lax.ppermute(x, 'ctx', [(p, p ^ s * cores) for p in range(peers)])  33 us
    ppermute x14, waiting for transfers between devices, across(): return lax.ppermute(x, 'ctx', [(p, p ^ s * cores) for p in range(peers)])  16.2 us
    pallas_call x1, Pallas kernels, body(): pl.pallas_call(functools.partial(chain_kernel, heads), out_shape=[jax.Sha...  11.6 us
    pallas_call x1, Pallas kernels, body(): pl.pallas_call(pack_kernel, out_shape=[jax.ShapeDtypeStruct((4 * rows + M...  2.51 us
    unnamed x12, local copies, waits for them, and re-layouts  1.71 us
    pallas_call x1, Pallas kernels, body(): pl.pallas_call(unpack_kernel, out_shape=[jax.ShapeDtypeStruct((rows, widt...  1.43 us
  transfers between devices with their start and end apart: 20, of which 10 were waited for; matrix products, arithmetic and copies ran while one was open for 0% of the time, Pallas kernels for 0%

profile of v5, /device:TPU:0, one launch (start us, length us, event | category | flops | bytes accessed | tf_op | source)
XLA Modules:
  0.0 69.1 jit_solution(15598403738119712528)
XLA Ops:
  0.6 2.5 %pack.1 = (bf16[528,128]{1,0:T(8,128)(2,1)}, bf16[528,128]{1,0:T(8,128)(2,1)}, bf16[528,128]{1,0:T(8,128)(2,1)}, bf16[528,128]{1,0:T(8,128)(2,1)}, bf16[528,128]...) custom-call(s32[1]{0:T(128)} %bitcast.chip_ref, ...), custom_call_target="tpu_custom_call" | custom-call | tf_op jit(solution)/shard_map/pack/pallas_call | solution.py:289
  3.2 3.0 %collective-permute-start = (bf16[528,128]{1,0:T(8,128)(2,1)}, bf16[528,128]{1,0:T(8,128)(2,1)S(1)}, u32[]{:S(2)}, u32[]{:S(2)}) collective-permute-start(bf16[528,128]{1,0:T(8,128)(2,1)} %get-tuple-element.25), channel_id=1, source_target_pairs={{0,2},{1,3},{2,0},{3,1},{4,6},{5,7},{6,4},{7,5},{8,10},{9,11},{10,... | collective-permute-start | bytes 405512 | tf_op jit(solution)/shard_map/ppermute | solution.py:284
  6.2 1.6 %collective-permute-start.1 = (bf16[528,128]{1,0:T(8,128)(2,1)}, bf16[528,128]{1,0:T(8,128)(2,1)S(1)}, u32[]{:S(2)}, u32[]{:S(2)}) collective-permute-start(bf16[528,128]{1,0:T(8,128)(2,1)} %get-tuple-element.26), channel_id=1, source_target_pairs={{0,4},{1,5},{2,6},{3,7},{4,0},{5,1},{6,2},{7,3},{8,12},{9,13},{10,... | collective-permute-start | bytes 405512 | tf_op jit(solution)/shard_map/ppermute | solution.py:284
  7.8 2.5 %collective-permute-start.2 = (bf16[528,128]{1,0:T(8,128)(2,1)}, bf16[528,128]{1,0:T(8,128)(2,1)S(1)}, u32[]{:S(2)}, u32[]{:S(2)}) collective-permute-start(bf16[528,128]{1,0:T(8,128)(2,1)} %get-tuple-element.27), channel_id=1, source_target_pairs={{0,12},{1,13},{2,14},{3,15},{4,8},{5,9},{6,10},{7,11},{8,4},{9,5},... | collective-permute-start | bytes 405512 | tf_op jit(solution)/shard_map/ppermute | solution.py:284
  10.3 1.3 %collective-permute-start.3 = (bf16[528,128]{1,0:T(8,128)(2,1)}, bf16[528,128]{1,0:T(8,128)(2,1)S(1)}, u32[]{:S(2)}, u32[]{:S(2)}) collective-permute-start(bf16[528,128]{1,0:T(8,128)(2,1)} %get-tuple-element.28), channel_id=1, source_target_pairs={{0,14},{1,15},{2,12},{3,13},{4,10},{5,11},{6,8},{7,9},{8,6},{9,7},... | collective-permute-start | bytes 405512 | tf_op jit(solution)/shard_map/ppermute | solution.py:284
  11.5 0.0 collective-permute-done.refs_1_
  11.5 0.0 collective-permute-done.1.refs_2_
  11.6 0.0 copy-start.2
  11.6 0.9 %copy-done.2 = bf16[528,128]{1,0:T(8,128)(2,1)S(1)} copy-done((bf16[528,128]{1,0:T(8,128)(2,1)S(1)}, bf16[528,128]{1,0:T(8,128)(2,1)}, u32[]{:S(2)}) %copy-start.2) | copy-done | bytes 135192
  12.5 0.0 copy-start.5
  12.5 0.0 copy-start.4
  12.5 0.0 copy-start.3
  12.5 0.1 collective-permute-start.7
  12.6 0.8 %copy-done.5 = bf16[528,128]{1,0:T(8,128)(2,1)S(1)} copy-done((bf16[528,128]{1,0:T(8,128)(2,1)S(1)}, bf16[528,128]{1,0:T(8,128)(2,1)}, u32[]{:S(2)}) %copy-start.5) | copy-done | bytes 135192
  13.4 4.0 %collective-permute-start.4 = (bf16[528,128]{1,0:T(8,128)(2,1)S(1)}, bf16[528,128]{1,0:T(8,128)(2,1)S(1)}, u32[]{:S(2)}, u32[]{:S(2)}) collective-permute-start(bf16[528,128]{1,0:T(8,128)(2,1)S(1)} %copy-done.5), channel_id=1, source_target_pairs={{0,8},{1,9},{2,10},{3,11},{4,12},{5,13},{6,14},{7,15},{8,0},{9,1},... | collective-permute-start | bytes 405512 | tf_op jit(solution)/shard_map/ppermute | solution.py:284
  17.3 0.0 copy-done.4
  17.3 0.0 copy-start.1
  17.3 0.0 collective-permute-start.5
  17.3 0.5 collective-permute-done.2.refs_1_
  17.8 0.0 copy-done.3
  17.8 8.5 %collective-permute-start.6 = (bf16[528,128]{1,0:T(8,128)(2,1)S(1)}, bf16[528,128]{1,0:T(8,128)(2,1)S(1)}, u32[]{:S(2)}, u32[]{:S(2)}) collective-permute-start(bf16[528,128]{1,0:T(8,128)(2,1)S(1)} %copy-done.3), channel_id=1, source_target_pairs={{0,6},{1,7},{2,4},{3,5},{4,2},{5,3},{6,0},{7,1},{8,14},{9,15},{10,... | collective-permute-start | bytes 405512 | tf_op jit(solution)/shard_map/ppermute | solution.py:284
  26.4 0.0 collective-permute-done.3.refs_2_
  26.4 0.0 collective-permute-start.8
  26.4 6.9 %collective-permute-done.4.refs_3_ = bf16[528,128]{1,0:T(8,128)(2,1)S(1)} collective-permute-done((bf16[528,128]{1,0:T(8,128)(2,1)S(1)}, bf16[528,128]{1,0:T(8,128)(2,1)S(1)}, u32[]{:S(2)}, u32[]{:S(2)}) %collective-permute-start.4) | collective-permute-done | bytes 135200 | tf_op jit(solution)/shard_map/ppermute | solution.py:284
  33.3 0.0 collective-permute-start.9
  33.3 0.6 collective-permute-done.5.refs_4_
  33.8 0.0 collective-permute-start.10
  33.8 0.0 collective-permute-done.6.refs_5_
  33.8 0.5 collective-permute-start.11
  34.3 0.0 collective-permute-done.8.refs_7_
  34.3 0.1 collective-permute-start.12
  34.4 0.2 collective-permute-done.9.refs_8_
  34.6 0.6 collective-permute-done.10.refs_9_
  35.2 0.2 collective-permute-done.11.refs_10_
  35.4 0.3 collective-permute-done.12.refs_11_
  35.7 0.0 collective-permute-done.7.refs_6_
  35.7 0.0 copy-done.1
  35.7 11.6 %chain.1 = (bf16[400,128]{1,0:T(8,128)(2,1)S(1)}, bf16[400,128]{1,0:T(8,128)(2,1)S(1)}, bf16[400,128]{1,0:T(8,128)(2,1)S(1)}, bf16[400,128]{1,0:T(8,128)(2,1)S(1...) custom-call(s32[8]{0:T(128)S(1)} %copy-done.1, ...), custom_call_target="tpu_custom_call" | custom-call | tf_op jit(solution)/shard_map/chain/pallas_call | solution.py:317
  47.3 4.4 %collective-permute-start.13 = (bf16[400,128]{1,0:T(8,128)(2,1)S(1)}, bf16[400,128]{1,0:T(8,128)(2,1)S(1)}, u32[]{:S(2)}, u32[]{:S(2)}) collective-permute-start(bf16[400,128]{1,0:T(8,128)(2,1)S(1)} %get-tuple-element.33), channel_id=1, source_target_pairs={{0,14},{1,15},{2,12},{3,13},{4,10},{5,11},{6,8},{7,9},{8,6},{9,7},... | collective-permute-start | bytes 307208 | tf_op jit(solution)/shard_map/ppermute | solution.py:284
  51.7 1.3 %collective-permute-start.14 = (bf16[400,128]{1,0:T(8,128)(2,1)S(1)}, bf16[400,128]{1,0:T(8,128)(2,1)S(1)}, u32[]{:S(2)}, u32[]{:S(2)}) collective-permute-start(bf16[400,128]{1,0:T(8,128)(2,1)S(1)} %get-tuple-element.34), channel_id=1, source_target_pairs={{0,12},{1,13},{2,14},{3,15},{4,8},{5,9},{6,10},{7,11},{8,4},{9,5},... | collective-permute-start | bytes 307208 | tf_op jit(solution)/shard_map/ppermute | solution.py:284
  53.0 0.0 collective-permute-start.15
  53.0 2.0 %collective-permute-start.16 = (bf16[400,128]{1,0:T(8,128)(2,1)S(1)}, bf16[400,128]{1,0:T(8,128)(2,1)S(1)}, u32[]{:S(2)}, u32[]{:S(2)}) collective-permute-start(bf16[400,128]{1,0:T(8,128)(2,1)S(1)} %get-tuple-element.36), channel_id=1, source_target_pairs={{0,8},{1,9},{2,10},{3,11},{4,12},{5,13},{6,14},{7,15},{8,0},{9,1},... | collective-permute-start | bytes 307208 | tf_op jit(solution)/shard_map/ppermute | solution.py:284
  55.0 2.0 %collective-permute-start.17 = (bf16[400,128]{1,0:T(8,128)(2,1)S(1)}, bf16[400,128]{1,0:T(8,128)(2,1)S(1)}, u32[]{:S(2)}, u32[]{:S(2)}) collective-permute-start(bf16[400,128]{1,0:T(8,128)(2,1)S(1)} %get-tuple-element.37), channel_id=1, source_target_pairs={{0,6},{1,7},{2,4},{3,5},{4,2},{5,3},{6,0},{7,1},{8,14},{9,15},{10,... | collective-permute-start | bytes 307208 | tf_op jit(solution)/shard_map/ppermute | solution.py:284
  57.0 0.0 collective-permute-done.13.refs_1_
  57.0 1.8 %collective-permute-start.18 = (bf16[400,128]{1,0:T(8,128)(2,1)S(1)}, bf16[400,128]{1,0:T(8,128)(2,1)S(1)}, u32[]{:S(2)}, u32[]{:S(2)}) collective-permute-start(bf16[400,128]{1,0:T(8,128)(2,1)S(1)} %get-tuple-element.38), channel_id=1, source_target_pairs={{0,4},{1,5},{2,6},{3,7},{4,0},{5,1},{6,2},{7,3},{8,12},{9,13},{10,... | collective-permute-start | bytes 307208 | tf_op jit(solution)/shard_map/ppermute | solution.py:284
  58.8 0.5 collective-permute-done.14.refs_2_
  59.3 0.0 copy-start
  59.3 0.6 collective-permute-start.19
  59.9 6.3 %collective-permute-done.15.refs_3_ = bf16[400,128]{1,0:T(8,128)(2,1)S(1)} collective-permute-done((bf16[400,128]{1,0:T(8,128)(2,1)S(1)}, bf16[400,128]{1,0:T(8,128)(2,1)S(1)}, u32[]{:S(2)}, u32[]{:S(2)}) %collective-permute-start.15) | collective-permute-done | bytes 102432 | tf_op jit(solution)/shard_map/ppermute | solution.py:284
  66.2 1.5 %collective-permute-done.16.refs_4_ = bf16[400,128]{1,0:T(8,128)(2,1)S(1)} collective-permute-done((bf16[400,128]{1,0:T(8,128)(2,1)S(1)}, bf16[400,128]{1,0:T(8,128)(2,1)S(1)}, u32[]{:S(2)}, u32[]{:S(2)}) %collective-permute-start.16) | collective-permute-done | bytes 102432 | tf_op jit(solution)/shard_map/ppermute | solution.py:284
  67.7 0.0 collective-permute-done.17.refs_5_
  67.7 0.0 collective-permute-done.18.refs_6_
  67.7 0.0 collective-permute-done.19.refs_7_
  67.7 0.0 copy-done
  67.7 1.4 %unpack.1 = (bf16[128,1024]{1,0:T(8,128)(2,1)}, bf16[128,1024]{1,0:T(8,128)(2,1)}, bf16[128,1024]{1,0:T(8,128)(2,1)}, bf16[8,128]{1,0:T(8,128)(2,1)}) custom-call(s32[1]{0:T(128)} %bitcast.chip_ref, s32[1,128]{1,0:T(1,128)S(1)} %bitcast.5, bf16[400,128]{1,0:T(8,128)(2,1)S(1)} %get-tuple-element.32.refs_0_, ...), custom_call_target="tpu_custom_call" | custom-call | tf_op jit(solution)/shard_map/unpack/pallas_call | solution.py:342
  (1 shorter events, 0.0 us)
Async XLA Ops:
  3.2 8.4 %collective-permute-start = (bf16[528,128]{1,0:T(8,128)(2,1)}, bf16[528,128]{1,0:T(8,128)(2,1)S(1)}, u32[]{:S(2)}, u32[]{:S(2)}) collective-permute-start(bf16[528,128]{1,0:T(8,128)(2,1)} %get-tuple-element.25), channel_id=1, source_target_pairs={{0,2},{1,3},{2,0},{3,1},{4,6},{5,7},{6,4},{7,5},{8,10},{9,11},{10,... | collective-permute-start | bytes 405512 | tf_op jit(solution)/shard_map/ppermute | solution.py:284
  6.2 5.4 %collective-permute-start.1 = (bf16[528,128]{1,0:T(8,128)(2,1)}, bf16[528,128]{1,0:T(8,128)(2,1)S(1)}, u32[]{:S(2)}, u32[]{:S(2)}) collective-permute-start(bf16[528,128]{1,0:T(8,128)(2,1)} %get-tuple-element.26), channel_id=1, source_target_pairs={{0,4},{1,5},{2,6},{3,7},{4,0},{5,1},{6,2},{7,3},{8,12},{9,13},{10,... | collective-permute-start | bytes 405512 | tf_op jit(solution)/shard_map/ppermute | solution.py:284
  7.8 10.1 %collective-permute-start.2 = (bf16[528,128]{1,0:T(8,128)(2,1)}, bf16[528,128]{1,0:T(8,128)(2,1)S(1)}, u32[]{:S(2)}, u32[]{:S(2)}) collective-permute-start(bf16[528,128]{1,0:T(8,128)(2,1)} %get-tuple-element.27), channel_id=1, source_target_pairs={{0,12},{1,13},{2,14},{3,15},{4,8},{5,9},{6,10},{7,11},{8,4},{9,5},... | collective-permute-start | bytes 405512 | tf_op jit(solution)/shard_map/ppermute | solution.py:284
  10.3 16.1 %collective-permute-start.3 = (bf16[528,128]{1,0:T(8,128)(2,1)}, bf16[528,128]{1,0:T(8,128)(2,1)S(1)}, u32[]{:S(2)}, u32[]{:S(2)}) collective-permute-start(bf16[528,128]{1,0:T(8,128)(2,1)} %get-tuple-element.28), channel_id=1, source_target_pairs={{0,14},{1,15},{2,12},{3,13},{4,10},{5,11},{6,8},{7,9},{8,6},{9,7},... | collective-permute-start | bytes 405512 | tf_op jit(solution)/shard_map/ppermute | solution.py:284
  11.6 0.9 %copy-start.2 = (bf16[528,128]{1,0:T(8,128)(2,1)S(1)}, bf16[528,128]{1,0:T(8,128)(2,1)}, u32[]{:S(2)}) copy-start(bf16[528,128]{1,0:T(8,128)(2,1)} %get-tuple-element.24.refs_0_) | copy-start | bytes 405508
  12.5 0.9 %copy-start.5 = (bf16[528,128]{1,0:T(8,128)(2,1)S(1)}, bf16[528,128]{1,0:T(8,128)(2,1)}, u32[]{:S(2)}) copy-start(bf16[528,128]{1,0:T(8,128)(2,1)} %get-tuple-element.29) | copy-start | bytes 405508
  12.5 4.9 %copy-start.4 = (bf16[528,128]{1,0:T(8,128)(2,1)S(1)}, bf16[528,128]{1,0:T(8,128)(2,1)}, u32[]{:S(2)}) copy-start(bf16[528,128]{1,0:T(8,128)(2,1)} %get-tuple-element.30) | copy-start | bytes 405508
  12.5 5.4 %copy-start.3 = (bf16[528,128]{1,0:T(8,128)(2,1)S(1)}, bf16[528,128]{1,0:T(8,128)(2,1)}, u32[]{:S(2)}) copy-start(bf16[528,128]{1,0:T(8,128)(2,1)} %get-tuple-element.31) | copy-start | bytes 405508
  12.5 23.2 %collective-permute-start.7 = (bf16[1584,128]{1,0:T(8,128)(2,1)S(1)}, bf16[1584,128]{1,0:T(8,128)(2,1)S(1)}, u32[]{:S(2)}, u32[]{:S(2)}) collective-permute-start(bf16[1584,128]{1,0:T(8,128)(2,1)S(1)} %join.1.refs_0_), channel_id=1, source_target_pairs={{0,1},{1,0},{2,3},{3,2},{4,5},{5,4},{6,7},{7,6},{8,9},{9,8},{10,11... | collective-permute-start | bytes 1216520 | tf_op jit(solution)/shard_map/ppermute | solution.py:287
  13.4 19.9 %collective-permute-start.4 = (bf16[528,128]{1,0:T(8,128)(2,1)S(1)}, bf16[528,128]{1,0:T(8,128)(2,1)S(1)}, u32[]{:S(2)}, u32[]{:S(2)}) collective-permute-start(bf16[528,128]{1,0:T(8,128)(2,1)S(1)} %copy-done.5), channel_id=1, source_target_pairs={{0,8},{1,9},{2,10},{3,11},{4,12},{5,13},{6,14},{7,15},{8,0},{9,1},... | collective-permute-start | bytes 405512 | tf_op jit(solution)/shard_map/ppermute | solution.py:284
  17.3 18.4 %copy-start.1 = (s32[8]{0:T(128)S(1)}, s32[8]{0:T(128)}, u32[]{:S(2)}) copy-start(s32[8]{0:T(128)} %lengths_ref.1) | copy-start | bytes 100
  17.3 16.5 %collective-permute-start.5 = (bf16[528,128]{1,0:T(8,128)(2,1)S(1)}, bf16[528,128]{1,0:T(8,128)(2,1)S(1)}, u32[]{:S(2)}, u32[]{:S(2)}) collective-permute-start(bf16[528,128]{1,0:T(8,128)(2,1)S(1)} %copy-done.4), channel_id=1, source_target_pairs={{0,10},{1,11},{2,8},{3,9},{4,14},{5,15},{6,12},{7,13},{8,2},{9,3},... | collective-permute-start | bytes 405512 | tf_op jit(solution)/shard_map/ppermute | solution.py:284
  17.8 16.0 %collective-permute-start.6 = (bf16[528,128]{1,0:T(8,128)(2,1)S(1)}, bf16[528,128]{1,0:T(8,128)(2,1)S(1)}, u32[]{:S(2)}, u32[]{:S(2)}) collective-permute-start(bf16[528,128]{1,0:T(8,128)(2,1)S(1)} %copy-done.3), channel_id=1, source_target_pairs={{0,6},{1,7},{2,4},{3,5},{4,2},{5,3},{6,0},{7,1},{8,14},{9,15},{10,... | collective-permute-start | bytes 405512 | tf_op jit(solution)/shard_map/ppermute | solution.py:284
  26.4 8.0 %collective-permute-start.8 = (bf16[528,128]{1,0:T(8,128)(2,1)S(1)}, bf16[528,128]{1,0:T(8,128)(2,1)S(1)}, u32[]{:S(2)}, u32[]{:S(2)}) collective-permute-start(bf16[528,128]{1,0:T(8,128)(2,1)S(1)} %collective-permute-done.2.refs_1_), channel_id=1, source_target_pairs={{0,1},{1,0},{2,3},{3,2},{4,5},{5,4},{6,7},{7,6},{8,9},{9,8},{10,11... | collective-permute-start | bytes 405512 | tf_op jit(solution)/shard_map/ppermute | solution.py:287
  33.3 1.4 %collective-permute-start.9 = (bf16[528,128]{1,0:T(8,128)(2,1)S(1)}, bf16[528,128]{1,0:T(8,128)(2,1)S(1)}, u32[]{:S(2)}, u32[]{:S(2)}) collective-permute-start(bf16[528,128]{1,0:T(8,128)(2,1)S(1)} %collective-permute-done.3.refs_2_), channel_id=1, source_target_pairs={{0,1},{1,0},{2,3},{3,2},{4,5},{5,4},{6,7},{7,6},{8,9},{9,8},{10,11... | collective-permute-start | bytes 405512 | tf_op jit(solution)/shard_map/ppermute | solution.py:287
  33.8 1.4 %collective-permute-start.10 = (bf16[528,128]{1,0:T(8,128)(2,1)S(1)}, bf16[528,128]{1,0:T(8,128)(2,1)S(1)}, u32[]{:S(2)}, u32[]{:S(2)}) collective-permute-start(bf16[528,128]{1,0:T(8,128)(2,1)S(1)} %collective-permute-done.4.refs_3_), channel_id=1, source_target_pairs={{0,1},{1,0},{2,3},{3,2},{4,5},{5,4},{6,7},{7,6},{8,9},{9,8},{10,11... | collective-permute-start | bytes 405512 | tf_op jit(solution)/shard_map/ppermute | solution.py:287
  33.8 1.5 %collective-permute-start.11 = (bf16[528,128]{1,0:T(8,128)(2,1)S(1)}, bf16[528,128]{1,0:T(8,128)(2,1)S(1)}, u32[]{:S(2)}, u32[]{:S(2)}) collective-permute-start(bf16[528,128]{1,0:T(8,128)(2,1)S(1)} %collective-permute-done.5.refs_4_), channel_id=1, source_target_pairs={{0,1},{1,0},{2,3},{3,2},{4,5},{5,4},{6,7},{7,6},{8,9},{9,8},{10,11... | collective-permute-start | bytes 405512 | tf_op jit(solution)/shard_map/ppermute | solution.py:287
  34.3 1.4 %collective-permute-start.12 = (bf16[528,128]{1,0:T(8,128)(2,1)S(1)}, bf16[528,128]{1,0:T(8,128)(2,1)S(1)}, u32[]{:S(2)}, u32[]{:S(2)}) collective-permute-start(bf16[528,128]{1,0:T(8,128)(2,1)S(1)} %collective-permute-done.6.refs_5_), channel_id=1, source_target_pairs={{0,1},{1,0},{2,3},{3,2},{4,5},{5,4},{6,7},{7,6},{8,9},{9,8},{10,11... | collective-permute-start | bytes 405512 | tf_op jit(solution)/shard_map/ppermute | solution.py:287
  47.3 9.7 %collective-permute-start.13 = (bf16[400,128]{1,0:T(8,128)(2,1)S(1)}, bf16[400,128]{1,0:T(8,128)(2,1)S(1)}, u32[]{:S(2)}, u32[]{:S(2)}) collective-permute-start(bf16[400,128]{1,0:T(8,128)(2,1)S(1)} %get-tuple-element.33), channel_id=1, source_target_pairs={{0,14},{1,15},{2,12},{3,13},{4,10},{5,11},{6,8},{7,9},{8,6},{9,7},... | collective-permute-start | bytes 307208 | tf_op jit(solution)/shard_map/ppermute | solution.py:284
  51.7 7.6 %collective-permute-start.14 = (bf16[400,128]{1,0:T(8,128)(2,1)S(1)}, bf16[400,128]{1,0:T(8,128)(2,1)S(1)}, u32[]{:S(2)}, u32[]{:S(2)}) collective-permute-start(bf16[400,128]{1,0:T(8,128)(2,1)S(1)} %get-tuple-element.34), channel_id=1, source_target_pairs={{0,12},{1,13},{2,14},{3,15},{4,8},{5,9},{6,10},{7,11},{8,4},{9,5},... | collective-permute-start | bytes 307208 | tf_op jit(solution)/shard_map/ppermute | solution.py:284
  53.0 13.2 %collective-permute-start.15 = (bf16[400,128]{1,0:T(8,128)(2,1)S(1)}, bf16[400,128]{1,0:T(8,128)(2,1)S(1)}, u32[]{:S(2)}, u32[]{:S(2)}) collective-permute-start(bf16[400,128]{1,0:T(8,128)(2,1)S(1)} %get-tuple-element.35), channel_id=1, source_target_pairs={{0,10},{1,11},{2,8},{3,9},{4,14},{5,15},{6,12},{7,13},{8,2},{9,3},... | collective-permute-start | bytes 307208 | tf_op jit(solution)/shard_map/ppermute | solution.py:284
  53.0 14.7 %collective-permute-start.16 = (bf16[400,128]{1,0:T(8,128)(2,1)S(1)}, bf16[400,128]{1,0:T(8,128)(2,1)S(1)}, u32[]{:S(2)}, u32[]{:S(2)}) collective-permute-start(bf16[400,128]{1,0:T(8,128)(2,1)S(1)} %get-tuple-element.36), channel_id=1, source_target_pairs={{0,8},{1,9},{2,10},{3,11},{4,12},{5,13},{6,14},{7,15},{8,0},{9,1},... | collective-permute-start | bytes 307208 | tf_op jit(solution)/shard_map/ppermute | solution.py:284
  55.0 12.6 %collective-permute-start.17 = (bf16[400,128]{1,0:T(8,128)(2,1)S(1)}, bf16[400,128]{1,0:T(8,128)(2,1)S(1)}, u32[]{:S(2)}, u32[]{:S(2)}) collective-permute-start(bf16[400,128]{1,0:T(8,128)(2,1)S(1)} %get-tuple-element.37), channel_id=1, source_target_pairs={{0,6},{1,7},{2,4},{3,5},{4,2},{5,3},{6,0},{7,1},{8,14},{9,15},{10,... | collective-permute-start | bytes 307208 | tf_op jit(solution)/shard_map/ppermute | solution.py:284
  57.0 10.7 %collective-permute-start.18 = (bf16[400,128]{1,0:T(8,128)(2,1)S(1)}, bf16[400,128]{1,0:T(8,128)(2,1)S(1)}, u32[]{:S(2)}, u32[]{:S(2)}) collective-permute-start(bf16[400,128]{1,0:T(8,128)(2,1)S(1)} %get-tuple-element.38), channel_id=1, source_target_pairs={{0,4},{1,5},{2,6},{3,7},{4,0},{5,1},{6,2},{7,3},{8,12},{9,13},{10,... | collective-permute-start | bytes 307208 | tf_op jit(solution)/shard_map/ppermute | solution.py:284
  59.3 8.4 %copy-start = (s32[128]{0:T(128)S(1)}, s32[128]{0:T(128)}, u32[]{:S(2)}) copy-start(s32[128]{0:T(128)} %param.12) | copy-start | bytes 1540
  59.3 8.4 %collective-permute-start.19 = (bf16[400,128]{1,0:T(8,128)(2,1)S(1)}, bf16[400,128]{1,0:T(8,128)(2,1)S(1)}, u32[]{:S(2)}, u32[]{:S(2)}) collective-permute-start(bf16[400,128]{1,0:T(8,128)(2,1)S(1)} %get-tuple-element.39), channel_id=1, source_target_pairs={{0,2},{1,3},{2,0},{3,1},{4,6},{5,7},{6,4},{7,5},{8,10},{9,11},{10,... | collective-permute-start | bytes 307208 | tf_op jit(solution)/shard_map/ppermute | solution.py:284

commit v6 on v5

--- a/solution.py
+++ b/solution.py
@@ -152,7 +152,7 @@
                 row = None
                 for n in range(n1, n1 + per):
                     begin = pl.multiple_of(at_ref[n, b], 16)
-                    turned = pltpu.roll(keys[n:n + 1], (n - n1) * window + SPAN - begin, 1)
+                    turned = pltpu.roll(keys[n:n + 1], ((n - n1) * window + SPAN - begin) & (SPAN - 1), 1)
                     row = turned if row is None else row + turned
                     found.append(jnp.concatenate(
                         [blocks[n][pl.ds(a * rows + begin, window), :] for a in range(4)], axis=1))
@@ -168,7 +168,6 @@
         last = cum_j[:, SPAN - 1:]
         gap = cum_i - cum_j
         weight = jnp.where(row_i >= col_j, jnp.exp(jnp.minimum(gap, 0.0)), 0.0)
-        weight_t = jnp.where(row_i <= col_j, jnp.exp(jnp.minimum(-gap, 0.0)), 0.0)
         query_gain = jnp.exp(cum_i)
         key_gain = jnp.exp(last - cum_i)
         key_end = (k.astype(F32) * key_gain).astype(BF16)
@@ -180,8 +179,7 @@
         state = fade(b) * state + dot(key_end, v, TN)
         pulled_ref[at, :] = dot(query_start, g, TN)
         weighted_ref[at, 0:SPAN] = (dot(g, v, NT) * weight).astype(BF16)
-        weighted_ref[at, SPAN:2 * SPAN] = (dot(v, g, NT) * weight_t).astype(BF16)
-        weighted_ref[at, 2 * SPAN:] = (dot(k, q, NT) * weight_t).astype(BF16)
+        weighted_ref[at, SPAN:] = (dot(q, k, NT) * weight).astype(BF16)
         return state
 
     def second(b, held):
@@ -191,8 +189,8 @@
         state = state_ref[at, :]
         grad = held.astype(BF16)
         dq = dot(weighted_ref[at, 0:SPAN], k, NN) + dot(gained_ref[at, 0:SPAN], state, NT)
-        dk = dot(weighted_ref[at, SPAN:2 * SPAN], q, NN) + dot(gained_ref[at, SPAN:2 * SPAN], grad, NT)
-        dv = dot(weighted_ref[at, 2 * SPAN:], g, NN) + dot(gained_ref[at, 2 * SPAN:], grad, NN)
+        dk = dot(weighted_ref[at, 0:SPAN], q, TN) + dot(gained_ref[at, SPAN:2 * SPAN], grad, NT)
+        dv = dot(weighted_ref[at, SPAN:], g, TN) + dot(gained_ref[at, 2 * SPAN:], grad, NN)
         term = jnp.sum(q.astype(F32) * dq - k.astype(F32) * dk, axis=1, keepdims=True)
         seg_i = segments(base + row_i, starts)
         seg_j = segments(base + iota((1, SPAN), 1), starts)
@@ -210,7 +208,7 @@
 
         return fade(b) * held + pulled_ref[at, :]
 
-    step = max(1, 128 // sources)
+    step = max(1, 256 // sources)
     empty = jnp.zeros((SPAN, SPAN), F32)
 
     def forward(turn, state):
@@ -329,7 +327,7 @@
             pltpu.VMEM((tall, SPAN), F32),
             pltpu.VMEM((frames, 4 * SPAN), BF16),
             pltpu.VMEM((frames, 3 * SPAN), BF16),
-            pltpu.VMEM((frames, 3 * SPAN), BF16),
+            pltpu.VMEM((frames, 2 * SPAN), BF16),
             pltpu.VMEM((frames, SPAN), F32),
             pltpu.VMEM((frames, SPAN), BF16),
             pltpu.VMEM((SPAN, SPAN), F32),

time: 69.3 us -> 69 us (level)
  no operation moved by 1% of the time
where the time goes in v6:
time: 69 us; the launch traced here: 68.8 us
  starting transfers between devices  33.6 us (49%)
  waiting for transfers between devices  17.5 us (25%)
  Pallas kernels  15.3 us (22%)
  local copies, waits for them, and re-layouts  1.71 us (2%)
  between operations  0.71 us (1%)
    ppermute x14, starting transfers between devices, across(): return lax.ppermute(x, 'ctx', [(p, p ^ s * cores) for p in range(peers)])  32.9 us
    ppermute x14, waiting for transfers between devices, across(): return lax.ppermute(x, 'ctx', [(p, p ^ s * cores) for p in range(peers)])  16.2 us
    pallas_call x1, Pallas kernels, body(): pl.pallas_call(functools.partial(chain_kernel, heads), out_shape=[jax.Sha...  11.3 us
    pallas_call x1, Pallas kernels, body(): pl.pallas_call(pack_kernel, out_shape=[jax.ShapeDtypeStruct((4 * rows + M...  2.51 us
    unnamed x12, local copies, waits for them, and re-layouts  1.71 us
    pallas_call x1, Pallas kernels, body(): pl.pallas_call(unpack_kernel, out_shape=[jax.ShapeDtypeStruct((rows, widt...  1.43 us
  transfers between devices with their start and end apart: 20, of which 10 were waited for; matrix products, arithmetic and copies ran while one was open for 0% of the time, Pallas kernels for 0%

profile of v6, /device:TPU:0, one launch (start us, length us, event | category | flops | bytes accessed | tf_op | source)
XLA Modules:
  0.0 68.8 jit_solution(18176144577278903172)
XLA Ops:
  0.6 2.5 %pack.1 = (bf16[528,128]{1,0:T(8,128)(2,1)}, bf16[528,128]{1,0:T(8,128)(2,1)}, bf16[528,128]{1,0:T(8,128)(2,1)}, bf16[528,128]{1,0:T(8,128)(2,1)}, bf16[528,128]...) custom-call(s32[1]{0:T(128)} %bitcast.chip_ref, ...), custom_call_target="tpu_custom_call" | custom-call | tf_op jit(solution)/shard_map/pack/pallas_call | solution.py:287
  3.2 3.0 %collective-permute-start = (bf16[528,128]{1,0:T(8,128)(2,1)}, bf16[528,128]{1,0:T(8,128)(2,1)S(1)}, u32[]{:S(2)}, u32[]{:S(2)}) collective-permute-start(bf16[528,128]{1,0:T(8,128)(2,1)} %get-tuple-element.25), channel_id=1, source_target_pairs={{0,2},{1,3},{2,0},{3,1},{4,6},{5,7},{6,4},{7,5},{8,10},{9,11},{10,... | collective-permute-start | bytes 405512 | tf_op jit(solution)/shard_map/ppermute | solution.py:282
  6.2 1.6 %collective-permute-start.1 = (bf16[528,128]{1,0:T(8,128)(2,1)}, bf16[528,128]{1,0:T(8,128)(2,1)S(1)}, u32[]{:S(2)}, u32[]{:S(2)}) collective-permute-start(bf16[528,128]{1,0:T(8,128)(2,1)} %get-tuple-element.26), channel_id=1, source_target_pairs={{0,4},{1,5},{2,6},{3,7},{4,0},{5,1},{6,2},{7,3},{8,12},{9,13},{10,... | collective-permute-start | bytes 405512 | tf_op jit(solution)/shard_map/ppermute | solution.py:282
  7.8 2.5 %collective-permute-start.2 = (bf16[528,128]{1,0:T(8,128)(2,1)}, bf16[528,128]{1,0:T(8,128)(2,1)S(1)}, u32[]{:S(2)}, u32[]{:S(2)}) collective-permute-start(bf16[528,128]{1,0:T(8,128)(2,1)} %get-tuple-element.27), channel_id=1, source_target_pairs={{0,12},{1,13},{2,14},{3,15},{4,8},{5,9},{6,10},{7,11},{8,4},{9,5},... | collective-permute-start | bytes 405512 | tf_op jit(solution)/shard_map/ppermute | solution.py:282
  10.3 1.3 %collective-permute-start.3 = (bf16[528,128]{1,0:T(8,128)(2,1)}, bf16[528,128]{1,0:T(8,128)(2,1)S(1)}, u32[]{:S(2)}, u32[]{:S(2)}) collective-permute-start(bf16[528,128]{1,0:T(8,128)(2,1)} %get-tuple-element.28), channel_id=1, source_target_pairs={{0,14},{1,15},{2,12},{3,13},{4,10},{5,11},{6,8},{7,9},{8,6},{9,7},... | collective-permute-start | bytes 405512 | tf_op jit(solution)/shard_map/ppermute | solution.py:282
  11.5 0.0 collective-permute-done.refs_1_
  11.5 0.0 collective-permute-done.1.refs_2_
  11.6 0.0 copy-start.2
  11.6 0.9 %copy-done.2 = bf16[528,128]{1,0:T(8,128)(2,1)S(1)} copy-done((bf16[528,128]{1,0:T(8,128)(2,1)S(1)}, bf16[528,128]{1,0:T(8,128)(2,1)}, u32[]{:S(2)}) %copy-start.2) | copy-done | bytes 135192
  12.5 0.0 copy-start.5
  12.5 0.0 copy-start.4
  12.5 0.0 copy-start.3
  12.5 0.1 collective-permute-start.7
  12.6 0.8 %copy-done.5 = bf16[528,128]{1,0:T(8,128)(2,1)S(1)} copy-done((bf16[528,128]{1,0:T(8,128)(2,1)S(1)}, bf16[528,128]{1,0:T(8,128)(2,1)}, u32[]{:S(2)}) %copy-start.5) | copy-done | bytes 135192
  13.4 4.0 %collective-permute-start.4 = (bf16[528,128]{1,0:T(8,128)(2,1)S(1)}, bf16[528,128]{1,0:T(8,128)(2,1)S(1)}, u32[]{:S(2)}, u32[]{:S(2)}) collective-permute-start(bf16[528,128]{1,0:T(8,128)(2,1)S(1)} %copy-done.5), channel_id=1, source_target_pairs={{0,8},{1,9},{2,10},{3,11},{4,12},{5,13},{6,14},{7,15},{8,0},{9,1},... | collective-permute-start | bytes 405512 | tf_op jit(solution)/shard_map/ppermute | solution.py:282
  17.3 0.0 copy-done.4
  17.3 0.0 copy-start.1
  17.3 0.0 collective-permute-start.5
  17.3 0.5 collective-permute-done.2.refs_1_
  17.8 0.0 copy-done.3
  17.8 8.5 %collective-permute-start.6 = (bf16[528,128]{1,0:T(8,128)(2,1)S(1)}, bf16[528,128]{1,0:T(8,128)(2,1)S(1)}, u32[]{:S(2)}, u32[]{:S(2)}) collective-permute-start(bf16[528,128]{1,0:T(8,128)(2,1)S(1)} %copy-done.3), channel_id=1, source_target_pairs={{0,6},{1,7},{2,4},{3,5},{4,2},{5,3},{6,0},{7,1},{8,14},{9,15},{10,... | collective-permute-start | bytes 405512 | tf_op jit(solution)/shard_map/ppermute | solution.py:282
  26.4 0.0 collective-permute-done.3.refs_2_
  26.4 0.0 collective-permute-start.8
  26.4 6.9 %collective-permute-done.4.refs_3_ = bf16[528,128]{1,0:T(8,128)(2,1)S(1)} collective-permute-done((bf16[528,128]{1,0:T(8,128)(2,1)S(1)}, bf16[528,128]{1,0:T(8,128)(2,1)S(1)}, u32[]{:S(2)}, u32[]{:S(2)}) %collective-permute-start.4) | collective-permute-done | bytes 135200 | tf_op jit(solution)/shard_map/ppermute | solution.py:282
  33.3 0.0 collective-permute-start.9
  33.3 0.6 collective-permute-done.5.refs_4_
  33.8 0.0 collective-permute-start.10
  33.8 0.0 collective-permute-done.6.refs_5_
  33.8 0.5 collective-permute-start.11
  34.3 0.0 collective-permute-done.8.refs_7_
  34.3 0.1 collective-permute-start.12
  34.4 0.2 collective-permute-done.9.refs_8_
  34.6 0.6 collective-permute-done.10.refs_9_
  35.2 0.2 collective-permute-done.11.refs_10_
  35.4 0.3 collective-permute-done.12.refs_11_
  35.7 0.0 collective-permute-done.7.refs_6_
  35.7 0.0 copy-done.1
  35.7 11.3 %chain.1 = (bf16[400,128]{1,0:T(8,128)(2,1)S(1)}, bf16[400,128]{1,0:T(8,128)(2,1)S(1)}, bf16[400,128]{1,0:T(8,128)(2,1)S(1)}, bf16[400,128]{1,0:T(8,128)(2,1)S(1...) custom-call(s32[8]{0:T(128)S(1)} %copy-done.1, ...), custom_call_target="tpu_custom_call" | custom-call | tf_op jit(solution)/shard_map/chain/pallas_call | solution.py:315
  47.0 4.4 %collective-permute-start.13 = (bf16[400,128]{1,0:T(8,128)(2,1)S(1)}, bf16[400,128]{1,0:T(8,128)(2,1)S(1)}, u32[]{:S(2)}, u32[]{:S(2)}) collective-permute-start(bf16[400,128]{1,0:T(8,128)(2,1)S(1)} %get-tuple-element.33), channel_id=1, source_target_pairs={{0,14},{1,15},{2,12},{3,13},{4,10},{5,11},{6,8},{7,9},{8,6},{9,7},... | collective-permute-start | bytes 307208 | tf_op jit(solution)/shard_map/ppermute | solution.py:282
  51.4 1.3 %collective-permute-start.14 = (bf16[400,128]{1,0:T(8,128)(2,1)S(1)}, bf16[400,128]{1,0:T(8,128)(2,1)S(1)}, u32[]{:S(2)}, u32[]{:S(2)}) collective-permute-start(bf16[400,128]{1,0:T(8,128)(2,1)S(1)} %get-tuple-element.34), channel_id=1, source_target_pairs={{0,12},{1,13},{2,14},{3,15},{4,8},{5,9},{6,10},{7,11},{8,4},{9,5},... | collective-permute-start | bytes 307208 | tf_op jit(solution)/shard_map/ppermute | solution.py:282
  52.7 0.0 collective-permute-start.15
  52.7 2.0 %collective-permute-start.16 = (bf16[400,128]{1,0:T(8,128)(2,1)S(1)}, bf16[400,128]{1,0:T(8,128)(2,1)S(1)}, u32[]{:S(2)}, u32[]{:S(2)}) collective-permute-start(bf16[400,128]{1,0:T(8,128)(2,1)S(1)} %get-tuple-element.36), channel_id=1, source_target_pairs={{0,8},{1,9},{2,10},{3,11},{4,12},{5,13},{6,14},{7,15},{8,0},{9,1},... | collective-permute-start | bytes 307208 | tf_op jit(solution)/shard_map/ppermute | solution.py:282
  54.7 2.0 %collective-permute-start.17 = (bf16[400,128]{1,0:T(8,128)(2,1)S(1)}, bf16[400,128]{1,0:T(8,128)(2,1)S(1)}, u32[]{:S(2)}, u32[]{:S(2)}) collective-permute-start(bf16[400,128]{1,0:T(8,128)(2,1)S(1)} %get-tuple-element.37), channel_id=1, source_target_pairs={{0,6},{1,7},{2,4},{3,5},{4,2},{5,3},{6,0},{7,1},{8,14},{9,15},{10,... | collective-permute-start | bytes 307208 | tf_op jit(solution)/shard_map/ppermute | solution.py:282
  56.7 0.0 collective-permute-done.13.refs_1_
  56.7 1.8 %collective-permute-start.18 = (bf16[400,128]{1,0:T(8,128)(2,1)S(1)}, bf16[400,128]{1,0:T(8,128)(2,1)S(1)}, u32[]{:S(2)}, u32[]{:S(2)}) collective-permute-start(bf16[400,128]{1,0:T(8,128)(2,1)S(1)} %get-tuple-element.38), channel_id=1, source_target_pairs={{0,4},{1,5},{2,6},{3,7},{4,0},{5,1},{6,2},{7,3},{8,12},{9,13},{10,... | collective-permute-start | bytes 307208 | tf_op jit(solution)/shard_map/ppermute | solution.py:282
  58.5 0.5 collective-permute-done.14.refs_2_
  59.0 0.0 copy-start
  59.0 0.6 collective-permute-start.19
  59.6 6.3 %collective-permute-done.15.refs_3_ = bf16[400,128]{1,0:T(8,128)(2,1)S(1)} collective-permute-done((bf16[400,128]{1,0:T(8,128)(2,1)S(1)}, bf16[400,128]{1,0:T(8,128)(2,1)S(1)}, u32[]{:S(2)}, u32[]{:S(2)}) %collective-permute-start.15) | collective-permute-done | bytes 102432 | tf_op jit(solution)/shard_map/ppermute | solution.py:282
  65.9 1.5 %collective-permute-done.16.refs_4_ = bf16[400,128]{1,0:T(8,128)(2,1)S(1)} collective-permute-done((bf16[400,128]{1,0:T(8,128)(2,1)S(1)}, bf16[400,128]{1,0:T(8,128)(2,1)S(1)}, u32[]{:S(2)}, u32[]{:S(2)}) %collective-permute-start.16) | collective-permute-done | bytes 102432 | tf_op jit(solution)/shard_map/ppermute | solution.py:282
  67.4 0.0 collective-permute-done.17.refs_5_
  67.4 0.0 collective-permute-done.18.refs_6_
  67.4 0.0 collective-permute-done.19.refs_7_
  67.4 0.0 copy-done
  67.4 1.4 %unpack.1 = (bf16[128,1024]{1,0:T(8,128)(2,1)}, bf16[128,1024]{1,0:T(8,128)(2,1)}, bf16[128,1024]{1,0:T(8,128)(2,1)}, bf16[8,128]{1,0:T(8,128)(2,1)}) custom-call(s32[1]{0:T(128)} %bitcast.chip_ref, s32[1,128]{1,0:T(1,128)S(1)} %bitcast.5, bf16[400,128]{1,0:T(8,128)(2,1)S(1)} %get-tuple-element.32.refs_0_, ...), custom_call_target="tpu_custom_call" | custom-call | tf_op jit(solution)/shard_map/unpack/pallas_call | solution.py:340
  (1 shorter events, 0.0 us)
Async XLA Ops:
  3.2 8.4 %collective-permute-start = (bf16[528,128]{1,0:T(8,128)(2,1)}, bf16[528,128]{1,0:T(8,128)(2,1)S(1)}, u32[]{:S(2)}, u32[]{:S(2)}) collective-permute-start(bf16[528,128]{1,0:T(8,128)(2,1)} %get-tuple-element.25), channel_id=1, source_target_pairs={{0,2},{1,3},{2,0},{3,1},{4,6},{5,7},{6,4},{7,5},{8,10},{9,11},{10,... | collective-permute-start | bytes 405512 | tf_op jit(solution)/shard_map/ppermute | solution.py:282
  6.2 5.4 %collective-permute-start.1 = (bf16[528,128]{1,0:T(8,128)(2,1)}, bf16[528,128]{1,0:T(8,128)(2,1)S(1)}, u32[]{:S(2)}, u32[]{:S(2)}) collective-permute-start(bf16[528,128]{1,0:T(8,128)(2,1)} %get-tuple-element.26), channel_id=1, source_target_pairs={{0,4},{1,5},{2,6},{3,7},{4,0},{5,1},{6,2},{7,3},{8,12},{9,13},{10,... | collective-permute-start | bytes 405512 | tf_op jit(solution)/shard_map/ppermute | solution.py:282
  7.8 10.1 %collective-permute-start.2 = (bf16[528,128]{1,0:T(8,128)(2,1)}, bf16[528,128]{1,0:T(8,128)(2,1)S(1)}, u32[]{:S(2)}, u32[]{:S(2)}) collective-permute-start(bf16[528,128]{1,0:T(8,128)(2,1)} %get-tuple-element.27), channel_id=1, source_target_pairs={{0,12},{1,13},{2,14},{3,15},{4,8},{5,9},{6,10},{7,11},{8,4},{9,5},... | collective-permute-start | bytes 405512 | tf_op jit(solution)/shard_map/ppermute | solution.py:282
  10.3 16.1 %collective-permute-start.3 = (bf16[528,128]{1,0:T(8,128)(2,1)}, bf16[528,128]{1,0:T(8,128)(2,1)S(1)}, u32[]{:S(2)}, u32[]{:S(2)}) collective-permute-start(bf16[528,128]{1,0:T(8,128)(2,1)} %get-tuple-element.28), channel_id=1, source_target_pairs={{0,14},{1,15},{2,12},{3,13},{4,10},{5,11},{6,8},{7,9},{8,6},{9,7},... | collective-permute-start | bytes 405512 | tf_op jit(solution)/shard_map/ppermute | solution.py:282
  11.6 0.9 %copy-start.2 = (bf16[528,128]{1,0:T(8,128)(2,1)S(1)}, bf16[528,128]{1,0:T(8,128)(2,1)}, u32[]{:S(2)}) copy-start(bf16[528,128]{1,0:T(8,128)(2,1)} %get-tuple-element.24.refs_0_) | copy-start | bytes 405508
  12.5 0.9 %copy-start.5 = (bf16[528,128]{1,0:T(8,128)(2,1)S(1)}, bf16[528,128]{1,0:T(8,128)(2,1)}, u32[]{:S(2)}) copy-start(bf16[528,128]{1,0:T(8,128)(2,1)} %get-tuple-element.29) | copy-start | bytes 405508
  12.5 4.9 %copy-start.4 = (bf16[528,128]{1,0:T(8,128)(2,1)S(1)}, bf16[528,128]{1,0:T(8,128)(2,1)}, u32[]{:S(2)}) copy-start(bf16[528,128]{1,0:T(8,128)(2,1)} %get-tuple-element.30) | copy-start | bytes 405508
  12.5 5.4 %copy-start.3 = (bf16[528,128]{1,0:T(8,128)(2,1)S(1)}, bf16[528,128]{1,0:T(8,128)(2,1)}, u32[]{:S(2)}) copy-start(bf16[528,128]{1,0:T(8,128)(2,1)} %get-tuple-element.31) | copy-start | bytes 405508
  12.5 23.2 %collective-permute-start.7 = (bf16[1584,128]{1,0:T(8,128)(2,1)S(1)}, bf16[1584,128]{1,0:T(8,128)(2,1)S(1)}, u32[]{:S(2)}, u32[]{:S(2)}) collective-permute-start(bf16[1584,128]{1,0:T(8,128)(2,1)S(1)} %join.1.refs_0_), channel_id=1, source_target_pairs={{0,1},{1,0},{2,3},{3,2},{4,5},{5,4},{6,7},{7,6},{8,9},{9,8},{10,11... | collective-permute-start | bytes 1216520 | tf_op jit(solution)/shard_map/ppermute | solution.py:285
  13.4 19.9 %collective-permute-start.4 = (bf16[528,128]{1,0:T(8,128)(2,1)S(1)}, bf16[528,128]{1,0:T(8,128)(2,1)S(1)}, u32[]{:S(2)}, u32[]{:S(2)}) collective-permute-start(bf16[528,128]{1,0:T(8,128)(2,1)S(1)} %copy-done.5), channel_id=1, source_target_pairs={{0,8},{1,9},{2,10},{3,11},{4,12},{5,13},{6,14},{7,15},{8,0},{9,1},... | collective-permute-start | bytes 405512 | tf_op jit(solution)/shard_map/ppermute | solution.py:282
  17.3 18.4 %copy-start.1 = (s32[8]{0:T(128)S(1)}, s32[8]{0:T(128)}, u32[]{:S(2)}) copy-start(s32[8]{0:T(128)} %lengths_ref.1) | copy-start | bytes 100
  17.3 16.5 %collective-permute-start.5 = (bf16[528,128]{1,0:T(8,128)(2,1)S(1)}, bf16[528,128]{1,0:T(8,128)(2,1)S(1)}, u32[]{:S(2)}, u32[]{:S(2)}) collective-permute-start(bf16[528,128]{1,0:T(8,128)(2,1)S(1)} %copy-done.4), channel_id=1, source_target_pairs={{0,10},{1,11},{2,8},{3,9},{4,14},{5,15},{6,12},{7,13},{8,2},{9,3},... | collective-permute-start | bytes 405512 | tf_op jit(solution)/shard_map/ppermute | solution.py:282
  17.8 16.0 %collective-permute-start.6 = (bf16[528,128]{1,0:T(8,128)(2,1)S(1)}, bf16[528,128]{1,0:T(8,128)(2,1)S(1)}, u32[]{:S(2)}, u32[]{:S(2)}) collective-permute-start(bf16[528,128]{1,0:T(8,128)(2,1)S(1)} %copy-done.3), channel_id=1, source_target_pairs={{0,6},{1,7},{2,4},{3,5},{4,2},{5,3},{6,0},{7,1},{8,14},{9,15},{10,... | collective-permute-start | bytes 405512 | tf_op jit(solution)/shard_map/ppermute | solution.py:282
  26.4 8.0 %collective-permute-start.8 = (bf16[528,128]{1,0:T(8,128)(2,1)S(1)}, bf16[528,128]{1,0:T(8,128)(2,1)S(1)}, u32[]{:S(2)}, u32[]{:S(2)}) collective-permute-start(bf16[528,128]{1,0:T(8,128)(2,1)S(1)} %collective-permute-done.2.refs_1_), channel_id=1, source_target_pairs={{0,1},{1,0},{2,3},{3,2},{4,5},{5,4},{6,7},{7,6},{8,9},{9,8},{10,11... | collective-permute-start | bytes 405512 | tf_op jit(solution)/shard_map/ppermute | solution.py:285
  33.3 1.4 %collective-permute-start.9 = (bf16[528,128]{1,0:T(8,128)(2,1)S(1)}, bf16[528,128]{1,0:T(8,128)(2,1)S(1)}, u32[]{:S(2)}, u32[]{:S(2)}) collective-permute-start(bf16[528,128]{1,0:T(8,128)(2,1)S(1)} %collective-permute-done.3.refs_2_), channel_id=1, source_target_pairs={{0,1},{1,0},{2,3},{3,2},{4,5},{5,4},{6,7},{7,6},{8,9},{9,8},{10,11... | collective-permute-start | bytes 405512 | tf_op jit(solution)/shard_map/ppermute | solution.py:285
  33.8 1.4 %collective-permute-start.10 = (bf16[528,128]{1,0:T(8,128)(2,1)S(1)}, bf16[528,128]{1,0:T(8,128)(2,1)S(1)}, u32[]{:S(2)}, u32[]{:S(2)}) collective-permute-start(bf16[528,128]{1,0:T(8,128)(2,1)S(1)} %collective-permute-done.4.refs_3_), channel_id=1, source_target_pairs={{0,1},{1,0},{2,3},{3,2},{4,5},{5,4},{6,7},{7,6},{8,9},{9,8},{10,11... | collective-permute-start | bytes 405512 | tf_op jit(solution)/shard_map/ppermute | solution.py:285
  33.8 1.5 %collective-permute-start.11 = (bf16[528,128]{1,0:T(8,128)(2,1)S(1)}, bf16[528,128]{1,0:T(8,128)(2,1)S(1)}, u32[]{:S(2)}, u32[]{:S(2)}) collective-permute-start(bf16[528,128]{1,0:T(8,128)(2,1)S(1)} %collective-permute-done.5.refs_4_), channel_id=1, source_target_pairs={{0,1},{1,0},{2,3},{3,2},{4,5},{5,4},{6,7},{7,6},{8,9},{9,8},{10,11... | collective-permute-start | bytes 405512 | tf_op jit(solution)/shard_map/ppermute | solution.py:285
  34.3 1.4 %collective-permute-start.12 = (bf16[528,128]{1,0:T(8,128)(2,1)S(1)}, bf16[528,128]{1,0:T(8,128)(2,1)S(1)}, u32[]{:S(2)}, u32[]{:S(2)}) collective-permute-start(bf16[528,128]{1,0:T(8,128)(2,1)S(1)} %collective-permute-done.6.refs_5_), channel_id=1, source_target_pairs={{0,1},{1,0},{2,3},{3,2},{4,5},{5,4},{6,7},{7,6},{8,9},{9,8},{10,11... | collective-permute-start | bytes 405512 | tf_op jit(solution)/shard_map/ppermute | solution.py:285
  47.0 9.7 %collective-permute-start.13 = (bf16[400,128]{1,0:T(8,128)(2,1)S(1)}, bf16[400,128]{1,0:T(8,128)(2,1)S(1)}, u32[]{:S(2)}, u32[]{:S(2)}) collective-permute-start(bf16[400,128]{1,0:T(8,128)(2,1)S(1)} %get-tuple-element.33), channel_id=1, source_target_pairs={{0,14},{1,15},{2,12},{3,13},{4,10},{5,11},{6,8},{7,9},{8,6},{9,7},... | collective-permute-start | bytes 307208 | tf_op jit(solution)/shard_map/ppermute | solution.py:282
  51.4 7.6 %collective-permute-start.14 = (bf16[400,128]{1,0:T(8,128)(2,1)S(1)}, bf16[400,128]{1,0:T(8,128)(2,1)S(1)}, u32[]{:S(2)}, u32[]{:S(2)}) collective-permute-start(bf16[400,128]{1,0:T(8,128)(2,1)S(1)} %get-tuple-element.34), channel_id=1, source_target_pairs={{0,12},{1,13},{2,14},{3,15},{4,8},{5,9},{6,10},{7,11},{8,4},{9,5},... | collective-permute-start | bytes 307208 | tf_op jit(solution)/shard_map/ppermute | solution.py:282
  52.7 13.2 %collective-permute-start.15 = (bf16[400,128]{1,0:T(8,128)(2,1)S(1)}, bf16[400,128]{1,0:T(8,128)(2,1)S(1)}, u32[]{:S(2)}, u32[]{:S(2)}) collective-permute-start(bf16[400,128]{1,0:T(8,128)(2,1)S(1)} %get-tuple-element.35), channel_id=1, source_target_pairs={{0,10},{1,11},{2,8},{3,9},{4,14},{5,15},{6,12},{7,13},{8,2},{9,3},... | collective-permute-start | bytes 307208 | tf_op jit(solution)/shard_map/ppermute | solution.py:282
  52.7 14.7 %collective-permute-start.16 = (bf16[400,128]{1,0:T(8,128)(2,1)S(1)}, bf16[400,128]{1,0:T(8,128)(2,1)S(1)}, u32[]{:S(2)}, u32[]{:S(2)}) collective-permute-start(bf16[400,128]{1,0:T(8,128)(2,1)S(1)} %get-tuple-element.36), channel_id=1, source_target_pairs={{0,8},{1,9},{2,10},{3,11},{4,12},{5,13},{6,14},{7,15},{8,0},{9,1},... | collective-permute-start | bytes 307208 | tf_op jit(solution)/shard_map/ppermute | solution.py:282
  54.7 12.6 %collective-permute-start.17 = (bf16[400,128]{1,0:T(8,128)(2,1)S(1)}, bf16[400,128]{1,0:T(8,128)(2,1)S(1)}, u32[]{:S(2)}, u32[]{:S(2)}) collective-permute-start(bf16[400,128]{1,0:T(8,128)(2,1)S(1)} %get-tuple-element.37), channel_id=1, source_target_pairs={{0,6},{1,7},{2,4},{3,5},{4,2},{5,3},{6,0},{7,1},{8,14},{9,15},{10,... | collective-permute-start | bytes 307208 | tf_op jit(solution)/shard_map/ppermute | solution.py:282
  56.7 10.7 %collective-permute-start.18 = (bf16[400,128]{1,0:T(8,128)(2,1)S(1)}, bf16[400,128]{1,0:T(8,128)(2,1)S(1)}, u32[]{:S(2)}, u32[]{:S(2)}) collective-permute-start(bf16[400,128]{1,0:T(8,128)(2,1)S(1)} %get-tuple-element.38), channel_id=1, source_target_pairs={{0,4},{1,5},{2,6},{3,7},{4,0},{5,1},{6,2},{7,3},{8,12},{9,13},{10,... | collective-permute-start | bytes 307208 | tf_op jit(solution)/shard_map/ppermute | solution.py:282
  59.0 8.4 %copy-start = (s32[128]{0:T(128)S(1)}, s32[128]{0:T(128)}, u32[]{:S(2)}) copy-start(s32[128]{0:T(128)} %param.12) | copy-start | bytes 1540
  59.0 8.4 %collective-permute-start.19 = (bf16[400,128]{1,0:T(8,128)(2,1)S(1)}, bf16[400,128]{1,0:T(8,128)(2,1)S(1)}, u32[]{:S(2)}, u32[]{:S(2)}) collective-permute-start(bf16[400,128]{1,0:T(8,128)(2,1)S(1)} %get-tuple-element.39), channel_id=1, source_target_pairs={{0,2},{1,3},{2,0},{3,1},{4,6},{5,7},{6,4},{7,5},{8,10},{9,11},{10,... | collective-permute-start | bytes 307208 | tf_op jit(solution)/shard_map/ppermute | solution.py:282

commit v7 on v6

--- a/solution.py
+++ b/solution.py
@@ -243,19 +243,22 @@
         outs[s][3 * rows:, :] = jnp.broadcast_to(found, (META, rows)).astype(BF16)
 
 
-def join_kernel(*refs):
-    size = refs[0].shape[0]
-    for n, ref in enumerate(refs[:-1]):
-        refs[-1][n * size:(n + 1) * size, :] = ref[...]
-
-
-def unpack_kernel(chip_ref, pos_ref, *refs):
+def join_kernel(pos_ref, *refs):
+    blocks, joined_ref, loose_ref = refs[:-2], refs[-2], refs[-1]
+    size = blocks[0].shape[0]
+    rows = pos_ref.shape[1]
+    for n, ref in enumerate(blocks):
+        joined_ref[n * size:(n + 1) * size, :] = ref[...]
+    _, rank = order(pos_ref[...])
+    loose_ref[...] = (rank == iota((rows, rows), 1)).astype(BF16)
+
+
+def unpack_kernel(chip_ref, loose_ref, *refs):
     heads = len(refs) - 4
     blocks, outs = refs[:heads], refs[heads:]
     rows = outs[0].shape[0]
     chip = chip_ref[0]
-    _, rank = order(pos_ref[...])
-    loose = (rank == iota((rows, rows), 1)).astype(BF16)
+    loose = loose_ref[...]
     line = iota((META, rows), 0)
     tails = jnp.zeros((META, rows), F32)
     for s in range(heads):
@@ -297,15 +300,15 @@
     )(chip, queries, keys, values, out_grad, log_decay.T, frame_pos.reshape(1, rows))
     got = [packets[0]] + [across(packets[s], COMING[s]) for s in range(1, heads)]
     size = 4 * rows + META
-    joined = pl.pallas_call(
+    joined, loose = pl.pallas_call(
         join_kernel,
-        out_shape=jax.ShapeDtypeStruct((TOGETHER * size, SPAN), BF16),
-        in_specs=[VMEM] * TOGETHER,
-        out_specs=VMEM,
+        out_shape=[jax.ShapeDtypeStruct((TOGETHER * size, SPAN), BF16), jax.ShapeDtypeStruct((rows, rows), BF16)],
+        in_specs=[VMEM] * (1 + TOGETHER),
+        out_specs=[VMEM] * 2,
         compiler_params=pltpu.CompilerParams(vmem_limit_bytes=4 * 2**20),
         cost_estimate=pl.CostEstimate(flops=2**30, bytes_accessed=2**18, transcendentals=0),
         name="join",
-    )(*got[:TOGETHER])
+    )(frame_pos.reshape(1, rows), *got[:TOGETHER])
     got = [joined, *got[TOGETHER:]]
     everything = list(got)
     for t in range(1, cores):
@@ -344,7 +347,7 @@
         out_specs=[VMEM] * 4,
         compiler_params=pltpu.CompilerParams(vmem_limit_bytes=12 * 2**20),
         name="unpack",
-    )(chip, frame_pos.reshape(1, rows), *returned)
+    )(chip, loose, *returned)
     return (*grads, tails.T)
 
 

time: 69 us -> 68.8 us (level)
  no operation moved by 1% of the time
where the time goes in v7:
time: 68.8 us; the launch traced here: 68.7 us
  starting transfers between devices  33.6 us (49%)
  waiting for transfers between devices  17.5 us (25%)
  Pallas kernels  15.3 us (22%)
  local copies, waits for them, and re-layouts  1.55 us (2%)
  between operations  0.72 us (1%)
    ppermute x14, starting transfers between devices, across(): return lax.ppermute(x, 'ctx', [(p, p ^ s * cores) for p in range(peers)])  33 us
    ppermute x14, waiting for transfers between devices, across(): return lax.ppermute(x, 'ctx', [(p, p ^ s * cores) for p in range(peers)])  16.2 us
    pallas_call x1, Pallas kernels, body(): pl.pallas_call(functools.partial(chain_kernel, heads), out_shape=[jax.Sha...  11.3 us
    pallas_call x1, Pallas kernels, body(): pl.pallas_call(pack_kernel, out_shape=[jax.ShapeDtypeStruct((4 * rows + M...  2.51 us
    unnamed x12, local copies, waits for them, and re-layouts  1.55 us
  transfers between devices with their start and end apart: 20, of which 10 were waited for; matrix products, arithmetic and copies ran while one was open for 0% of the time, Pallas kernels for 0%

profile of v7, /device:TPU:0, one launch (start us, length us, event | category | flops | bytes accessed | tf_op | source)
XLA Modules:
  0.0 68.7 jit_solution(13592359844398838261)
XLA Ops:
  0.6 2.5 %pack.1 = (bf16[528,128]{1,0:T(8,128)(2,1)}, bf16[528,128]{1,0:T(8,128)(2,1)}, bf16[528,128]{1,0:T(8,128)(2,1)}, bf16[528,128]{1,0:T(8,128)(2,1)}, bf16[528,128]...) custom-call(s32[1]{0:T(128)} %bitcast.chip_ref, ...), custom_call_target="tpu_custom_call" | custom-call | tf_op jit(solution)/shard_map/pack/pallas_call | solution.py:290
  3.2 3.0 %collective-permute-start = (bf16[528,128]{1,0:T(8,128)(2,1)}, bf16[528,128]{1,0:T(8,128)(2,1)S(1)}, u32[]{:S(2)}, u32[]{:S(2)}) collective-permute-start(bf16[528,128]{1,0:T(8,128)(2,1)} %get-tuple-element.27), channel_id=1, source_target_pairs={{0,2},{1,3},{2,0},{3,1},{4,6},{5,7},{6,4},{7,5},{8,10},{9,11},{10,... | collective-permute-start | bytes 405512 | tf_op jit(solution)/shard_map/ppermute | solution.py:285
  6.2 1.6 %collective-permute-start.1 = (bf16[528,128]{1,0:T(8,128)(2,1)}, bf16[528,128]{1,0:T(8,128)(2,1)S(1)}, u32[]{:S(2)}, u32[]{:S(2)}) collective-permute-start(bf16[528,128]{1,0:T(8,128)(2,1)} %get-tuple-element.28), channel_id=1, source_target_pairs={{0,4},{1,5},{2,6},{3,7},{4,0},{5,1},{6,2},{7,3},{8,12},{9,13},{10,... | collective-permute-start | bytes 405512 | tf_op jit(solution)/shard_map/ppermute | solution.py:285
  7.8 2.5 %collective-permute-start.2 = (bf16[528,128]{1,0:T(8,128)(2,1)}, bf16[528,128]{1,0:T(8,128)(2,1)S(1)}, u32[]{:S(2)}, u32[]{:S(2)}) collective-permute-start(bf16[528,128]{1,0:T(8,128)(2,1)} %get-tuple-element.31), channel_id=1, source_target_pairs={{0,12},{1,13},{2,14},{3,15},{4,8},{5,9},{6,10},{7,11},{8,4},{9,5},... | collective-permute-start | bytes 405512 | tf_op jit(solution)/shard_map/ppermute | solution.py:285
  10.2 0.0 copy-start
  10.3 1.3 %collective-permute-start.3 = (bf16[528,128]{1,0:T(8,128)(2,1)}, bf16[528,128]{1,0:T(8,128)(2,1)S(1)}, u32[]{:S(2)}, u32[]{:S(2)}) collective-permute-start(bf16[528,128]{1,0:T(8,128)(2,1)} %get-tuple-element.32), channel_id=1, source_target_pairs={{0,14},{1,15},{2,12},{3,13},{4,10},{5,11},{6,8},{7,9},{8,6},{9,7},... | collective-permute-start | bytes 405512 | tf_op jit(solution)/shard_map/ppermute | solution.py:285
  11.5 0.0 collective-permute-done.refs_1_
  11.5 0.0 collective-permute-done.1.refs_2_
  11.5 0.0 copy-done
  11.6 0.0 copy-start.2
  11.6 0.9 %copy-done.2 = bf16[528,128]{1,0:T(8,128)(2,1)S(1)} copy-done((bf16[528,128]{1,0:T(8,128)(2,1)S(1)}, bf16[528,128]{1,0:T(8,128)(2,1)}, u32[]{:S(2)}) %copy-start.2) | copy-done | bytes 135192
  12.5 0.0 copy-start.5
  12.5 0.0 copy-start.4
  12.5 0.0 copy-start.3
  12.5 0.2 join.1
  12.7 0.1 collective-permute-start.7
  12.7 0.6 copy-done.5
  13.4 4.0 %collective-permute-start.4 = (bf16[528,128]{1,0:T(8,128)(2,1)S(1)}, bf16[528,128]{1,0:T(8,128)(2,1)S(1)}, u32[]{:S(2)}, u32[]{:S(2)}) collective-permute-start(bf16[528,128]{1,0:T(8,128)(2,1)S(1)} %copy-done.5), channel_id=1, source_target_pairs={{0,8},{1,9},{2,10},{3,11},{4,12},{5,13},{6,14},{7,15},{8,0},{9,1},... | collective-permute-start | bytes 405512 | tf_op jit(solution)/shard_map/ppermute | solution.py:285
  17.3 0.0 copy-done.4
  17.3 0.0 copy-start.1
  17.3 0.0 collective-permute-start.5
  17.3 0.5 collective-permute-done.2.refs_1_
  17.8 0.0 copy-done.3
  17.8 8.5 %collective-permute-start.6 = (bf16[528,128]{1,0:T(8,128)(2,1)S(1)}, bf16[528,128]{1,0:T(8,128)(2,1)S(1)}, u32[]{:S(2)}, u32[]{:S(2)}) collective-permute-start(bf16[528,128]{1,0:T(8,128)(2,1)S(1)} %copy-done.3), channel_id=1, source_target_pairs={{0,6},{1,7},{2,4},{3,5},{4,2},{5,3},{6,0},{7,1},{8,14},{9,15},{10,... | collective-permute-start | bytes 405512 | tf_op jit(solution)/shard_map/ppermute | solution.py:285
  26.4 0.0 collective-permute-done.3.refs_2_
  26.4 0.0 collective-permute-start.8
  26.4 6.9 %collective-permute-done.4.refs_3_ = bf16[528,128]{1,0:T(8,128)(2,1)S(1)} collective-permute-done((bf16[528,128]{1,0:T(8,128)(2,1)S(1)}, bf16[528,128]{1,0:T(8,128)(2,1)S(1)}, u32[]{:S(2)}, u32[]{:S(2)}) %collective-permute-start.4) | collective-permute-done | bytes 135200 | tf_op jit(solution)/shard_map/ppermute | solution.py:285
  33.3 0.0 collective-permute-start.9
  33.3 0.5 collective-permute-done.5.refs_4_
  33.8 0.0 collective-permute-start.10
  33.8 0.0 collective-permute-done.6.refs_5_
  33.8 0.5 collective-permute-start.11
  34.3 0.0 collective-permute-done.8.refs_7_
  34.3 0.1 collective-permute-start.12
  34.4 0.2 collective-permute-done.9.refs_8_
  34.6 0.6 collective-permute-done.10.refs_9_
  35.2 0.2 collective-permute-done.11.refs_10_
  35.4 0.3 collective-permute-done.12.refs_11_
  35.7 0.0 collective-permute-done.7.refs_6_
  35.7 0.0 copy-done.1
  35.7 11.3 %chain.1 = (bf16[400,128]{1,0:T(8,128)(2,1)S(1)}, bf16[400,128]{1,0:T(8,128)(2,1)S(1)}, bf16[400,128]{1,0:T(8,128)(2,1)S(1)}, bf16[400,128]{1,0:T(8,128)(2,1)S(1...) custom-call(s32[8]{0:T(128)S(1)} %copy-done.1, ...), custom_call_target="tpu_custom_call" | custom-call | tf_op jit(solution)/shard_map/chain/pallas_call | solution.py:318
  47.0 4.4 %collective-permute-start.13 = (bf16[400,128]{1,0:T(8,128)(2,1)S(1)}, bf16[400,128]{1,0:T(8,128)(2,1)S(1)}, u32[]{:S(2)}, u32[]{:S(2)}) collective-permute-start(bf16[400,128]{1,0:T(8,128)(2,1)S(1)} %get-tuple-element.37), channel_id=1, source_target_pairs={{0,14},{1,15},{2,12},{3,13},{4,10},{5,11},{6,8},{7,9},{8,6},{9,7},... | collective-permute-start | bytes 307208 | tf_op jit(solution)/shard_map/ppermute | solution.py:285
  51.4 1.3 %collective-permute-start.14 = (bf16[400,128]{1,0:T(8,128)(2,1)S(1)}, bf16[400,128]{1,0:T(8,128)(2,1)S(1)}, u32[]{:S(2)}, u32[]{:S(2)}) collective-permute-start(bf16[400,128]{1,0:T(8,128)(2,1)S(1)} %get-tuple-element.38), channel_id=1, source_target_pairs={{0,12},{1,13},{2,14},{3,15},{4,8},{5,9},{6,10},{7,11},{8,4},{9,5},... | collective-permute-start | bytes 307208 | tf_op jit(solution)/shard_map/ppermute | solution.py:285
  52.7 0.0 collective-permute-start.15
  52.7 2.0 %collective-permute-start.16 = (bf16[400,128]{1,0:T(8,128)(2,1)S(1)}, bf16[400,128]{1,0:T(8,128)(2,1)S(1)}, u32[]{:S(2)}, u32[]{:S(2)}) collective-permute-start(bf16[400,128]{1,0:T(8,128)(2,1)S(1)} %get-tuple-element.40), channel_id=1, source_target_pairs={{0,8},{1,9},{2,10},{3,11},{4,12},{5,13},{6,14},{7,15},{8,0},{9,1},... | collective-permute-start | bytes 307208 | tf_op jit(solution)/shard_map/ppermute | solution.py:285
  54.7 2.0 %collective-permute-start.17 = (bf16[400,128]{1,0:T(8,128)(2,1)S(1)}, bf16[400,128]{1,0:T(8,128)(2,1)S(1)}, u32[]{:S(2)}, u32[]{:S(2)}) collective-permute-start(bf16[400,128]{1,0:T(8,128)(2,1)S(1)} %get-tuple-element.41), channel_id=1, source_target_pairs={{0,6},{1,7},{2,4},{3,5},{4,2},{5,3},{6,0},{7,1},{8,14},{9,15},{10,... | collective-permute-start | bytes 307208 | tf_op jit(solution)/shard_map/ppermute | solution.py:285
  56.7 0.0 collective-permute-done.13.refs_1_
  56.7 1.9 %collective-permute-start.18 = (bf16[400,128]{1,0:T(8,128)(2,1)S(1)}, bf16[400,128]{1,0:T(8,128)(2,1)S(1)}, u32[]{:S(2)}, u32[]{:S(2)}) collective-permute-start(bf16[400,128]{1,0:T(8,128)(2,1)S(1)} %get-tuple-element.42), channel_id=1, source_target_pairs={{0,4},{1,5},{2,6},{3,7},{4,0},{5,1},{6,2},{7,3},{8,12},{9,13},{10,... | collective-permute-start | bytes 307208 | tf_op jit(solution)/shard_map/ppermute | solution.py:285
  58.6 0.4 collective-permute-done.14.refs_2_
  59.0 0.6 collective-permute-start.19
  59.6 6.3 %collective-permute-done.15.refs_3_ = bf16[400,128]{1,0:T(8,128)(2,1)S(1)} collective-permute-done((bf16[400,128]{1,0:T(8,128)(2,1)S(1)}, bf16[400,128]{1,0:T(8,128)(2,1)S(1)}, u32[]{:S(2)}, u32[]{:S(2)}) %collective-permute-start.15) | collective-permute-done | bytes 102432 | tf_op jit(solution)/shard_map/ppermute | solution.py:285
  65.9 1.5 %collective-permute-done.16.refs_4_ = bf16[400,128]{1,0:T(8,128)(2,1)S(1)} collective-permute-done((bf16[400,128]{1,0:T(8,128)(2,1)S(1)}, bf16[400,128]{1,0:T(8,128)(2,1)S(1)}, u32[]{:S(2)}, u32[]{:S(2)}) %collective-permute-start.16) | collective-permute-done | bytes 102432 | tf_op jit(solution)/shard_map/ppermute | solution.py:285
  67.4 0.0 collective-permute-done.17.refs_5_
  67.4 0.0 collective-permute-done.18.refs_6_
  67.4 0.0 collective-permute-done.19.refs_7_
  67.4 1.3 %unpack.1 = (bf16[128,1024]{1,0:T(8,128)(2,1)}, bf16[128,1024]{1,0:T(8,128)(2,1)}, bf16[128,1024]{1,0:T(8,128)(2,1)}, bf16[8,128]{1,0:T(8,128)(2,1)}) custom-call(s32[1]{0:T(128)} %bitcast.chip_ref, bf16[128,128]{1,0:T(8,128)(2,1)S(1)} %get-tuple-element.29.loose_ref, bf16[400,128]{1,0:T(8,128)(2,1)S(1)} %get-tuple-element.36.refs_0_, ...), custom_call_target="tpu_custom_call" | custom-call | tf_op jit(solution)/shard_map/unpack/pallas_call | solution.py:343
Async XLA Ops:
  3.2 8.4 %collective-permute-start = (bf16[528,128]{1,0:T(8,128)(2,1)}, bf16[528,128]{1,0:T(8,128)(2,1)S(1)}, u32[]{:S(2)}, u32[]{:S(2)}) collective-permute-start(bf16[528,128]{1,0:T(8,128)(2,1)} %get-tuple-element.27), channel_id=1, source_target_pairs={{0,2},{1,3},{2,0},{3,1},{4,6},{5,7},{6,4},{7,5},{8,10},{9,11},{10,... | collective-permute-start | bytes 405512 | tf_op jit(solution)/shard_map/ppermute | solution.py:285
  6.2 5.4 %collective-permute-start.1 = (bf16[528,128]{1,0:T(8,128)(2,1)}, bf16[528,128]{1,0:T(8,128)(2,1)S(1)}, u32[]{:S(2)}, u32[]{:S(2)}) collective-permute-start(bf16[528,128]{1,0:T(8,128)(2,1)} %get-tuple-element.28), channel_id=1, source_target_pairs={{0,4},{1,5},{2,6},{3,7},{4,0},{5,1},{6,2},{7,3},{8,12},{9,13},{10,... | collective-permute-start | bytes 405512 | tf_op jit(solution)/shard_map/ppermute | solution.py:285
  7.8 10.1 %collective-permute-start.2 = (bf16[528,128]{1,0:T(8,128)(2,1)}, bf16[528,128]{1,0:T(8,128)(2,1)S(1)}, u32[]{:S(2)}, u32[]{:S(2)}) collective-permute-start(bf16[528,128]{1,0:T(8,128)(2,1)} %get-tuple-element.31), channel_id=1, source_target_pairs={{0,12},{1,13},{2,14},{3,15},{4,8},{5,9},{6,10},{7,11},{8,4},{9,5},... | collective-permute-start | bytes 405512 | tf_op jit(solution)/shard_map/ppermute | solution.py:285
  10.2 1.3 %copy-start = (s32[128]{0:T(128)S(1)}, s32[128]{0:T(128)}, u32[]{:S(2)}) copy-start(s32[128]{0:T(128)} %param.12) | copy-start | bytes 1540
  10.3 16.1 %collective-permute-start.3 = (bf16[528,128]{1,0:T(8,128)(2,1)}, bf16[528,128]{1,0:T(8,128)(2,1)S(1)}, u32[]{:S(2)}, u32[]{:S(2)}) collective-permute-start(bf16[528,128]{1,0:T(8,128)(2,1)} %get-tuple-element.32), channel_id=1, source_target_pairs={{0,14},{1,15},{2,12},{3,13},{4,10},{5,11},{6,8},{7,9},{8,6},{9,7},... | collective-permute-start | bytes 405512 | tf_op jit(solution)/shard_map/ppermute | solution.py:285
  11.6 0.9 %copy-start.2 = (bf16[528,128]{1,0:T(8,128)(2,1)S(1)}, bf16[528,128]{1,0:T(8,128)(2,1)}, u32[]{:S(2)}) copy-start(bf16[528,128]{1,0:T(8,128)(2,1)} %get-tuple-element.26.refs_0_) | copy-start | bytes 405508
  12.5 0.9 %copy-start.5 = (bf16[528,128]{1,0:T(8,128)(2,1)S(1)}, bf16[528,128]{1,0:T(8,128)(2,1)}, u32[]{:S(2)}) copy-start(bf16[528,128]{1,0:T(8,128)(2,1)} %get-tuple-element.33) | copy-start | bytes 405508
  12.5 4.9 %copy-start.4 = (bf16[528,128]{1,0:T(8,128)(2,1)S(1)}, bf16[528,128]{1,0:T(8,128)(2,1)}, u32[]{:S(2)}) copy-start(bf16[528,128]{1,0:T(8,128)(2,1)} %get-tuple-element.34) | copy-start | bytes 405508
  12.5 5.4 %copy-start.3 = (bf16[528,128]{1,0:T(8,128)(2,1)S(1)}, bf16[528,128]{1,0:T(8,128)(2,1)}, u32[]{:S(2)}) copy-start(bf16[528,128]{1,0:T(8,128)(2,1)} %get-tuple-element.35) | copy-start | bytes 405508
  12.7 23.0 %collective-permute-start.7 = (bf16[1584,128]{1,0:T(8,128)(2,1)S(1)}, bf16[1584,128]{1,0:T(8,128)(2,1)S(1)}, u32[]{:S(2)}, u32[]{:S(2)}) collective-permute-start(bf16[1584,128]{1,0:T(8,128)(2,1)S(1)} %get-tuple-element.30.refs_0_), channel_id=1, source_target_pairs={{0,1},{1,0},{2,3},{3,2},{4,5},{5,4},{6,7},{7,6},{8,9},{9,8},{10,11... | collective-permute-start | bytes 1216520 | tf_op jit(solution)/shard_map/ppermute | solution.py:288
  13.4 19.9 %collective-permute-start.4 = (bf16[528,128]{1,0:T(8,128)(2,1)S(1)}, bf16[528,128]{1,0:T(8,128)(2,1)S(1)}, u32[]{:S(2)}, u32[]{:S(2)}) collective-permute-start(bf16[528,128]{1,0:T(8,128)(2,1)S(1)} %copy-done.5), channel_id=1, source_target_pairs={{0,8},{1,9},{2,10},{3,11},{4,12},{5,13},{6,14},{7,15},{8,0},{9,1},... | collective-permute-start | bytes 405512 | tf_op jit(solution)/shard_map/ppermute | solution.py:285
  17.3 18.4 %copy-start.1 = (s32[8]{0:T(128)S(1)}, s32[8]{0:T(128)}, u32[]{:S(2)}) copy-start(s32[8]{0:T(128)} %lengths_ref.1) | copy-start | bytes 100
  17.3 16.5 %collective-permute-start.5 = (bf16[528,128]{1,0:T(8,128)(2,1)S(1)}, bf16[528,128]{1,0:T(8,128)(2,1)S(1)}, u32[]{:S(2)}, u32[]{:S(2)}) collective-permute-start(bf16[528,128]{1,0:T(8,128)(2,1)S(1)} %copy-done.4), channel_id=1, source_target_pairs={{0,10},{1,11},{2,8},{3,9},{4,14},{5,15},{6,12},{7,13},{8,2},{9,3},... | collective-permute-start | bytes 405512 | tf_op jit(solution)/shard_map/ppermute | solution.py:285
  17.8 16.0 %collective-permute-start.6 = (bf16[528,128]{1,0:T(8,128)(2,1)S(1)}, bf16[528,128]{1,0:T(8,128)(2,1)S(1)}, u32[]{:S(2)}, u32[]{:S(2)}) collective-permute-start(bf16[528,128]{1,0:T(8,128)(2,1)S(1)} %copy-done.3), channel_id=1, source_target_pairs={{0,6},{1,7},{2,4},{3,5},{4,2},{5,3},{6,0},{7,1},{8,14},{9,15},{10,... | collective-permute-start | bytes 405512 | tf_op jit(solution)/shard_map/ppermute | solution.py:285
  26.4 8.0 %collective-permute-start.8 = (bf16[528,128]{1,0:T(8,128)(2,1)S(1)}, bf16[528,128]{1,0:T(8,128)(2,1)S(1)}, u32[]{:S(2)}, u32[]{:S(2)}) collective-permute-start(bf16[528,128]{1,0:T(8,128)(2,1)S(1)} %collective-permute-done.2.refs_1_), channel_id=1, source_target_pairs={{0,1},{1,0},{2,3},{3,2},{4,5},{5,4},{6,7},{7,6},{8,9},{9,8},{10,11... | collective-permute-start | bytes 405512 | tf_op jit(solution)/shard_map/ppermute | solution.py:288
  33.3 1.4 %collective-permute-start.9 = (bf16[528,128]{1,0:T(8,128)(2,1)S(1)}, bf16[528,128]{1,0:T(8,128)(2,1)S(1)}, u32[]{:S(2)}, u32[]{:S(2)}) collective-permute-start(bf16[528,128]{1,0:T(8,128)(2,1)S(1)} %collective-permute-done.3.refs_2_), channel_id=1, source_target_pairs={{0,1},{1,0},{2,3},{3,2},{4,5},{5,4},{6,7},{7,6},{8,9},{9,8},{10,11... | collective-permute-start | bytes 405512 | tf_op jit(solution)/shard_map/ppermute | solution.py:288
  33.8 1.4 %collective-permute-start.10 = (bf16[528,128]{1,0:T(8,128)(2,1)S(1)}, bf16[528,128]{1,0:T(8,128)(2,1)S(1)}, u32[]{:S(2)}, u32[]{:S(2)}) collective-permute-start(bf16[528,128]{1,0:T(8,128)(2,1)S(1)} %collective-permute-done.4.refs_3_), channel_id=1, source_target_pairs={{0,1},{1,0},{2,3},{3,2},{4,5},{5,4},{6,7},{7,6},{8,9},{9,8},{10,11... | collective-permute-start | bytes 405512 | tf_op jit(solution)/shard_map/ppermute | solution.py:288
  33.8 1.5 %collective-permute-start.11 = (bf16[528,128]{1,0:T(8,128)(2,1)S(1)}, bf16[528,128]{1,0:T(8,128)(2,1)S(1)}, u32[]{:S(2)}, u32[]{:S(2)}) collective-permute-start(bf16[528,128]{1,0:T(8,128)(2,1)S(1)} %collective-permute-done.5.refs_4_), channel_id=1, source_target_pairs={{0,1},{1,0},{2,3},{3,2},{4,5},{5,4},{6,7},{7,6},{8,9},{9,8},{10,11... | collective-permute-start | bytes 405512 | tf_op jit(solution)/shard_map/ppermute | solution.py:288
  34.3 1.4 %collective-permute-start.12 = (bf16[528,128]{1,0:T(8,128)(2,1)S(1)}, bf16[528,128]{1,0:T(8,128)(2,1)S(1)}, u32[]{:S(2)}, u32[]{:S(2)}) collective-permute-start(bf16[528,128]{1,0:T(8,128)(2,1)S(1)} %collective-permute-done.6.refs_5_), channel_id=1, source_target_pairs={{0,1},{1,0},{2,3},{3,2},{4,5},{5,4},{6,7},{7,6},{8,9},{9,8},{10,11... | collective-permute-start | bytes 405512 | tf_op jit(solution)/shard_map/ppermute | solution.py:288
  47.0 9.7 %collective-permute-start.13 = (bf16[400,128]{1,0:T(8,128)(2,1)S(1)}, bf16[400,128]{1,0:T(8,128)(2,1)S(1)}, u32[]{:S(2)}, u32[]{:S(2)}) collective-permute-start(bf16[400,128]{1,0:T(8,128)(2,1)S(1)} %get-tuple-element.37), channel_id=1, source_target_pairs={{0,14},{1,15},{2,12},{3,13},{4,10},{5,11},{6,8},{7,9},{8,6},{9,7},... | collective-permute-start | bytes 307208 | tf_op jit(solution)/shard_map/ppermute | solution.py:285
  51.4 7.6 %collective-permute-start.14 = (bf16[400,128]{1,0:T(8,128)(2,1)S(1)}, bf16[400,128]{1,0:T(8,128)(2,1)S(1)}, u32[]{:S(2)}, u32[]{:S(2)}) collective-permute-start(bf16[400,128]{1,0:T(8,128)(2,1)S(1)} %get-tuple-element.38), channel_id=1, source_target_pairs={{0,12},{1,13},{2,14},{3,15},{4,8},{5,9},{6,10},{7,11},{8,4},{9,5},... | collective-permute-start | bytes 307208 | tf_op jit(solution)/shard_map/ppermute | solution.py:285
  52.7 13.2 %collective-permute-start.15 = (bf16[400,128]{1,0:T(8,128)(2,1)S(1)}, bf16[400,128]{1,0:T(8,128)(2,1)S(1)}, u32[]{:S(2)}, u32[]{:S(2)}) collective-permute-start(bf16[400,128]{1,0:T(8,128)(2,1)S(1)} %get-tuple-element.39), channel_id=1, source_target_pairs={{0,10},{1,11},{2,8},{3,9},{4,14},{5,15},{6,12},{7,13},{8,2},{9,3},... | collective-permute-start | bytes 307208 | tf_op jit(solution)/shard_map/ppermute | solution.py:285
  52.7 14.7 %collective-permute-start.16 = (bf16[400,128]{1,0:T(8,128)(2,1)S(1)}, bf16[400,128]{1,0:T(8,128)(2,1)S(1)}, u32[]{:S(2)}, u32[]{:S(2)}) collective-permute-start(bf16[400,128]{1,0:T(8,128)(2,1)S(1)} %get-tuple-element.40), channel_id=1, source_target_pairs={{0,8},{1,9},{2,10},{3,11},{4,12},{5,13},{6,14},{7,15},{8,0},{9,1},... | collective-permute-start | bytes 307208 | tf_op jit(solution)/shard_map/ppermute | solution.py:285
  54.7 12.6 %collective-permute-start.17 = (bf16[400,128]{1,0:T(8,128)(2,1)S(1)}, bf16[400,128]{1,0:T(8,128)(2,1)S(1)}, u32[]{:S(2)}, u32[]{:S(2)}) collective-permute-start(bf16[400,128]{1,0:T(8,128)(2,1)S(1)} %get-tuple-element.41), channel_id=1, source_target_pairs={{0,6},{1,7},{2,4},{3,5},{4,2},{5,3},{6,0},{7,1},{8,14},{9,15},{10,... | collective-permute-start | bytes 307208 | tf_op jit(solution)/shard_map/ppermute | solution.py:285
  56.7 10.7 %collective-permute-start.18 = (bf16[400,128]{1,0:T(8,128)(2,1)S(1)}, bf16[400,128]{1,0:T(8,128)(2,1)S(1)}, u32[]{:S(2)}, u32[]{:S(2)}) collective-permute-start(bf16[400,128]{1,0:T(8,128)(2,1)S(1)} %get-tuple-element.42), channel_id=1, source_target_pairs={{0,4},{1,5},{2,6},{3,7},{4,0},{5,1},{6,2},{7,3},{8,12},{9,13},{10,... | collective-permute-start | bytes 307208 | tf_op jit(solution)/shard_map/ppermute | solution.py:285
  59.0 8.4 %collective-permute-start.19 = (bf16[400,128]{1,0:T(8,128)(2,1)S(1)}, bf16[400,128]{1,0:T(8,128)(2,1)S(1)}, u32[]{:S(2)}, u32[]{:S(2)}) collective-permute-start(bf16[400,128]{1,0:T(8,128)(2,1)S(1)} %get-tuple-element.43), channel_id=1, source_target_pairs={{0,2},{1,3},{2,0},{3,1},{4,6},{5,7},{6,4},{7,5},{8,10},{9,11},{10,... | collective-permute-start | bytes 307208 | tf_op jit(solution)/shard_map/ppermute | solution.py:285
